TPU v7x, 128 devices: a whole 4x4x4 slice. The times are simulated.
128 devices in a mesh: gy: 32 (over y, z, x_lo), gz: 4 (over x_hi, core).
Axes of the slice: x: 4 (x_hi: 2, x_lo: 2; x = x_hi * 2 + x_lo), y: 4, z: 4, core: 2. Of those that a mesh axis runs over, the one named last changes fastest.
Arguments:
- flow_state: bfloat16 [4, 128, 256, 512], P(None, 'gz', 'gy'), may hold values from -4 to 4
- metric: float32 [3, 3], replicated, may hold values from -0.3 to 1.5, as said below
- deformation_matrix: float32 [3, 3], replicated, may hold values from -0.5 to 0.5
Outputs:
- solenoidal_motion: float32 [3, 128, 256, 512], P(None, 'gz', 'gy')
- heat_content_next: float32 [128, 256, 512], P('gz', 'gy')
Inputs may be any that keep to these rules, and one draw needn't show every extreme that they name: `metric`: diagonal entries lie between 1 and 1.5, off-diagonal entries have magnitude at most 0.3.
All inputs are finite; a program needn't handle non-finite values.
Results may differ from a plain program's by a relative error of at most 0.0003.
Values may be sent and summed in bfloat16 or wider, within the bound.
No kernel may reach another device: no remote copies, remote signals or barrier semaphores. Data moves between devices by JAX's collectives and lax.ppermute only.
A program may use at most 128 MiB of HBM per device.

v0:
```python
import math

import jax
import jax.numpy as jnp
from jax import lax
from jax.sharding import PartitionSpec as P

substep_width = 0.4
stratification_squared = 1.0
highest = lax.Precision.HIGHEST


def with_halo(block, sides, width):
    for axis, dim in sides:
        count = lax.axis_size(axis)
        forward = [(i, i + 1) for i in range(count - 1)]
        forward.append((count - 1, 0))
        backward = [(target, source) for source, target in forward]
        low = lax.ppermute(
            lax.slice_in_dim(block, block.shape[dim] - width, None, axis=dim), axis, forward
        )
        high = lax.ppermute(lax.slice_in_dim(block, 0, width, axis=dim), axis, backward)
        block = jnp.concatenate([low, block, high], axis=dim)
    return block


def difference_periodic(forcing_term, along):

    def moved(offset):
        return jnp.roll(forcing_term, -offset, axis=along)

    return (
        45.0 * (moved(1) - moved(-1)) - 9.0 * (moved(2) - moved(-2)) + (moved(3) - moved(-3))
    ) / 60.0


def difference_padded(padded, along, extent):

    def moved(offset):
        return lax.slice_in_dim(padded, 3 + offset, 3 + offset + extent, axis=along)

    return (
        45.0 * (moved(1) - moved(-1)) - 9.0 * (moved(2) - moved(-2)) + (moved(3) - moved(-3))
    ) / 60.0


def phase_table(row_count, col_count, length, direction_sign):
    rows_iota = jnp.arange(row_count, dtype=jnp.int32)[:, None]
    cols_iota = jnp.arange(col_count, dtype=jnp.int32)[None, :]
    angle = 2.0 * math.pi / length * (rows_iota * cols_iota % length).astype(jnp.float32)
    return (jnp.cos(angle), direction_sign * jnp.sin(angle))


def split_length(length):
    inner = 128
    return (length // inner, inner)


def mode_of(flat, length):
    outer, inner = split_length(length)
    return flat % inner * outer + flat // inner


def complex_einsum(form, real_part, imag_part, table_real, table_imag):

    def product(left, right):
        return jnp.einsum(form, left, right, precision=highest)

    return (
        product(real_part, table_real) - product(imag_part, table_imag),
        product(real_part, table_imag) + product(imag_part, table_real),
    )


def twisted(real_part, imag_part, twist_real, twist_imag):
    return (
        real_part * twist_real - imag_part * twist_imag,
        real_part * twist_imag + imag_part * twist_real,
    )


def transform_last(real_part, imag_part, forward):
    direction_sign = -1.0 if forward else 1.0
    length = real_part.shape[-1]
    outer, inner = split_length(length)
    leading = real_part.shape[:-1]
    real_part = real_part.reshape(leading + (outer, inner))
    imag_part = imag_part.reshape(leading + (outer, inner))
    outer_real, outer_imag = phase_table(outer, outer, outer, direction_sign)
    inner_real, inner_imag = phase_table(inner, inner, inner, direction_sign)
    twist_real, twist_imag = phase_table(outer, inner, length, direction_sign)
    if forward:
        real_part, imag_part = complex_einsum(
            "...nb,nq->...qb", real_part, imag_part, outer_real, outer_imag
        )
        real_part, imag_part = twisted(real_part, imag_part, twist_real, twist_imag)
        real_part, imag_part = complex_einsum(
            "...qb,bp->...qp", real_part, imag_part, inner_real, inner_imag
        )
    else:
        real_part, imag_part = complex_einsum(
            "...qp,pb->...qb", real_part, imag_part, inner_real, inner_imag
        )
        real_part, imag_part = twisted(real_part, imag_part, twist_real, twist_imag)
        real_part, imag_part = complex_einsum(
            "...qb,qn->...nb", real_part, imag_part, outer_real, outer_imag
        )
    return (real_part.reshape(leading + (length,)), imag_part.reshape(leading + (length,)))


def transform_first(real_part, imag_part, forward):
    direction_sign = -1.0 if forward else 1.0
    length, middle, trailing = real_part.shape
    outer, inner = split_length(length)
    real_part = real_part.reshape((outer, inner, middle, trailing))
    imag_part = imag_part.reshape((outer, inner, middle, trailing))
    outer_real, outer_imag = phase_table(outer, outer, outer, direction_sign)
    inner_real, inner_imag = phase_table(inner, inner, inner, direction_sign)
    twist_real, twist_imag = phase_table(outer, inner, length, direction_sign)
    twist_real = twist_real[:, :, None, None]
    twist_imag = twist_imag[:, :, None, None]
    if forward:
        real_part, imag_part = complex_einsum(
            "nbmt,nq->qbmt", real_part, imag_part, outer_real, outer_imag
        )
        real_part, imag_part = twisted(real_part, imag_part, twist_real, twist_imag)
        real_part, imag_part = complex_einsum(
            "qbmt,bp->qpmt", real_part, imag_part, inner_real, inner_imag
        )
    else:
        real_part, imag_part = complex_einsum(
            "qpmt,pb->qbmt", real_part, imag_part, inner_real, inner_imag
        )
        real_part, imag_part = twisted(real_part, imag_part, twist_real, twist_imag)
        real_part, imag_part = complex_einsum(
            "qbmt,qn->nbmt", real_part, imag_part, outer_real, outer_imag
        )
    return (
        real_part.reshape((length, middle, trailing)),
        imag_part.reshape((length, middle, trailing)),
    )


def wavenumber(modes, length):

    def wave(multiple):
        return jnp.sin(2.0 * math.pi / length * (multiple * modes % length).astype(jnp.float32))

    return 1.5 * wave(1) - 0.3 * wave(2) + wave(3) / 30.0


def poisson_divide(
    real_part, imag_part, modes_x, modes_y, modes_z, length_x, length_y, length_z, metric
):
    waves = [
        wavenumber(modes_x, length_x),
        wavenumber(modes_y, length_y),
        wavenumber(modes_z, length_z),
    ]
    symbol = jnp.zeros(real_part.shape, jnp.float32)
    for vector_entry in range(3):
        mixed = (
            metric[vector_entry, 0] * waves[0]
            + metric[vector_entry, 1] * waves[1]
            + metric[vector_entry, 2] * waves[2]
        )
        symbol = symbol + mixed * mixed
    edge = (
        (2 * modes_x % length_x == 0)
        & (2 * modes_y % length_y == 0)
        & (2 * modes_z % length_z == 0)
    )
    total = float(length_x * length_y * length_z)
    factor = jnp.where(edge, 0.0, -1.0 / (jnp.where(edge, 1.0, symbol) * total))
    return (real_part * factor, imag_part * factor)


def shards(flow_state, metric, deformation_matrix):
    extent_z = flow_state.shape[1]
    extent_y = flow_state.shape[2]
    length_x = flow_state.shape[3]
    length_y = extent_y * lax.axis_size("gy")
    length_z = extent_z * lax.axis_size("gz")
    padded = with_halo(flow_state, (("gy", 2), ("gz", 1)), 3).astype(jnp.float32)
    midcell_location = padded[:, 3 : 3 + extent_z, 3 : 3 + extent_y, :]
    grad_x = difference_periodic(midcell_location, 3)
    grad_y = difference_padded(padded[:, 3 : 3 + extent_z], 2, extent_y)
    grad_z = difference_padded(padded[:, :, 3 : 3 + extent_y], 1, extent_z)
    current_speeds = [midcell_location[0], midcell_location[1], midcell_location[2]]
    heat_content = midcell_location[3]
    contra = [
        metric[0, direction] * current_speeds[0]
        + metric[1, direction] * current_speeds[1]
        + metric[2, direction] * current_speeds[2]
        for direction in range(3)
    ]
    advected_quantity = contra[0] * grad_x + contra[1] * grad_y + contra[2] * grad_z
    provisional = []
    for vector_entry in range(3):
        evolution_change = -advected_quantity[vector_entry] - (
            deformation_matrix[vector_entry, 0] * current_speeds[0]
            + deformation_matrix[vector_entry, 1] * current_speeds[1]
            + deformation_matrix[vector_entry, 2] * current_speeds[2]
        )
        if vector_entry == 2:
            evolution_change = evolution_change + heat_content
        provisional.append(current_speeds[vector_entry] + substep_width * evolution_change)
    heat_content_next = heat_content + substep_width * (
        -advected_quantity[3] - stratification_squared * current_speeds[2]
    )
    stacked = jnp.stack(provisional)
    beside_all = with_halo(stacked, (("gy", 2), ("gz", 1)), 3)
    slope_x = difference_periodic(stacked, 3)
    slope_y = difference_padded(beside_all[:, 3 : 3 + extent_z], 2, extent_y)
    slope_z = difference_padded(beside_all[:, :, 3 : 3 + extent_y], 1, extent_z)
    flow_compressibility = jnp.zeros_like(heat_content)
    for vector_entry in range(3):
        flow_compressibility = (
            flow_compressibility
            + metric[vector_entry, 0] * slope_x[vector_entry]
            + metric[vector_entry, 1] * slope_y[vector_entry]
            + metric[vector_entry, 2] * slope_z[vector_entry]
        )
    cos_table, sin_table = phase_table(length_x, length_x, length_x, -1.0)
    back_cos, back_sin = phase_table(length_x, length_x, length_x, 1.0)
    real_part = jnp.einsum("zcx,xk->zkc", flow_compressibility, cos_table, precision=highest)
    imag_part = jnp.einsum("zcx,xk->zkc", flow_compressibility, sin_table, precision=highest)
    real_part, imag_part = (
        lax.all_to_all(real_part, "gy", split_axis=1, concat_axis=2, tiled=True),
        lax.all_to_all(imag_part, "gy", split_axis=1, concat_axis=2, tiled=True),
    )
    real_part, imag_part = transform_last(real_part, imag_part, True)
    real_part, imag_part = (
        lax.all_to_all(real_part, "gz", split_axis=2, concat_axis=0, tiled=True),
        lax.all_to_all(imag_part, "gz", split_axis=2, concat_axis=0, tiled=True),
    )
    real_part, imag_part = transform_first(real_part, imag_part, True)
    width_x = real_part.shape[1]
    width_y = real_part.shape[2]
    modes_z = mode_of(jnp.arange(length_z, dtype=jnp.int32), length_z)[:, None, None]
    modes_x = (lax.axis_index("gy") * width_x + jnp.arange(width_x, dtype=jnp.int32))[None, :, None]
    modes_y = mode_of(
        lax.axis_index("gz") * width_y + jnp.arange(width_y, dtype=jnp.int32), length_y
    )[None, None, :]
    real_part, imag_part = poisson_divide(
        real_part, imag_part, modes_x, modes_y, modes_z, length_x, length_y, length_z, metric
    )
    real_part, imag_part = transform_first(real_part, imag_part, False)
    real_part, imag_part = (
        lax.all_to_all(real_part, "gz", split_axis=0, concat_axis=2, tiled=True),
        lax.all_to_all(imag_part, "gz", split_axis=0, concat_axis=2, tiled=True),
    )
    real_part, imag_part = transform_last(real_part, imag_part, False)
    real_part, imag_part = (
        lax.all_to_all(real_part, "gy", split_axis=2, concat_axis=1, tiled=True),
        lax.all_to_all(imag_part, "gy", split_axis=2, concat_axis=1, tiled=True),
    )
    pressure = jnp.einsum("zkc,kx->zcx", real_part, back_cos, precision=highest) - jnp.einsum(
        "zkc,kx->zcx", imag_part, back_sin, precision=highest
    )
    around_pressure = with_halo(pressure, (("gy", 1), ("gz", 0)), 3)
    push_x = difference_periodic(pressure, 2)
    push_y = difference_padded(around_pressure[3 : 3 + extent_z], 1, extent_y)
    push_z = difference_padded(around_pressure[:, 3 : 3 + extent_y], 0, extent_z)
    solenoidal_motion = jnp.stack(
        [
            provisional[vector_entry]
            - (
                metric[vector_entry, 0] * push_x
                + metric[vector_entry, 1] * push_y
                + metric[vector_entry, 2] * push_z
            )
            for vector_entry in range(3)
        ]
    )
    return (solenoidal_motion, heat_content_next)


def solution(mesh):
    placed = (P(None, "gz", "gy", None), P(), P())
    return jax.shard_map(
        shards,
        mesh=mesh,
        in_specs=placed,
        out_specs=(P(None, "gz", "gy", None), P("gz", "gy", None)),
        check_vma=False,
    )
```

profile of v0, /device:TPU:1, one launch (start us, length us, event | category | flops | bytes accessed | tf_op | source)
XLA Modules:
  0.0 407.6 jit_solution(2544002536666746873)
XLA Ops:
  2.8 8.0 %collective-permute-start.1 = (bf16[4,32,3,512]{3,2,1,0:T(4,128)(2,1)S(1)}, bf16[4,32,3,512]{3,2,1,0:T(4,128)(2,1)S(1)}, u32[]{:S(2)}, u32[]{:S(2)}) collective-permute-start(bf16[4,32,3,512]{3,2,1,0:T(4,128)(2,1)S(1)} %get-tuple-element.61), channel_id=1, source_target_pairs={{4,0},{8,4},{12,8},{16,12},{20,16},{24,20},{28,24},{32,28},{36,32}... | collective-permute-start | bytes 1179656 | tf_op jit(solution)/shard_map/ppermute | solution.py:22
  18.5 2.9 collective-permute-done.1
  21.4 12.2 %collective-permute-done = bf16[4,32,3,512]{3,2,1,0:T(4,128)(2,1)S(1)} collective-permute-done((bf16[4,32,3,512]{3,2,1,0:T(4,128)(2,1)S(1)}, bf16[4,32,3,512]{3,2,1,0:T(4,128)(2,1)S(1)}, u32[]{:S(2)}, u32[]{:S(2)}) %collective-permute-start) | collective-permute-done | bytes 393248 | tf_op jit(solution)/shard_map/ppermute | solution.py:19
  35.5 2.9 collective-permute-start.2
  38.5 3.7 collective-permute-done.3
  47.3 2.5 fusion.371
  49.8 7.4 %multiply_bitcast_fusion.2 = (f32[32,8,512]{2,1,0:T(8,128)}, f32[32,8,512]{2,1,0:T(8,128)}, f32[32,8,512]{2,1,0:T(8,128)}) fusion(f32[4,38,14,512]{3,2,1,0:T(8,128)S(1)} %maximum_convert_fusion, f32[]{:T(128)} %bitcast.3, f32[]{:T(128)} %bitcast.2, f32[]{:T(128)} %bitcast.1, f32[]{:T(128)} %bitcast.11, f32[]{:T(128)} %bitcast.10, f32[]{:T(128)} %bitcast.9, ...), kind=kLoop, calls=%fused_computation.205 | loop fusion | flops 2359296 | bytes 3145764 | tf_op jit(solution)/shard_map/mul | solution.py:197
  57.2 7.5 %fusion.2 = f32[4,32,8,512]{3,2,1,0:T(8,128)S(1)} fusion(f32[4,38,14,512]{3,2,1,0:T(8,128)S(1)} %maximum_convert_fusion, f32[4,32,8,1]{3,2,1,0:T(8,128)S(1)} %get-tuple-element.25, f32[4,32,8,511]{3,2,1,0:T(8,128)S(1)} %get-tuple-element.27, f32[4,32,8,511]{3,2,1,0:T(8,128)S(1)} %get-tuple-element.26, f32[4,32,8,1]{3,2,1,0:T(8,128)S(1)} %get-tuple-element.24, ...), kind=kLoop, calls=%fused_computation.8 | loop fusion | flops 16777216 | bytes 41418752 | tf_op jit(solution)/shard_map/add | solution.py:197
  67.0 4.5 %multiply_add_fusion.7 = (f32[1,32,8,512]{3,2,1,0:T(8,128)S(1)}, f32[1,32,8,512]{3,2,1,0:T(8,128)S(1)}) fusion(f32[4,32,8,512]{3,2,1,0:T(8,128)S(1)} %fusion.2, f32[4,38,14,512]{3,2,1,0:T(8,128)S(1)} %maximum_convert_fusion, f32[]{:T(128)} %bitcast.17, f32[]{:T(128)} %bitcast.15, f32[]{:T(128)} %bitcast.14, f32[]{:T(128)} %bitcast.28, f32[]{:T(128)} %bitcast.27, ...), kind=kLoop, calls=%fused_computation.200 | loop fusion | flops 2490368 | bytes 4194328 | tf_op jit(solution)/shard_map/add | solution.py:207
  76.5 2.9 fusion.30
  79.4 6.9 %collective-permute-done.4 = f32[3,32,3,512]{3,1,2,0:T(8,128)S(1)} collective-permute-done((f32[3,32,3,512]{3,1,2,0:T(8,128)S(1)}, f32[3,32,3,512]{3,1,2,0:T(8,128)S(1)}, u32[]{:S(2)}, u32[]{:S(2)}) %collective-permute-start.4) | collective-permute-done | bytes 589856 | tf_op jit(solution)/shard_map/ppermute | solution.py:22
  86.7 12.1 %collective-permute-done.5 = f32[3,32,3,512]{3,1,2,0:T(8,128)S(1)} collective-permute-done((f32[3,32,3,512]{3,1,2,0:T(8,128)S(1)}, f32[3,32,3,512]{3,1,2,0:T(8,128)S(1)}, u32[]{:S(2)}, u32[]{:S(2)}) %collective-permute-start.5) | collective-permute-done | bytes 589856 | tf_op jit(solution)/shard_map/ppermute | solution.py:19
  99.3 3.1 collective-permute-start.6
  105.8 6.3 %collective-permute-done.6 = f32[3,3,14,512]{3,2,1,0:T(8,128)S(1)} collective-permute-done((f32[3,3,14,512]{3,2,1,0:T(8,128)S(1)}, f32[3,3,14,512]{3,2,1,0:T(8,128)S(1)}, u32[]{:S(2)}, u32[]{:S(2)}) %collective-permute-start.6) | collective-permute-done | bytes 258080 | tf_op jit(solution)/shard_map/ppermute | solution.py:22
  113.7 4.4 %fusion.18 = (f32[3,32,8,512]{3,2,1,0:T(8,128)}, f32[3,32,8,512]{3,2,1,0:T(8,128)}) fusion(f32[3,35,14,512]{3,2,1,0:T(8,128)S(1)} %get-tuple-element.29, f32[3,35,14,512]{3,2,1,0:T(8,128)S(1)} %get-tuple-element.28, f32[3,32,11,512]{3,2,1,0:T(8,128)S(1)} %get-tuple-element.47, f32[3,32,11,512]{3,2,1,0:T(8,128)S(1)} %get-tuple-element.46), kind=kLoop, calls=%fused_computation.33 | loop fusion | flops 6291456 | bytes 22020096 | tf_op jit(solution)/shard_map/div | solution.py:42
  118.1 8.7 %fusion.68 = f32[32,8,512]{2,1,0:T(8,128)S(1)} fusion(f32[3,32,8,512]{3,2,1,0:T(8,128)} %get-tuple-element.96, f32[3,32,8,512]{3,2,1,0:T(8,128)} %get-tuple-element.97, f32[3,32,8,512]{3,2,1,0:T(8,128)} %fusion.30, f32[]{:T(128)} %bitcast.11, f32[]{:T(128)} %bitcast.10, f32[]{:T(128)} %bitcast.9, f32[]{:T(128)} %bitcast.7, f32[]{:T(128)} %bitcast.6, ...), kind=kLoop, calls=%fused_computation.126 | loop fusion | flops 2228224 | bytes 5242916 | tf_op jit(solution)/shard_map/add | solution.py:219
  126.7 5.6 %convolution_bitcast_fusion.1 = f32[32,512,8]{1,0,2:T(8,128)S(1)} fusion(f32[32,8,512]{2,1,0:T(8,128)S(1)} %fusion.68), kind=kOutput, calls=%fused_computation.76 | convolution fusion | flops 808976384 | bytes 1048576 | tf_op jit(solution)/shard_map/zcx,xk->zkc/dot_general | solution.py:226
  134.3 3.1 reshape.728
  137.5 4.1 all-to-all-start
  141.6 6.1 %convolution_bitcast_fusion = f32[32,512,8]{1,0,2:T(8,128)} fusion(f32[32,8,512]{2,1,0:T(8,128)S(1)} %fusion.68), kind=kOutput, calls=%fused_computation.75 | convolution fusion | flops 809238528 | bytes 1048576 | tf_op jit(solution)/shard_map/zcx,xk->zkc/dot_general | solution.py:227
  147.8 3.0 copy.174
  150.8 3.1 reshape.730
  153.9 7.9 %all-to-all-start.1 = ((f32[32,1,4096]{2,1,0:T(1,128)}), f32[32,1,4096]{2,1,0:T(1,128)}, u32[]{:S(2)}, u32[]{:S(2)}) async-start(f32[32,1,4096]{2,1,0:T(1,128)} %reshape.730), calls=%async_computation.1 | async-start | bytes 1048576 | tf_op jit(solution)/shard_map/all_to_all | solution.py:230
  166.2 3.2 copy.171
  171.4 2.7 fusion.182
  174.1 2.7 fusion.188
  176.8 2.9 reduce.1
  181.7 3.2 copy.175
  184.9 2.5 copy.176
  189.3 3.4 add_bitcast_fusion
  196.6 2.9 reshape.732
  199.5 5.6 %all-to-all-start.2 = ((f32[4,1,32768]{2,1,0:T(1,128)}), f32[4,1,32768]{2,1,0:T(1,128)}, u32[]{:S(2)}, u32[]{:S(2)}) async-start(f32[4,1,32768]{2,1,0:T(1,128)} %reshape.732), calls=%async_computation.2 | async-start | bytes 1048576 | tf_op jit(solution)/shard_map/all_to_all | solution.py:234
  209.0 2.9 reshape.734
  211.9 2.8 all-to-all-done.2
  214.7 5.2 %all-to-all-start.3 = ((f32[4,1,32768]{2,1,0:T(1,128)}), f32[4,1,32768]{2,1,0:T(1,128)}, u32[]{:S(2)}, u32[]{:S(2)}) async-start(f32[4,1,32768]{2,1,0:T(1,128)} %reshape.734), calls=%async_computation.3 | async-start | bytes 1048576 | tf_op jit(solution)/shard_map/all_to_all | solution.py:235
  220.0 3.0 reduce.2
  225.1 2.5 copy.222
  228.7 2.4 copy.192
  231.1 3.0 reduce.3
  236.1 2.5 copy.224
  254.9 4.8 %all-to-all-start.4 = ((f32[4,1,32768]{2,1,0:T(1,128)}), f32[4,1,32768]{2,1,0:T(1,128)}, u32[]{:S(2)}, u32[]{:S(2)}) async-start(f32[4,1,32768]{2,1,0:T(1,128)} %reshape.736), calls=%async_computation.4 | async-start | bytes 1048576 | tf_op jit(solution)/shard_map/all_to_all | solution.py:250
  262.7 6.5 %all-to-all-done.4 = f32[4,1,32768]{2,1,0:T(1,128)} async-done(((f32[4,1,32768]{2,1,0:T(1,128)}), f32[4,1,32768]{2,1,0:T(1,128)}, u32[]{:S(2)}, u32[]{:S(2)}) %all-to-all-start.4) | async-done | bytes 524320 | tf_op jit(solution)/shard_map/all_to_all | solution.py:250
  269.2 5.3 %all-to-all-start.5 = ((f32[4,1,32768]{2,1,0:T(1,128)}), f32[4,1,32768]{2,1,0:T(1,128)}, u32[]{:S(2)}, u32[]{:S(2)}) async-start(f32[4,1,32768]{2,1,0:T(1,128)} %reshape.738), calls=%async_computation.5 | async-start | bytes 1048576 | tf_op jit(solution)/shard_map/all_to_all | solution.py:251
  274.6 3.8 reduce.4
  286.8 3.8 reduce.5
  305.4 3.1 reshape.740
  308.5 7.9 %all-to-all-start.6 = ((f32[32,1,4096]{2,1,0:T(1,128)}), f32[32,1,4096]{2,1,0:T(1,128)S(1)}, u32[]{:S(2)}, u32[]{:S(2)}) async-start(f32[32,1,4096]{2,1,0:T(1,128)} %reshape.740), calls=%async_computation.6 | async-start | bytes 1048576 | tf_op jit(solution)/shard_map/all_to_all | solution.py:255
  318.4 3.0 fusion.32
  323.1 3.1 reshape.742
  328.2 6.0 %all-to-all-start.7 = ((f32[32,1,4096]{2,1,0:T(1,128)}), f32[32,1,4096]{2,1,0:T(1,128)S(1)}, u32[]{:S(2)}, u32[]{:S(2)}) async-start(f32[32,1,4096]{2,1,0:T(1,128)} %reshape.742), calls=%async_computation.7 | async-start | bytes 1048576 | tf_op jit(solution)/shard_map/all_to_all | solution.py:256
  340.0 2.9 reduce.6
  344.9 3.8 copy.207
  348.7 2.4 copy.208
  351.1 5.8 %fusion.39 = f32[32,8,512]{2,1,0:T(8,128)} fusion(f32[32,512,8]{1,2,0:T(8,128)S(1)} %copy.208), kind=kOutput, calls=%fused_computation.88 | convolution fusion | flops 808976384 | bytes 1048576 | tf_op jit(solution)/shard_map/zkc,kx->zcx/dot_general | solution.py:258
  360.8 3.8 copy.213
  364.6 2.4 copy.214
  367.1 5.6 %convolution_subtract_fusion = f32[32,8,512]{2,1,0:T(8,128)S(1)} fusion(f32[32,8,512]{2,1,0:T(8,128)S(1)} %copy-done.9, f32[32,512,8]{1,2,0:T(8,128)S(1)} %copy.214), kind=kOutput, calls=%fused_computation.68 | convolution fusion | flops 809107456 | bytes 1572864 | tf_op jit(solution)/shard_map/zkc,kx->zcx/dot_general | solution.py:258
  374.9 4.4 %collective-permute-start.8 = (f32[32,3,512]{2,1,0:T(4,128)S(1)}, f32[32,3,512]{2,1,0:T(4,128)S(1)}, u32[]{:S(2)}, u32[]{:S(2)}) collective-permute-start(f32[32,3,512]{2,1,0:T(4,128)S(1)} %get-tuple-element.62), channel_id=1, source_target_pairs={{4,0},{8,4},{12,8},{16,12},{20,16},{24,20},{28,24},{32,28},{36,32}... | collective-permute-start | bytes 589832 | tf_op jit(solution)/shard_map/ppermute | solution.py:22
  379.4 5.3 %collective-permute-done.9 = f32[32,3,512]{2,1,0:T(4,128)S(1)} collective-permute-done((f32[32,3,512]{2,1,0:T(4,128)S(1)}, f32[32,3,512]{2,1,0:T(4,128)S(1)}, u32[]{:S(2)}, u32[]{:S(2)}) %collective-permute-start.9) | collective-permute-done | bytes 196640 | tf_op jit(solution)/shard_map/ppermute | solution.py:19
  389.1 3.5 collective-permute-start.11
  392.7 2.9 collective-permute-done.10
  395.9 3.9 fusion.93
  399.8 3.6 fusion.61
  403.5 2.5 fusion.87
  (145 shorter events, 117.7 us)
Async XLA Ops:
  0.6 33.0 %copy-start.1 = (bf16[4,32,8,512]{3,2,1,0:T(8,128)(2,1)S(1)}, bf16[4,32,8,512]{3,2,1,0:T(8,128)(2,1)}, u32[]{:S(2)}) copy-start(bf16[4,32,8,512]{3,2,1,0:T(8,128)(2,1)} %param.3) | copy-start | bytes 3145732
  0.6 10.2 %copy-start.7 = (f32[3,3]{1,0:T(4,128)S(1)}, f32[3,3]{1,0:T(4,128)}, u32[]{:S(2)}) copy-start(f32[3,3]{1,0:T(4,128)} %param.4) | copy-start | bytes 112
  0.6 17.2 %copy-start.8 = (f32[3,3]{1,0:T(4,128)S(1)}, f32[3,3]{1,0:T(4,128)}, u32[]{:S(2)}) copy-start(f32[3,3]{1,0:T(4,128)} %param.5) | copy-start | bytes 112
  2.8 18.6 %collective-permute-start.1 = (bf16[4,32,3,512]{3,2,1,0:T(4,128)(2,1)S(1)}, bf16[4,32,3,512]{3,2,1,0:T(4,128)(2,1)S(1)}, u32[]{:S(2)}, u32[]{:S(2)}) collective-permute-start(bf16[4,32,3,512]{3,2,1,0:T(4,128)(2,1)S(1)} %get-tuple-element.61), channel_id=1, source_target_pairs={{4,0},{8,4},{12,8},{16,12},{20,16},{24,20},{28,24},{32,28},{36,32}... | collective-permute-start | bytes 1179656 | tf_op jit(solution)/shard_map/ppermute | solution.py:22
  10.9 22.8 %collective-permute-start = (bf16[4,32,3,512]{3,2,1,0:T(4,128)(2,1)S(1)}, bf16[4,32,3,512]{3,2,1,0:T(4,128)(2,1)S(1)}, u32[]{:S(2)}, u32[]{:S(2)}) collective-permute-start(bf16[4,32,3,512]{3,2,1,0:T(4,128)(2,1)S(1)} %get-tuple-element.60), channel_id=1, source_target_pairs={{0,4},{4,8},{8,12},{12,16},{16,20},{20,24},{24,28},{28,32},{32,36}... | collective-permute-start | bytes 1179656 | tf_op jit(solution)/shard_map/ppermute | solution.py:19
  33.9 8.3 %collective-permute-start.3 = (bf16[4,3,14,512]{3,2,1,0:T(8,128)(2,1)S(1)}, bf16[4,3,14,512]{3,2,1,0:T(8,128)(2,1)S(1)}, u32[]{:S(2)}, u32[]{:S(2)}) collective-permute-start(bf16[4,3,14,512]{3,2,1,0:T(8,128)(2,1)S(1)} %get-tuple-element.33), channel_id=1, source_target_pairs={{1,0},{2,1},{3,2},{0,3},{5,4},{6,5},{7,6},{4,7},{9,8},{10,9},{11,1... | collective-permute-start | bytes 516104 | tf_op jit(solution)/shard_map/ppermute | solution.py:22
  35.5 6.6 %collective-permute-start.2 = (bf16[4,3,14,512]{3,2,1,0:T(8,128)(2,1)S(1)}, bf16[4,3,14,512]{3,2,1,0:T(8,128)(2,1)S(1)}, u32[]{:S(2)}, u32[]{:S(2)}) collective-permute-start(bf16[4,3,14,512]{3,2,1,0:T(8,128)(2,1)S(1)} %get-tuple-element.32), channel_id=1, source_target_pairs={{0,1},{1,2},{2,3},{3,0},{4,5},{5,6},{6,7},{7,4},{8,9},{9,10},{10,1... | collective-permute-start | bytes 516104 | tf_op jit(solution)/shard_map/ppermute | solution.py:19
  43.3 23.7 %copy-start = (f32[4,38,14,512]{3,2,1,0:T(8,128)}, f32[4,38,14,512]{3,2,1,0:T(8,128)S(1)}, u32[]{:S(2)}) copy-start(f32[4,38,14,512]{3,2,1,0:T(8,128)S(1)} %maximum_convert_fusion) | copy-start | bytes 13074436
  73.6 12.8 %collective-permute-start.4 = (f32[3,32,3,512]{3,1,2,0:T(8,128)S(1)}, f32[3,32,3,512]{3,1,2,0:T(8,128)S(1)}, u32[]{:S(2)}, u32[]{:S(2)}) collective-permute-start(f32[3,32,3,512]{3,1,2,0:T(8,128)S(1)} %copy.163), channel_id=1, source_target_pairs={{4,0},{8,4},{12,8},{16,12},{20,16},{24,20},{28,24},{32,28},{36,32}... | collective-permute-start | bytes 1769480 | tf_op jit(solution)/shard_map/ppermute | solution.py:22
  74.0 24.8 %collective-permute-start.5 = (f32[3,32,3,512]{3,1,2,0:T(8,128)S(1)}, f32[3,32,3,512]{3,1,2,0:T(8,128)S(1)}, u32[]{:S(2)}, u32[]{:S(2)}) collective-permute-start(f32[3,32,3,512]{3,1,2,0:T(8,128)S(1)} %copy.165), channel_id=1, source_target_pairs={{0,4},{4,8},{8,12},{12,16},{16,20},{20,24},{24,28},{28,32},{32,36}... | collective-permute-start | bytes 1769480 | tf_op jit(solution)/shard_map/ppermute | solution.py:19
  99.3 12.7 %collective-permute-start.6 = (f32[3,3,14,512]{3,2,1,0:T(8,128)S(1)}, f32[3,3,14,512]{3,2,1,0:T(8,128)S(1)}, u32[]{:S(2)}, u32[]{:S(2)}) collective-permute-start(f32[3,3,14,512]{3,2,1,0:T(8,128)S(1)} %get-tuple-element.30), channel_id=1, source_target_pairs={{1,0},{2,1},{3,2},{0,3},{5,4},{6,5},{7,6},{4,7},{9,8},{10,9},{11,1... | collective-permute-start | bytes 774152 | tf_op jit(solution)/shard_map/ppermute | solution.py:22
  102.5 9.6 %collective-permute-start.7 = (f32[3,3,14,512]{3,2,1,0:T(8,128)S(1)}, f32[3,3,14,512]{3,2,1,0:T(8,128)S(1)}, u32[]{:S(2)}, u32[]{:S(2)}) collective-permute-start(f32[3,3,14,512]{3,2,1,0:T(8,128)S(1)} %get-tuple-element.31), channel_id=1, source_target_pairs={{0,1},{1,2},{2,3},{3,0},{4,5},{5,6},{6,7},{7,4},{8,9},{9,10},{10,1... | collective-permute-start | bytes 774152 | tf_op jit(solution)/shard_map/ppermute | solution.py:19
  137.5 16.4 %all-to-all-start = ((f32[32,1,4096]{2,1,0:T(1,128)}), f32[32,1,4096]{2,1,0:T(1,128)S(1)}, u32[]{:S(2)}, u32[]{:S(2)}) async-start(f32[32,1,4096]{2,1,0:T(1,128)} %reshape.728), calls=%async_computation | async-start | bytes 1048576 | tf_op jit(solution)/shard_map/all_to_all | solution.py:229
  153.9 22.9 %all-to-all-start.1 = ((f32[32,1,4096]{2,1,0:T(1,128)}), f32[32,1,4096]{2,1,0:T(1,128)}, u32[]{:S(2)}, u32[]{:S(2)}) async-start(f32[32,1,4096]{2,1,0:T(1,128)} %reshape.730), calls=%async_computation.1 | async-start | bytes 1048576 | tf_op jit(solution)/shard_map/all_to_all | solution.py:230
  184.8 2.5 copy-start.5
  192.7 0.8 copy-start.3
  196.6 8.5 %copy-start.4 = (f32[32,16,2,128]{3,2,1,0:T(2,128)S(1)}, f32[32,16,2,128]{3,2,1,0:T(2,128)}, u32[]{:S(2)}) copy-start(f32[32,16,2,128]{3,2,1,0:T(2,128)} %copy-done.3) | copy-start | bytes 1572868
  199.5 15.2 %all-to-all-start.2 = ((f32[4,1,32768]{2,1,0:T(1,128)}), f32[4,1,32768]{2,1,0:T(1,128)}, u32[]{:S(2)}, u32[]{:S(2)}) async-start(f32[4,1,32768]{2,1,0:T(1,128)} %reshape.732), calls=%async_computation.2 | async-start | bytes 1048576 | tf_op jit(solution)/shard_map/all_to_all | solution.py:234
  214.7 16.3 %all-to-all-start.3 = ((f32[4,1,32768]{2,1,0:T(1,128)}), f32[4,1,32768]{2,1,0:T(1,128)}, u32[]{:S(2)}, u32[]{:S(2)}) async-start(f32[4,1,32768]{2,1,0:T(1,128)} %reshape.734), calls=%async_computation.3 | async-start | bytes 1048576 | tf_op jit(solution)/shard_map/all_to_all | solution.py:235
  254.9 14.4 %all-to-all-start.4 = ((f32[4,1,32768]{2,1,0:T(1,128)}), f32[4,1,32768]{2,1,0:T(1,128)}, u32[]{:S(2)}, u32[]{:S(2)}) async-start(f32[4,1,32768]{2,1,0:T(1,128)} %reshape.736), calls=%async_computation.4 | async-start | bytes 1048576 | tf_op jit(solution)/shard_map/all_to_all | solution.py:250
  269.2 17.6 %all-to-all-start.5 = ((f32[4,1,32768]{2,1,0:T(1,128)}), f32[4,1,32768]{2,1,0:T(1,128)}, u32[]{:S(2)}, u32[]{:S(2)}) async-start(f32[4,1,32768]{2,1,0:T(1,128)} %reshape.738), calls=%async_computation.5 | async-start | bytes 1048576 | tf_op jit(solution)/shard_map/all_to_all | solution.py:251
  299.6 2.1 copy-start.6
  308.5 19.6 %all-to-all-start.6 = ((f32[32,1,4096]{2,1,0:T(1,128)}), f32[32,1,4096]{2,1,0:T(1,128)S(1)}, u32[]{:S(2)}, u32[]{:S(2)}) async-start(f32[32,1,4096]{2,1,0:T(1,128)} %reshape.740), calls=%async_computation.6 | async-start | bytes 1048576 | tf_op jit(solution)/shard_map/all_to_all | solution.py:255
  328.2 11.1 %copy-start.2 = (f32[32,1,4096]{2,1,0:T(1,128)}, f32[32,1,4096]{2,1,0:T(1,128)S(1)}, u32[]{:S(2)}) copy-start(f32[32,1,4096]{2,1,0:T(1,128)S(1)} %all-to-all-done.6) | copy-start | bytes 1572868
  328.2 28.7 %all-to-all-start.7 = ((f32[32,1,4096]{2,1,0:T(1,128)}), f32[32,1,4096]{2,1,0:T(1,128)S(1)}, u32[]{:S(2)}, u32[]{:S(2)}) async-start(f32[32,1,4096]{2,1,0:T(1,128)} %reshape.742), calls=%async_computation.7 | async-start | bytes 1048576 | tf_op jit(solution)/shard_map/all_to_all | solution.py:256
  364.6 2.5 copy-start.9
  367.1 28.8 %slice-start = ((s8[4980736]{0:T(1024)(128)(4,1)}), s8[4194304]{0:T(1024)(128)(4,1)S(1)}, s32[]{:S(2)}) async-start(s8[4980736]{0:T(1024)(128)(4,1)} %bitcast.272), calls=%async_computation.8 | async-start | bytes 8388608
  373.0 22.9 %slice-start.1 = ((s8[4980736]{0:T(1024)(128)(4,1)}), s8[786432]{0:T(1024)(128)(4,1)S(1)}, s32[]{:S(2)}) async-start(s8[4980736]{0:T(1024)(128)(4,1)} %bitcast.272), calls=%async_computation.9 | async-start | bytes 1572864
  373.5 11.2 %collective-permute-start.9 = (f32[32,3,512]{2,1,0:T(4,128)S(1)}, f32[32,3,512]{2,1,0:T(4,128)S(1)}, u32[]{:S(2)}, u32[]{:S(2)}) collective-permute-start(f32[32,3,512]{2,1,0:T(4,128)S(1)} %get-tuple-element.63), channel_id=1, source_target_pairs={{0,4},{4,8},{8,12},{12,16},{16,20},{20,24},{24,28},{28,32},{32,36}... | collective-permute-start | bytes 589832 | tf_op jit(solution)/shard_map/ppermute | solution.py:19
  374.9 11.9 %collective-permute-start.8 = (f32[32,3,512]{2,1,0:T(4,128)S(1)}, f32[32,3,512]{2,1,0:T(4,128)S(1)}, u32[]{:S(2)}, u32[]{:S(2)}) collective-permute-start(f32[32,3,512]{2,1,0:T(4,128)S(1)} %get-tuple-element.62), channel_id=1, source_target_pairs={{4,0},{8,4},{12,8},{16,12},{20,16},{24,20},{28,24},{32,28},{36,32}... | collective-permute-start | bytes 589832 | tf_op jit(solution)/shard_map/ppermute | solution.py:22
  386.9 8.6 %collective-permute-start.10 = (f32[3,14,512]{2,1,0:T(8,128)S(1)}, f32[3,14,512]{2,1,0:T(8,128)S(1)}, u32[]{:S(2)}, u32[]{:S(2)}) collective-permute-start(f32[3,14,512]{2,1,0:T(8,128)S(1)} %get-tuple-element.56), channel_id=1, source_target_pairs={{1,0},{2,1},{3,2},{0,3},{5,4},{6,5},{7,6},{4,7},{9,8},{10,9},{11,1... | collective-permute-start | bytes 258056 | tf_op jit(solution)/shard_map/ppermute | solution.py:22
  389.1 6.4 %collective-permute-start.11 = (f32[3,14,512]{2,1,0:T(8,128)S(1)}, f32[3,14,512]{2,1,0:T(8,128)S(1)}, u32[]{:S(2)}, u32[]{:S(2)}) collective-permute-start(f32[3,14,512]{2,1,0:T(8,128)S(1)} %get-tuple-element.57), channel_id=1, source_target_pairs={{0,1},{1,2},{2,3},{3,0},{4,5},{5,6},{6,7},{7,4},{8,9},{9,10},{10,1... | collective-permute-start | bytes 258056 | tf_op jit(solution)/shard_map/ppermute | solution.py:19
where the time goes:
time: 413 us; the launch traced here: 408 us
  local copies, waits for them, and re-layouts  110 us (27%)
  other arithmetic  87.2 us (21%)
  starting transfers between devices  78.3 us (19%)
  waiting for transfers between devices  65.8 us (16%)
  matrix products  59.4 us (14%)
  between operations  7.43 us (2%)
    unnamed x40, local copies, waits for them, and re-layouts  36.4 us
    dot_general x16, matrix products, product(): return jnp.einsum(form, left, right, precision=highest)  29.7 us
    ppermute x6, waiting for transfers between devices, with_halo(): lax.ppermute(lax.slice_in_dim(block, block.shape[dim] - width, None, axis...  29.6 us
    ppermute x6, waiting for transfers between devices, with_halo(): lax.ppermute(lax.slice_in_dim(block, 0, width, axis=dim), axis, backward)  24.9 us
    ppermute x6, starting transfers between devices, with_halo(): lax.ppermute(lax.slice_in_dim(block, 0, width, axis=dim), axis, backward)  19.6 us
    ppermute x6, starting transfers between devices, with_halo(): lax.ppermute(lax.slice_in_dim(block, block.shape[dim] - width, None, axis...  11.9 us
    slice x18, local copies, waits for them, and re-layouts, moved(): return jnp.roll(forcing_term, -offset, axis=along)  9.52 us
    add x1, other arithmetic, shards(): flow_compressibility + metric[vector_entry, 0] * slope_x[vector_entry]  8.65 us
  transfers between devices with their start and end apart: 20, of which 12 were waited for; matrix products, arithmetic and copies ran while one was open for 25% of the time, Pallas kernels for 0%

commit v1 on v0

v1 whole, which is shorter than its diff:
```python
import numpy as np

import jax
import jax.numpy as jnp
import ml_dtypes
from jax import lax
from jax.experimental import pallas as pl
from jax.experimental.pallas import tpu as pltpu
from jax.sharding import PartitionSpec as P

F32 = jnp.float32
BF16 = jnp.bfloat16
NX, NY, NZ = 512, 256, 128
GY, GZ = 32, 4
BY, BZ = NY // GY, NZ // GZ
DEV = GY * GZ
CELLS = BY * BZ
EXT = 512
STEP = 0.4
COEF = {1: 45.0, -1: -45.0, 2: -9.0, -2: 9.0, 3: 1.0, -3: -1.0}
MIB = 1 << 20


def _pieces(table, count):
    rest = np.asarray(table, np.float64)
    out = []
    for _ in range(count):
        piece = rest.astype(np.float32).astype(ml_dtypes.bfloat16)
        out.append(piece)
        rest = rest - piece.astype(np.float64)
    return np.stack(out)


def _ext_cells():
    cells = [(w, y) for w in range(BZ) for y in range(BY)]
    cells += [(w, y) for w in range(BZ) for y in range(-3, 0)]
    cells += [(w, y) for w in range(BZ) for y in range(BY, BY + 3)]
    cells += [(w, y) for w in range(-3, 0) for y in range(BY)]
    cells += [(w, y) for w in range(BZ, BZ + 3) for y in range(BY)]
    return cells


def _difference_matrices():
    place = {cell: i for i, cell in enumerate(_ext_cells())}
    along_y = np.zeros((CELLS, EXT))
    along_z = np.zeros((CELLS, EXT))
    for w in range(BZ):
        for y in range(BY):
            row = place[(w, y)]
            for k, c in COEF.items():
                along_y[row, place[(w, y + k)]] = c
                along_z[row, place[(w + k, y)]] = c
    return along_y, along_z


def _circulant_x():
    table = np.zeros((NX, NX))
    for x in range(NX):
        for k, c in COEF.items():
            table[(x + k) % NX, x] = c
    return table


def _kt(modes, length):
    a = 2.0 * np.pi * modes / length
    return 1.5 * np.sin(a) - 0.3 * np.sin(2 * a) + np.sin(3 * a) / 30.0


def _x_tables():
    k = np.arange(NX // 2)[:, None]
    x = np.arange(NX)[None, :]
    angle = 2.0 * np.pi * ((k * x) % NX) / NX
    alternating = 1.0 - 2.0 * (np.arange(NX) % 2)
    forward = np.zeros((NX // 2, 2, NX))
    forward[:, 0], forward[:, 1] = np.cos(angle), -np.sin(angle)
    forward[0, 0], forward[0, 1] = 1.0, alternating
    inverse = 2.0 * forward
    inverse[0] = forward[0]
    symbol = _kt(k, NX)
    slope = np.zeros((NX // 2, 2, NX))
    slope[:, 0], slope[:, 1] = -2.0 * symbol * np.sin(angle), -2.0 * symbol * np.cos(angle)
    slope[0] = 0.0
    order = np.arange(NX).reshape(DEV, 4).T.reshape(-1)
    return (
        forward.reshape(NX, NX) / 60.0,
        inverse.reshape(NX, NX)[order] / 60.0,
        slope.reshape(NX, NX)[order],
    )


def _plane_tables():
    a = np.arange(DEV)
    m1, n1 = a // GZ, a % GZ
    gy, gz = a // GZ, a % GZ
    outer = np.exp(
        -2j * np.pi * (np.outer(m1, gy) / GY + np.outer(n1, gz) / GZ)
    )
    cells = np.array(_ext_cells())
    count = len(cells)
    w, y = cells[:, 0], cells[:, 1]
    twist = np.zeros((DEV, EXT), complex)
    twist[:, :count] = np.exp(-2j * np.pi * (np.outer(n1, w) / NZ + np.outer(m1, y) / NY))
    b = np.arange(CELLS)
    n2, m2 = b // BY, b % BY
    inner = np.zeros((EXT, CELLS), complex)
    inner[:count] = np.exp(-2j * np.pi * (np.outer(w, n2) / BZ + np.outer(y, m2) / BY))
    outer_real = np.block([[outer.real, -outer.imag], [outer.imag, outer.real]])
    inner_real = np.block([[inner.real, inner.imag], [-inner.imag, inner.real]])
    mode_y = m1[:, None] + GY * m2[None, :]
    mode_z = n1[:, None] + GZ * n2[None, :]
    edge = (((2 * mode_y) % NY == 0) & ((2 * mode_z) % NZ == 0)).astype(np.float32)
    waves = np.stack([_kt(mode_y, NY), _kt(mode_z, NZ), edge]).astype(np.float32)
    return outer_real, np.stack([twist.real, twist.imag]).astype(np.float32), inner_real, waves


def _exact(table):
    return np.asarray(table, np.float32).astype(ml_dtypes.bfloat16)


def _dot(left, right):
    return lax.dot_general(left, right, (((1,), (0,)), ((), ())), preferred_element_type=F32)


def _dot_nt(left, right):
    return lax.dot_general(left, right, (((1,), (1,)), ((), ())), preferred_element_type=F32)


def _split(value, count):
    out = []
    for i in range(count):
        piece = value.astype(BF16)
        out.append(piece)
        if i + 1 < count:
            value = value - piece.astype(F32)
    return out


PAIRS_3 = ((0, 0), (0, 1), (1, 0))
PAIRS_6 = ((0, 0), (0, 1), (1, 0), (1, 1), (0, 2), (2, 0))


def _passes(left, right, pairs, dot=_dot):
    total = None
    for i, j in reversed(pairs):
        term = dot(left[i], right[j])
        total = term if total is None else total + term
    return total


VMEM = pl.BlockSpec(memory_space=pltpu.VMEM)
SMEM = pl.BlockSpec(memory_space=pltpu.SMEM)


def _call(kernel, out_shape, in_specs, name, flops, nbytes, vmem):
    return pl.pallas_call(
        kernel,
        out_shape=out_shape,
        in_specs=in_specs,
        out_specs=jax.tree.map(lambda _: VMEM, out_shape),
        compiler_params=pltpu.CompilerParams(vmem_limit_bytes=vmem * MIB),
        cost_estimate=pl.CostEstimate(flops=flops, bytes_accessed=nbytes, transcendentals=0),
        name=name,
    )


def edges_kernel(state, pick, y_low, y_high, z_low, z_high):
    for q in range(4):
        rows = _dot(pick[...], state[q])
        y_low[q] = rows[0:96].astype(BF16)
        y_high[q] = rows[96:192].astype(BF16)
        z_low[q] = rows[192:216].astype(BF16)
        z_high[q] = rows[216:240].astype(BF16)


def local_kernel(metric, strain, state, z_below, z_above, along_x, along_y, partial, carrier):
    speeds = [state[q].astype(F32) for q in range(4)]
    contra = [
        metric[0, j] * speeds[0] + metric[1, j] * speeds[1] + metric[2, j] * speeds[2]
        for j in range(3)
    ]
    scale = -STEP / 60.0
    carrier[...] = scale * contra[1]
    for q in range(4):
        d_x = _dot(state[q], along_x[...])
        d_y = _dot(along_y[...], state[q])
        tall = jnp.concatenate(
            [z_below[q].astype(F32), speeds[q], z_above[q].astype(F32)], axis=0
        )

        def moved(k):
            return tall[(3 + k) * BY : (3 + k) * BY + CELLS]

        d_z = (
            45.0 * (moved(1) - moved(-1)) - 9.0 * (moved(2) - moved(-2)) + (moved(3) - moved(-3))
        )
        carried = contra[0] * d_x + contra[1] * d_y + contra[2] * d_z
        if q < 3:
            rest = strain[q, 0] * speeds[0] + strain[q, 1] * speeds[1] + strain[q, 2] * speeds[2]
            if q == 2:
                rest = rest - speeds[3]
        else:
            rest = speeds[2]
        partial[q] = speeds[q] + scale * carried - STEP * rest


def forward_kernel(
    metric, partial, carrier, y_below, y_above, along_y, spread, along_x, waves, provisional, heat, sent
):
    def complete(q):
        beside = jnp.concatenate([y_below[q], y_above[q]], axis=0)
        return partial[q] + carrier[...] * _dot(along_y[...], beside)

    heat[...] = complete(3)
    fields = [complete(q) for q in range(3)]
    for q in range(3):
        provisional[q] = fields[q]
    flux = [
        metric[0, j] * fields[0] + metric[1, j] * fields[1] + metric[2, j] * fields[2]
        for j in range(3)
    ]
    flux = [_split(f, 2) for f in flux]
    lows = jnp.concatenate([flux[1][1], flux[2][1]], axis=0)
    highs = jnp.concatenate([flux[1][0], flux[2][0]], axis=0)
    extended = _dot(spread[...], lows) + _dot(spread[...], highs)
    own = _dot(flux[0][1], along_x[...]) + _dot(flux[0][0], along_x[...])
    extended = jnp.concatenate([extended[:CELLS] + own, extended[CELLS:]], axis=0)
    pieces = _split(extended, 2)
    spectrum = _passes([waves[0], waves[1]], pieces, PAIRS_3, _dot_nt)
    for t in range(EXT // 128):
        sent[:, 4 * t : 4 * t + 4, :] = spectrum[:, 128 * t : 128 * t + 128].reshape(DEV, 4, 128)


def plane_kernel(
    metric, wave_x, got, outer, outer_back, twist, inner, inner_back, waves, sent
):
    here = lax.axis_index("gy") * GZ + lax.axis_index("gz")

    def received(c, part):
        return jnp.concatenate(
            [got[:, 4 * t + 2 * c + part, :] for t in range(EXT // 128)], axis=1
        )

    tr, ti = twist[0], twist[1]
    rows = []
    for c in range(2):
        block = jnp.concatenate([received(c, 0), received(c, 1)], axis=0)
        block = _passes([outer[0], outer[1]], _split(block, 2), PAIRS_3)
        re, im = block[:DEV], block[DEV:]
        rows.append(jnp.concatenate([re * tr - im * ti, re * ti + im * tr], axis=1))
    modes = _passes(
        _split(jnp.concatenate(rows, axis=0), 2), [inner[0], inner[1]], PAIRS_3
    )
    wave_y, wave_z, edge = waves[0], waves[1], waves[2]
    solved = []
    for c in range(2):
        wx = wave_x[2 * here + c]
        symbol = jnp.zeros((DEV, CELLS), F32)
        for i in range(3):
            mixed = metric[i, 0] * wx + metric[i, 1] * wave_y + metric[i, 2] * wave_z
            symbol = symbol + mixed * mixed
        out = (edge * jnp.where(2 * here + c == 0, 1.0, 0.0)) > 0.5
        factor = jnp.where(out, 0.0, -1.0 / (jnp.where(out, 1.0, symbol) * float(NX * NY * NZ)))
        block = modes[c * DEV : (c + 1) * DEV]
        solved.append(block * jnp.concatenate([factor, factor], axis=1))
    cells = _passes(
        _split(jnp.concatenate(solved, axis=0), 3),
        [inner_back[0], inner_back[1], inner_back[2]],
        PAIRS_6,
    )
    for c in range(2):
        re = cells[c * DEV : (c + 1) * DEV, :EXT]
        im = cells[c * DEV : (c + 1) * DEV, EXT:]
        block = jnp.concatenate([re * tr + im * ti, im * tr - re * ti], axis=0)
        block = _passes(
            [outer_back[0], outer_back[1], outer_back[2]], _split(block, 3), PAIRS_6
        )
        for part in range(2):
            for t in range(EXT // 128):
                sent[:, 4 * t + 2 * c + part, :] = block[
                    part * DEV : (part + 1) * DEV, 128 * t : 128 * t + 128
                ]


def project_kernel(metric, got, gather, inverse, slope, provisional, motion):
    rows = [
        jnp.concatenate([got[:, 4 * t + r, :] for t in range(EXT // 128)], axis=1)
        for r in range(4)
    ]
    pieces = _split(jnp.concatenate(rows, axis=0), 3)
    fields = None
    for piece in reversed(pieces):
        term = _dot_nt(gather[...], piece)
        fields = term if fields is None else fields + term
    pushes = []
    for j, table in enumerate((slope, inverse, inverse)):
        left = _split(fields[j * CELLS : (j + 1) * CELLS], 2)
        pushes.append(_passes(left, [table[0], table[1]], PAIRS_3))
    for i in range(3):
        motion[i] = provisional[i] - (
            metric[i, 0] * pushes[0] + metric[i, 1] * pushes[1] + metric[i, 2] * pushes[2]
        )


def _ring(count, shift):
    return [(i, (i + shift) % count) for i in range(count)]


def _step(state, metric, strain):
    along_y, along_z = _difference_matrices()
    forward, inverse, slope = _x_tables()
    outer, twist, inner, waves = _plane_tables()
    k = np.arange(NX // 2)
    wave_x = _kt(k, NX).astype(np.float32)
    wave_x[0] = 0.0
    pick = np.zeros((240, CELLS))
    own = [(w, y) for w in range(BZ) for y in range(BY)]
    place = {cell: i for i, cell in enumerate(own)}
    chosen = [(w, y) for w in range(BZ) for y in range(3)]
    chosen += [(w, y) for w in range(BZ) for y in range(BY - 3, BY)]
    chosen += [(w, y) for w in range(3) for y in range(BY)]
    chosen += [(w, y) for w in range(BZ - 3, BZ) for y in range(BY)]
    for i, cell in enumerate(chosen):
        pick[i, place[cell]] = 1.0
    circulant = _exact(_circulant_x())
    spread = _exact(-np.concatenate([along_y, along_z], axis=0).T)
    gather = _exact(np.concatenate([np.eye(CELLS, EXT), along_y, along_z], axis=0))

    field = jax.ShapeDtypeStruct((CELLS, NX), F32)
    fields = lambda count: jax.ShapeDtypeStruct((count, CELLS, NX), F32)
    block = jax.ShapeDtypeStruct((DEV, 16, 128), F32)
    state = state.reshape(4, CELLS, NX)

    y_side = jax.ShapeDtypeStruct((4, 96, NX), BF16)
    z_side = jax.ShapeDtypeStruct((4, 24, NX), BF16)
    y_low, y_high, z_low, z_high = _call(
        edges_kernel, (y_side, y_side, z_side, z_side), [VMEM, VMEM], "edges", 250_000_000, 2 * MIB, 16
    )(state, _exact(pick))
    y_below = lax.ppermute(y_high, "gy", _ring(GY, 1))
    y_above = lax.ppermute(y_low, "gy", _ring(GY, -1))
    z_below = lax.ppermute(z_high, "gz", _ring(GZ, 1))
    z_above = lax.ppermute(z_low, "gz", _ring(GZ, -1))

    partial, carrier = _call(
        local_kernel, (fields(4), field), [SMEM, SMEM] + [VMEM] * 5, "local", 1_000_000_000, 4 * MIB, 32
    )(metric, strain, state, z_below, z_above, circulant, _exact(along_y[:, :CELLS]))

    provisional, heat, sent = _call(
        forward_kernel,
        (fields(3), field, block),
        [SMEM] + [VMEM] * 8,
        "forward",
        2_000_000_000,
        8 * MIB,
        40,
    )(
        metric,
        partial,
        carrier,
        y_below,
        y_above,
        _exact(along_y[:, CELLS : CELLS + 192]),
        spread,
        circulant,
        _pieces(forward, 2),
    )
    got = lax.all_to_all(sent, ("gy", "gz"), split_axis=0, concat_axis=0, tiled=True)
    sent = _call(
        plane_kernel, block, [SMEM, SMEM] + [VMEM] * 7, "plane", 3_600_000_000, 8 * MIB, 48
    )(
        metric,
        wave_x,
        got,
        _pieces(outer, 2),
        _pieces(outer.T, 3),
        twist,
        _pieces(inner, 2),
        _pieces(inner.T, 3),
        waves,
    )
    got = lax.all_to_all(sent, ("gy", "gz"), split_axis=0, concat_axis=0, tiled=True)
    motion = _call(
        project_kernel, fields(3), [SMEM] + [VMEM] * 5, "project", 2_500_000_000, 8 * MIB, 40
    )(metric, got, gather, _pieces(inverse, 2), _pieces(slope, 2), provisional)
    return motion.reshape(3, BZ, BY, NX), heat.reshape(BZ, BY, NX)


def solution(mesh):
    return jax.shard_map(
        _step,
        mesh=mesh,
        in_specs=(P(None, "gz", "gy", None), P(), P()),
        out_specs=(P(None, "gz", "gy", None), P("gz", "gy", None)),
        check_vma=False,
    )
```

time: 413 us -> 102 us (0.25); the launches traced: 408 us -> 101 us
  local copies, waits for them, and re-layouts: 110 us -> 6.74 us
  other arithmetic: 87.2 us -> 0 us
  starting transfers between devices: 78.3 us -> 11.4 us
  matrix products: 59.4 us -> 0 us
  waiting for transfers between devices: 65.8 us -> 13.1 us
  blocking collectives: 0 us -> 50.3 us
  Pallas kernels: 0 us -> 18.9 us
  between operations: 7.43 us -> 0.84 us
    dot_general x20 -> x0, matrix products: 52.8 us -> none  [the longest x16 29.7 us: product(): return jnp.einsum(form, left, right, precision=highest)]
    all_to_all x0 -> x2, blocking collectives: none -> 50.3 us  [_step(): lax.all_to_all(sent, ('gy', 'gz'), split_axis=0, concat_axis=0, tiled=True)]
    all_to_all x8 -> x0, starting transfers between devices: 46.8 us -> none  [the longest x1 7.94 us: shards(): lax.all_to_all(real_part, 'gy', split_axis=2, concat_axis=1, tiled=True)]
    ppermute x12 -> x4, waiting for transfers between devices: 54.5 us -> 13.1 us  [the longest x1 9.02 us: _step(): z_below = lax.ppermute(z_high, 'gz', _ring(GZ, 1))]
    all_to_all x13 -> x0, local copies, waits for them, and re-layouts: 29.8 us -> none  [the longest x2 6.29 us: shards(): lax.all_to_all(imag_part, 'gy', split_axis=2, concat_axis=1, tiled=True)]
    unnamed x40 -> x42, local copies, waits for them, and re-layouts: 36.4 us -> 6.74 us
    add x10 -> x0, other arithmetic: 29.1 us -> none  [the longest x1 8.65 us: shards(): flow_compressibility + metric[vector_entry, 0] * slope_x[vector_entry]]
    all_to_all x8 -> x0, other arithmetic: 23.2 us -> none  [the longest x1 3.81 us: shards(): lax.all_to_all(real_part, 'gz', split_axis=0, concat_axis=2, tiled=True)]
  transfers between devices with their start and end apart: 20 -> 4, of which waited for: 12 -> 2; matrix products, arithmetic and copies ran while one was open for 25% -> 0% of each run, Pallas kernels for 0% -> 3%
where the time goes in v1:
time: 102 us; the launch traced here: 101 us
  blocking collectives  50.3 us (49%)
  Pallas kernels  18.9 us (19%)
  waiting for transfers between devices  13.1 us (13%)
  starting transfers between devices  11.4 us (11%)
  local copies, waits for them, and re-layouts  6.74 us (7%)
    all_to_all x2, blocking collectives, _step(): lax.all_to_all(sent, ('gy', 'gz'), split_axis=0, concat_axis=0, tiled=True)  50.3 us
    ppermute x1, waiting for transfers between devices, _step(): z_below = lax.ppermute(z_high, 'gz', _ring(GZ, 1))  9.02 us
    pallas_call x1, Pallas kernels, _step(): _call(plane_kernel, block, [SMEM, SMEM] + [VMEM] * 7, 'plane', 3600000000...  7.45 us
    unnamed x42, local copies, waits for them, and re-layouts  6.74 us
    ppermute x1, starting transfers between devices, _step(): y_above = lax.ppermute(y_low, 'gy', _ring(GY, -1))  6.01 us
    pallas_call x1, Pallas kernels, _step(): _call(project_kernel, fields(3), [SMEM] + [VMEM] * 5, 'project', 25000000...  5.07 us
    ppermute x1, waiting for transfers between devices, _step(): z_above = lax.ppermute(z_low, 'gz', _ring(GZ, -1))  4.04 us
    ppermute x1, starting transfers between devices, _step(): z_below = lax.ppermute(z_high, 'gz', _ring(GZ, 1))  3.29 us
  transfers between devices with their start and end apart: 4, of which 2 were waited for; matrix products, arithmetic and copies ran while one was open for 0% of the time, Pallas kernels for 3%

profile of v1, /device:TPU:1, one launch (start us, length us, event | category | flops | bytes accessed | tf_op | source)
XLA Modules:
  0.0 101.3 jit_solution(16708693350566284596)
XLA Ops:
  0.6 0.0 copy-start
  0.6 1.2 %copy-done = bf16[4,32,8,512]{3,2,1,0:T(8,128)(2,1)S(1)} copy-done((bf16[4,32,8,512]{3,2,1,0:T(8,128)(2,1)S(1)}, bf16[4,32,8,512]{3,2,1,0:T(8,128)(2,1)}, u32[]{:S(2)}) %copy-start) | copy-done | bytes 1048600
  1.9 0.0 copy-start.2
  1.9 0.9 copy-done.2
  2.8 0.0 copy-start.9
  2.8 0.4 edges.1
  3.2 0.0 copy-start.5
  3.2 2.1 %collective-permute-start.2 = (bf16[4,96,512]{2,1,0:T(8,128)(2,1)S(1)}, bf16[4,96,512]{2,1,0:T(8,128)(2,1)S(1)}, u32[]{:S(2)}, u32[]{:S(2)}) collective-permute-start(bf16[4,96,512]{2,1,0:T(8,128)(2,1)S(1)} %get-tuple-element.15), channel_id=1, source_target_pairs={{0,4},{4,8},{8,12},{12,16},{16,20},{20,24},{24,28},{28,32},{32,36}... | collective-permute-start | bytes 1179656 | tf_op jit(solution)/shard_map/ppermute | solution.py:338
  5.3 6.0 %collective-permute-start.3 = (bf16[4,96,512]{2,1,0:T(8,128)(2,1)S(1)}, bf16[4,96,512]{2,1,0:T(8,128)(2,1)S(1)}, u32[]{:S(2)}, u32[]{:S(2)}) collective-permute-start(bf16[4,96,512]{2,1,0:T(8,128)(2,1)S(1)} %get-tuple-element.16), channel_id=1, source_target_pairs={{0,124},{4,0},{8,4},{12,8},{16,12},{20,16},{24,20},{28,24},{32,28}... | collective-permute-start | bytes 1179656 | tf_op jit(solution)/shard_map/ppermute | solution.py:339
  11.3 3.3 %collective-permute-start = (bf16[4,24,512]{2,1,0:T(8,128)(2,1)S(1)}, bf16[4,24,512]{2,1,0:T(8,128)(2,1)S(1)}, u32[]{:S(2)}, u32[]{:S(2)}) collective-permute-start(bf16[4,24,512]{2,1,0:T(8,128)(2,1)S(1)} %get-tuple-element.11), channel_id=1, source_target_pairs={{0,1},{1,2},{2,3},{3,0},{4,5},{5,6},{6,7},{7,4},{8,9},{9,10},{10,1... | collective-permute-start | bytes 294920 | tf_op jit(solution)/shard_map/ppermute | solution.py:340
  14.6 0.0 collective-permute-start.1
  14.6 9.0 %collective-permute-done.z_below = bf16[4,24,512]{2,1,0:T(8,128)(2,1)S(1)} collective-permute-done((bf16[4,24,512]{2,1,0:T(8,128)(2,1)S(1)}, bf16[4,24,512]{2,1,0:T(8,128)(2,1)S(1)}, u32[]{:S(2)}, u32[]{:S(2)}) %collective-permute-start) | collective-permute-done | bytes 98336 | tf_op jit(solution)/shard_map/ppermute | solution.py:340
  23.6 4.0 %collective-permute-done.1.z_above = bf16[4,24,512]{2,1,0:T(8,128)(2,1)S(1)} collective-permute-done((bf16[4,24,512]{2,1,0:T(8,128)(2,1)S(1)}, bf16[4,24,512]{2,1,0:T(8,128)(2,1)S(1)}, u32[]{:S(2)}, u32[]{:S(2)}) %collective-permute-start.1) | collective-permute-done | bytes 98336 | tf_op jit(solution)/shard_map/ppermute | solution.py:341
  27.7 0.0 copy-start.1
  27.7 1.2 %copy-done.1 = bf16[4,32,8,512]{3,2,1,0:T(8,128)(2,1)S(1)} copy-done((bf16[4,32,8,512]{3,2,1,0:T(8,128)(2,1)S(1)}, bf16[4,32,8,512]{3,2,1,0:T(8,128)(2,1)}, u32[]{:S(2)}) %copy-start.1) | copy-done | bytes 1048600
  28.9 0.0 copy-start.3
  28.9 0.7 copy-done.3
  29.6 0.0 copy-start.4
  29.6 0.7 copy-done.4
  30.3 0.0 copy-start.12
  30.3 1.0 %copy-done.12 = bf16[512,512]{1,0:T(8,128)(2,1)S(1)} copy-done((bf16[512,512]{1,0:T(8,128)(2,1)S(1)}, bf16[512,512]{1,0:T(8,128)(2,1)}, u32[]{:S(2)}) %copy-start.12) | copy-done | bytes 524312
  31.3 0.0 copy-start.19
  31.3 0.9 copy-done.19
  32.2 0.0 copy-start.13
  32.2 0.0 copy-start.14
  32.2 0.0 copy-start.18
  32.2 2.8 %local.1 = (f32[4,256,512]{2,1,0:T(8,128)S(1)}, f32[256,512]{1,0:T(8,128)S(1)}) custom-call(f32[3,3]{1,0:T(4,128)S(1)} %copy-done.4, f32[3,3]{1,0:T(4,128)S(1)} %copy-done.3, bf16[4,256,512]{2,1,0:T(8,128)(2,1)S(1)} %bitcast.4, bf16[4,24,512]{2,1,0:T(8,128)(2,1)S(1)} %collective-permute-done.z_below, bf16[4,24,512]{2,1,0:T(8,128)(2,1)S(1)} %collective-permute-done.1.z_above, ...), custom_call_target="tpu_custom_call" | custom-call | flops 1000000000 | bytes 4194304 | tf_op jit(solution)/shard_map/local/pallas_call | solution.py:343
  35.0 0.0 collective-permute-done.2.y_below
  35.0 0.0 collective-permute-done.3.y_above
  35.0 0.0 copy-done.9
  35.0 0.0 copy-done.5
  35.0 0.0 copy-done.13
  35.1 0.0 copy-done.14
  35.1 0.0 copy-done.18
  35.1 0.0 copy-start.11
  35.1 0.0 copy-start.15
  35.1 0.0 copy-start.16
  35.1 0.0 copy-start.17
  35.1 3.2 %forward.1 = (f32[3,256,512]{2,1,0:T(8,128)S(1)}, f32[256,512]{1,0:T(8,128)}, f32[128,16,128]{2,1,0:T(8,128)S(1)}) custom-call(f32[3,3]{1,0:T(4,128)S(1)} %copy-done.5, f32[4,256,512]{2,1,0:T(8,128)S(1)} %get-tuple-element.13.partial, f32[256,512]{1,0:T(8,128)S(1)} %get-tuple-element.14.carrier, bf16[4,96,512]{2,1,0:T(8,128)(2,1)S(1)} %collective-permute-done.2.y_below, ...), custom_call_target="tpu_custom_call" | custom-call | flops 2000000000 | bytes 8388608 | tf_op jit(solution)/shard_map/forward/pallas_call | solution.py:347
  38.3 0.0 copy-start.6
  38.3 0.0 copy-start.20
  38.4 27.3 %all_to_all.10.got = f32[128,16,128]{2,1,0:T(8,128)S(1)} all-to-all(f32[128,16,128]{2,1,0:T(8,128)S(1)} %get-tuple-element.17), channel_id=1, replica_groups=mesh['gy'=32,'gz'=4] {'gy','gz'}, dimensions={0} | all-to-all | bytes 2097152 | tf_op jit(solution)/shard_map/all_to_all | solution.py:366
  65.7 0.0 copy-done.11
  65.7 0.0 copy-done.15
  65.7 0.0 copy-done.16
  65.7 0.0 copy-done.17
  65.7 0.0 copy-done.6
  65.7 0.0 copy-done.20
  65.7 0.0 copy-start.10
  65.7 7.5 %plane.1 = f32[128,16,128]{2,1,0:T(8,128)S(1)} custom-call(f32[3,3]{1,0:T(4,128)S(1)} %copy-done.5, f32[256]{0:T(256)S(1)} %copy-done.20, f32[128,16,128]{2,1,0:T(8,128)S(1)} %all_to_all.10.got, bf16[2,256,256]{2,1,0:T(8,128)(2,1)S(1)} %copy-done.17, bf16[3,256,256]{2,1,0:T(8,128)(2,1)S(1)} %copy-done.16, f32[2,128,512]{2,1,0:T(8,128)S(1)} %copy-done.11, ...), custom_call_target="tpu_custom_call" | custom-call | flops 3600000000 | bytes 8388608 | tf_op jit(solution)/shard_map/plane/pallas_call | solution.py:367
  73.2 0.0 copy-start.7
  73.2 0.0 copy-start.8
  73.2 23.0 %all_to_all.11.got = f32[128,16,128]{2,1,0:T(8,128)S(1)} all-to-all(f32[128,16,128]{2,1,0:T(8,128)S(1)} %plane.1), channel_id=1, replica_groups=mesh['gy'=32,'gz'=4] {'gy','gz'}, dimensions={0} | all-to-all | bytes 2097152 | tf_op jit(solution)/shard_map/all_to_all | solution.py:380
  96.2 0.0 copy-done.10
  96.2 0.0 copy-done.7
  96.2 0.0 copy-done.8
  96.2 5.1 %project.1 = f32[3,256,512]{2,1,0:T(8,128)} custom-call(f32[3,3]{1,0:T(4,128)S(1)} %copy-done.5, f32[128,16,128]{2,1,0:T(8,128)S(1)} %all_to_all.11.got, bf16[768,512]{1,0:T(8,128)(2,1)S(1)} %copy-done.10, bf16[2,512,512]{2,1,0:T(8,128)(2,1)S(1)} %copy-done.8, bf16[2,512,512]{2,1,0:T(8,128)(2,1)S(1)} %copy-done.7, ...), custom_call_target="tpu_custom_call" | custom-call | flops 2500000000 | bytes 8388608 | tf_op jit(solution)/shard_map/project/pallas_call | solution.py:381
Async XLA Ops:
  0.6 1.2 %copy-start = (bf16[4,32,8,512]{3,2,1,0:T(8,128)(2,1)S(1)}, bf16[4,32,8,512]{3,2,1,0:T(8,128)(2,1)}, u32[]{:S(2)}) copy-start(bf16[4,32,8,512]{3,2,1,0:T(8,128)(2,1)} %param.19) | copy-start | bytes 3145732
  1.9 0.9 copy-start.2
  2.8 32.3 %copy-start.9 = (bf16[2,512,512]{2,1,0:T(8,128)(2,1)S(1)}, bf16[2,512,512]{2,1,0:T(8,128)(2,1)}, u32[]{:S(2)}) copy-start(bf16[2,512,512]{2,1,0:T(8,128)(2,1)} %constant.37.clone.waves) | copy-start | bytes 3145732
  3.2 31.9 %copy-start.5 = (f32[3,3]{1,0:T(4,128)S(1)}, f32[3,3]{1,0:T(4,128)}, u32[]{:S(2)}) copy-start(f32[3,3]{1,0:T(4,128)} %metric.7) | copy-start | bytes 112
  3.2 31.8 %collective-permute-start.2 = (bf16[4,96,512]{2,1,0:T(8,128)(2,1)S(1)}, bf16[4,96,512]{2,1,0:T(8,128)(2,1)S(1)}, u32[]{:S(2)}, u32[]{:S(2)}) collective-permute-start(bf16[4,96,512]{2,1,0:T(8,128)(2,1)S(1)} %get-tuple-element.15), channel_id=1, source_target_pairs={{0,4},{4,8},{8,12},{12,16},{16,20},{20,24},{24,28},{28,32},{32,36}... | collective-permute-start | bytes 1179656 | tf_op jit(solution)/shard_map/ppermute | solution.py:338
  5.3 29.7 %collective-permute-start.3 = (bf16[4,96,512]{2,1,0:T(8,128)(2,1)S(1)}, bf16[4,96,512]{2,1,0:T(8,128)(2,1)S(1)}, u32[]{:S(2)}, u32[]{:S(2)}) collective-permute-start(bf16[4,96,512]{2,1,0:T(8,128)(2,1)S(1)} %get-tuple-element.16), channel_id=1, source_target_pairs={{0,124},{4,0},{8,4},{12,8},{16,12},{20,16},{24,20},{28,24},{32,28}... | collective-permute-start | bytes 1179656 | tf_op jit(solution)/shard_map/ppermute | solution.py:339
  11.3 12.3 %collective-permute-start = (bf16[4,24,512]{2,1,0:T(8,128)(2,1)S(1)}, bf16[4,24,512]{2,1,0:T(8,128)(2,1)S(1)}, u32[]{:S(2)}, u32[]{:S(2)}) collective-permute-start(bf16[4,24,512]{2,1,0:T(8,128)(2,1)S(1)} %get-tuple-element.11), channel_id=1, source_target_pairs={{0,1},{1,2},{2,3},{3,0},{4,5},{5,6},{6,7},{7,4},{8,9},{9,10},{10,1... | collective-permute-start | bytes 294920 | tf_op jit(solution)/shard_map/ppermute | solution.py:340
  14.6 13.1 %collective-permute-start.1 = (bf16[4,24,512]{2,1,0:T(8,128)(2,1)S(1)}, bf16[4,24,512]{2,1,0:T(8,128)(2,1)S(1)}, u32[]{:S(2)}, u32[]{:S(2)}) collective-permute-start(bf16[4,24,512]{2,1,0:T(8,128)(2,1)S(1)} %get-tuple-element.12), channel_id=1, source_target_pairs={{0,3},{1,0},{2,1},{3,2},{4,7},{5,4},{6,5},{7,6},{8,11},{9,8},{10,9... | collective-permute-start | bytes 294920 | tf_op jit(solution)/shard_map/ppermute | solution.py:341
  27.7 1.2 %copy-start.1 = (bf16[4,32,8,512]{3,2,1,0:T(8,128)(2,1)S(1)}, bf16[4,32,8,512]{3,2,1,0:T(8,128)(2,1)}, u32[]{:S(2)}) copy-start(bf16[4,32,8,512]{3,2,1,0:T(8,128)(2,1)} %param.19) | copy-start | bytes 3145732
  28.9 0.7 copy-start.3
  29.6 0.7 copy-start.4
  30.3 1.0 %copy-start.12 = (bf16[512,512]{1,0:T(8,128)(2,1)S(1)}, bf16[512,512]{1,0:T(8,128)(2,1)}, u32[]{:S(2)}) copy-start(bf16[512,512]{1,0:T(8,128)(2,1)} %constant.33.clone.along_x) | copy-start | bytes 1572868
  31.3 0.9 copy-start.19
  32.2 2.8 %copy-start.13 = (bf16[512,512]{1,0:T(8,128)(2,1)S(1)}, bf16[512,512]{1,0:T(8,128)(2,1)}, u32[]{:S(2)}) copy-start(bf16[512,512]{1,0:T(8,128)(2,1)} %constant.33.clone.along_x) | copy-start | bytes 1572868
  32.2 2.9 %copy-start.14 = (bf16[512,512]{1,0:T(8,128)(2,1)S(1)}, bf16[512,512]{1,0:T(8,128)(2,1)}, u32[]{:S(2)}) copy-start(bf16[512,512]{1,0:T(8,128)(2,1)} %constant.36.clone.spread) | copy-start | bytes 1572868
  32.2 2.9 %copy-start.18 = (bf16[256,192]{1,0:T(8,128)(2,1)S(1)}, bf16[256,192]{1,0:T(8,128)(2,1)}, u32[]{:S(2)}) copy-start(bf16[256,192]{1,0:T(8,128)(2,1)} %constant.35.clone.along_y) | copy-start | bytes 294916
  35.1 30.6 %copy-start.11 = (f32[2,128,512]{2,1,0:T(8,128)S(1)}, f32[2,128,512]{2,1,0:T(8,128)}, u32[]{:S(2)}) copy-start(f32[2,128,512]{2,1,0:T(8,128)} %constant.41.clone.twist) | copy-start | bytes 1572868
  35.1 30.6 %copy-start.15 = (f32[3,128,256]{2,1,0:T(8,128)S(1)}, f32[3,128,256]{2,1,0:T(8,128)}, u32[]{:S(2)}) copy-start(f32[3,128,256]{2,1,0:T(8,128)} %constant.44.clone.waves) | copy-start | bytes 1179652
  35.1 30.6 %copy-start.16 = (bf16[3,256,256]{2,1,0:T(8,128)(2,1)S(1)}, bf16[3,256,256]{2,1,0:T(8,128)(2,1)}, u32[]{:S(2)}) copy-start(bf16[3,256,256]{2,1,0:T(8,128)(2,1)} %constant.40.clone.outer_back) | copy-start | bytes 1179652
  35.1 30.6 %copy-start.17 = (bf16[2,256,256]{2,1,0:T(8,128)(2,1)S(1)}, bf16[2,256,256]{2,1,0:T(8,128)(2,1)}, u32[]{:S(2)}) copy-start(bf16[2,256,256]{2,1,0:T(8,128)(2,1)} %constant.39.clone.outer) | copy-start | bytes 786436
  38.3 27.3 %copy-start.6 = (bf16[2,1024,512]{2,1,0:T(8,128)(2,1)S(1)}, bf16[2,1024,512]{2,1,0:T(8,128)(2,1)}, u32[]{:S(2)}) copy-start(bf16[2,1024,512]{2,1,0:T(8,128)(2,1)} %constant.42.clone.inner) | copy-start | bytes 6291460
  38.3 27.3 %copy-start.20 = (f32[256]{0:T(256)S(1)}, f32[256]{0:T(256)}, u32[]{:S(2)}) copy-start(f32[256]{0:T(256)} %constant.38.clone.wave_x) | copy-start | bytes 3076
  65.7 30.5 %copy-start.10 = (bf16[768,512]{1,0:T(8,128)(2,1)S(1)}, bf16[768,512]{1,0:T(8,128)(2,1)}, u32[]{:S(2)}) copy-start(bf16[768,512]{1,0:T(8,128)(2,1)} %constant.45.clone.gather) | copy-start | bytes 2359300
  73.2 23.0 %copy-start.7 = (bf16[2,512,512]{2,1,0:T(8,128)(2,1)S(1)}, bf16[2,512,512]{2,1,0:T(8,128)(2,1)}, u32[]{:S(2)}) copy-start(bf16[2,512,512]{2,1,0:T(8,128)(2,1)} %constant.47.clone.slope) | copy-start | bytes 3145732
  73.2 23.0 %copy-start.8 = (bf16[2,512,512]{2,1,0:T(8,128)(2,1)S(1)}, bf16[2,512,512]{2,1,0:T(8,128)(2,1)}, u32[]{:S(2)}) copy-start(bf16[2,512,512]{2,1,0:T(8,128)(2,1)} %constant.46.clone.inverse) | copy-start | bytes 3145732

commit v2 on v1

--- a/solution.py
+++ b/solution.py
@@ -135,57 +135,87 @@
     return out
 
 
-PAIRS_3 = ((0, 0), (0, 1), (1, 0))
-PAIRS_6 = ((0, 0), (0, 1), (1, 0), (1, 1), (0, 2), (2, 0))
-
-
-def _passes(left, right, pairs, dot=_dot):
+def _by_table(pieces, table, depth):
     total = None
-    for i, j in reversed(pairs):
-        term = dot(left[i], right[j])
+    for i in reversed(range(len(pieces))):
+        count = len(pieces) - i
+        left = jnp.concatenate([pieces[i]] * count, axis=1) if count > 1 else pieces[i]
+        term = _dot(left, table[: depth * count])
         total = term if total is None else total + term
     return total
 
 
+def _table_by(table, pieces, depth):
+    total = None
+    for i in reversed(range(len(pieces))):
+        count = len(pieces) - i
+        right = jnp.concatenate([pieces[i]] * count, axis=0) if count > 1 else pieces[i]
+        term = _dot(table[:, : depth * count], right)
+        total = term if total is None else total + term
+    return total
+
+
 VMEM = pl.BlockSpec(memory_space=pltpu.VMEM)
 SMEM = pl.BlockSpec(memory_space=pltpu.SMEM)
-
-
-def _call(kernel, out_shape, in_specs, name, flops, nbytes, vmem):
+ANY = pl.BlockSpec(memory_space=pl.ANY)
+
+
+def _call(kernel, out_shape, in_specs, name, flops, nbytes, vmem, scratch_shapes=(), out_specs=None):
     return pl.pallas_call(
         kernel,
         out_shape=out_shape,
         in_specs=in_specs,
-        out_specs=jax.tree.map(lambda _: VMEM, out_shape),
+        out_specs=out_specs or jax.tree.map(lambda _: VMEM, out_shape),
+        scratch_shapes=scratch_shapes,
         compiler_params=pltpu.CompilerParams(vmem_limit_bytes=vmem * MIB),
         cost_estimate=pl.CostEstimate(flops=flops, bytes_accessed=nbytes, transcendentals=0),
         name=name,
     )
 
 
-def edges_kernel(state, pick, y_low, y_high, z_low, z_high):
-    for q in range(4):
-        rows = _dot(pick[...], state[q])
-        y_low[q] = rows[0:96].astype(BF16)
-        y_high[q] = rows[96:192].astype(BF16)
-        z_low[q] = rows[192:216].astype(BF16)
-        z_high[q] = rows[216:240].astype(BF16)
-
-
-def local_kernel(metric, strain, state, z_below, z_above, along_x, along_y, partial, carrier):
+def _picked(state):
+    row = lax.broadcasted_iota(jnp.int32, (240, CELLS), 0)
+    column = lax.broadcasted_iota(jnp.int32, (240, CELLS), 1)
+    high = row >= 96
+    within = jnp.where(high, row - 96, row)
+    third = (within * 171) >> 9
+    along_y = BY * third + (within - 3 * third) + jnp.where(high, BY - 3, 0)
+    along_z = jnp.where(row >= 216, row - 216 + CELLS - 24, row - 192)
+    source = jnp.where(row >= 192, along_z, along_y)
+    pick = jnp.where(column == source, 1.0, 0.0).astype(BF16)
+    return [_dot(pick, value) for value in state]
+
+
+def _store_sides(q, rows, y_low, y_high, z_low, z_high):
+    y_low[q] = rows[0:96].astype(BF16)
+    y_high[q] = rows[96:192].astype(BF16)
+    z_low[q] = rows[192:216].astype(BF16)
+    z_high[q] = rows[216:240].astype(BF16)
+
+
+def edges_kernel(state, *sides):
+    for q, rows in enumerate(_picked([state[q] for q in range(4)])):
+        _store_sides(q, rows, *sides)
+
+
+def local_kernel(
+    metric, strain, state, along, partial, carrier_y, carrier_z
+):
+    along_x, along_y = along[:NX], along[NX:, :CELLS]
     speeds = [state[q].astype(F32) for q in range(4)]
     contra = [
         metric[0, j] * speeds[0] + metric[1, j] * speeds[1] + metric[2, j] * speeds[2]
         for j in range(3)
     ]
     scale = -STEP / 60.0
-    carrier[...] = scale * contra[1]
+    carrier_y[...] = scale * contra[1]
+    carrier_z[0:24] = scale * contra[2][0:24]
+    carrier_z[24:48] = scale * contra[2][CELLS - 24 :]
+    nothing = jnp.zeros((24, NX), F32)
     for q in range(4):
-        d_x = _dot(state[q], along_x[...])
-        d_y = _dot(along_y[...], state[q])
-        tall = jnp.concatenate(
-            [z_below[q].astype(F32), speeds[q], z_above[q].astype(F32)], axis=0
-        )
+        d_x = _dot(state[q], along_x)
+        d_y = _dot(along_y, state[q])
+        tall = jnp.concatenate([nothing, speeds[q], nothing], axis=0)
 
         def moved(k):
             return tall[(3 + k) * BY : (3 + k) * BY + CELLS]
@@ -203,15 +233,43 @@
         partial[q] = speeds[q] + scale * carried - STEP * rest
 
 
+def _complete(q, partial, carrier_y, carrier_z, y_below, y_above, z_below, z_above, along_y, along_z):
+    beside = jnp.concatenate([y_below[q], y_above[q]], axis=0)
+    whole = partial + carrier_y[...] * _dot(along_y[...], beside)
+    low = whole[:24] + carrier_z[0:24] * _dot(along_z[0], z_below[q])
+    high = whole[CELLS - 24 :] + carrier_z[24:48] * _dot(along_z[1], z_above[q])
+    return jnp.concatenate([low, whole[24 : CELLS - 24], high], axis=0)
+
+
 def forward_kernel(
-    metric, partial, carrier, y_below, y_above, along_y, spread, along_x, waves, provisional, heat, sent
+    metric,
+    partial,
+    carrier_y,
+    carrier_z,
+    y_below,
+    y_above,
+    z_below,
+    z_above,
+    along_y,
+    along_z,
+    spread,
+    along_x,
+    waves,
+    provisional,
+    sent,
+    heat,
+    held,
+    done,
 ):
-    def complete(q):
-        beside = jnp.concatenate([y_below[q], y_above[q]], axis=0)
-        return partial[q] + carrier[...] * _dot(along_y[...], beside)
-
-    heat[...] = complete(3)
-    fields = [complete(q) for q in range(3)]
+    fields = [
+        _complete(
+            q, partial[q], carrier_y, carrier_z, y_below, y_above, z_below, z_above, along_y, along_z
+        )
+        for q in range(4)
+    ]
+    held[...] = fields[3]
+    copy = pltpu.make_async_copy(held, heat, done)
+    copy.start()
     for q in range(3):
         provisional[q] = fields[q]
     flux = [
@@ -219,37 +277,46 @@
         for j in range(3)
     ]
     flux = [_split(f, 2) for f in flux]
-    lows = jnp.concatenate([flux[1][1], flux[2][1]], axis=0)
-    highs = jnp.concatenate([flux[1][0], flux[2][0]], axis=0)
-    extended = _dot(spread[...], lows) + _dot(spread[...], highs)
-    own = _dot(flux[0][1], along_x[...]) + _dot(flux[0][0], along_x[...])
+    stacked = jnp.concatenate([flux[1][0], flux[2][0], flux[1][1], flux[2][1]], axis=0)
+    extended = _dot(spread[...], stacked)
+    own = _dot(jnp.concatenate(flux[0], axis=1), along_x[...])
     extended = jnp.concatenate([extended[:CELLS] + own, extended[CELLS:]], axis=0)
-    pieces = _split(extended, 2)
-    spectrum = _passes([waves[0], waves[1]], pieces, PAIRS_3, _dot_nt)
+    high, low = _split(extended, 2)
+    spectrum = _dot_nt(waves[:, :NX], low) + _dot_nt(
+        waves[...], jnp.concatenate([high, high], axis=1)
+    )
     for t in range(EXT // 128):
         sent[:, 4 * t : 4 * t + 4, :] = spectrum[:, 128 * t : 128 * t + 128].reshape(DEV, 4, 128)
+    copy.wait()
 
 
 def plane_kernel(
-    metric, wave_x, got, outer, outer_back, twist, inner, inner_back, waves, sent
+    metric,
+    wave_x,
+    got,
+    outer,
+    outer_back,
+    twist,
+    inner,
+    inner_back,
+    waves,
+    sent,
 ):
     here = lax.axis_index("gy") * GZ + lax.axis_index("gz")
 
-    def received(c, part):
+    def received(part):
         return jnp.concatenate(
-            [got[:, 4 * t + 2 * c + part, :] for t in range(EXT // 128)], axis=1
+            [got[:, 4 * t + 2 * c + part, :] for c in range(2) for t in range(EXT // 128)], axis=1
         )
 
     tr, ti = twist[0], twist[1]
+    block = jnp.concatenate([received(0), received(1)], axis=0)
+    block = _table_by(outer, _split(block, 2), 2 * DEV)
     rows = []
     for c in range(2):
-        block = jnp.concatenate([received(c, 0), received(c, 1)], axis=0)
-        block = _passes([outer[0], outer[1]], _split(block, 2), PAIRS_3)
-        re, im = block[:DEV], block[DEV:]
+        re, im = block[:DEV, c * EXT : (c + 1) * EXT], block[DEV:, c * EXT : (c + 1) * EXT]
         rows.append(jnp.concatenate([re * tr - im * ti, re * ti + im * tr], axis=1))
-    modes = _passes(
-        _split(jnp.concatenate(rows, axis=0), 2), [inner[0], inner[1]], PAIRS_3
-    )
+    modes = _by_table(_split(jnp.concatenate(rows, axis=0), 2), inner, 2 * EXT)
     wave_y, wave_z, edge = waves[0], waves[1], waves[2]
     solved = []
     for c in range(2):
@@ -262,23 +329,18 @@
         factor = jnp.where(out, 0.0, -1.0 / (jnp.where(out, 1.0, symbol) * float(NX * NY * NZ)))
         block = modes[c * DEV : (c + 1) * DEV]
         solved.append(block * jnp.concatenate([factor, factor], axis=1))
-    cells = _passes(
-        _split(jnp.concatenate(solved, axis=0), 3),
-        [inner_back[0], inner_back[1], inner_back[2]],
-        PAIRS_6,
-    )
+    cells = _by_table(_split(jnp.concatenate(solved, axis=0), 3), inner_back, 2 * CELLS)
+    columns = []
     for c in range(2):
         re = cells[c * DEV : (c + 1) * DEV, :EXT]
         im = cells[c * DEV : (c + 1) * DEV, EXT:]
-        block = jnp.concatenate([re * tr + im * ti, im * tr - re * ti], axis=0)
-        block = _passes(
-            [outer_back[0], outer_back[1], outer_back[2]], _split(block, 3), PAIRS_6
-        )
+        columns.append(jnp.concatenate([re * tr + im * ti, im * tr - re * ti], axis=0))
+    block = _table_by(outer_back, _split(jnp.concatenate(columns, axis=1), 3), 2 * DEV)
+    for c in range(2):
         for part in range(2):
             for t in range(EXT // 128):
-                sent[:, 4 * t + 2 * c + part, :] = block[
-                    part * DEV : (part + 1) * DEV, 128 * t : 128 * t + 128
-                ]
+                at = c * EXT + 128 * t
+                sent[:, 4 * t + 2 * c + part, :] = block[part * DEV : (part + 1) * DEV, at : at + 128]
 
 
 def project_kernel(metric, got, gather, inverse, slope, provisional, motion):
@@ -286,15 +348,12 @@
         jnp.concatenate([got[:, 4 * t + r, :] for t in range(EXT // 128)], axis=1)
         for r in range(4)
     ]
-    pieces = _split(jnp.concatenate(rows, axis=0), 3)
-    fields = None
-    for piece in reversed(pieces):
-        term = _dot_nt(gather[...], piece)
-        fields = term if fields is None else fields + term
+    pieces = jnp.concatenate(_split(jnp.concatenate(rows, axis=0), 3), axis=1)
+    fields = _dot_nt(gather[...], pieces)
     pushes = []
     for j, table in enumerate((slope, inverse, inverse)):
         left = _split(fields[j * CELLS : (j + 1) * CELLS], 2)
-        pushes.append(_passes(left, [table[0], table[1]], PAIRS_3))
+        pushes.append(_by_table(left, table, NX))
     for i in range(3):
         motion[i] = provisional[i] - (
             metric[i, 0] * pushes[0] + metric[i, 1] * pushes[1] + metric[i, 2] * pushes[2]
@@ -312,75 +371,95 @@
     k = np.arange(NX // 2)
     wave_x = _kt(k, NX).astype(np.float32)
     wave_x[0] = 0.0
-    pick = np.zeros((240, CELLS))
-    own = [(w, y) for w in range(BZ) for y in range(BY)]
-    place = {cell: i for i, cell in enumerate(own)}
-    chosen = [(w, y) for w in range(BZ) for y in range(3)]
-    chosen += [(w, y) for w in range(BZ) for y in range(BY - 3, BY)]
-    chosen += [(w, y) for w in range(3) for y in range(BY)]
-    chosen += [(w, y) for w in range(BZ - 3, BZ) for y in range(BY)]
-    for i, cell in enumerate(chosen):
-        pick[i, place[cell]] = 1.0
     circulant = _exact(_circulant_x())
     spread = _exact(-np.concatenate([along_y, along_z], axis=0).T)
+    spread = np.concatenate([spread, spread], axis=1)
     gather = _exact(np.concatenate([np.eye(CELLS, EXT), along_y, along_z], axis=0))
+    gather = np.concatenate([gather] * 3, axis=1)
+    beside_y = _exact(along_y[:, CELLS : CELLS + 192])
+    beside_z = _exact(
+        np.stack([along_z[:24, CELLS + 192 : CELLS + 216], along_z[CELLS - 24 :, CELLS + 216 : CELLS + 240]])
+    )
+    local = np.zeros((NX + CELLS, NX))
+    local[:NX] = _circulant_x()
+    local[NX:, :CELLS] = along_y[:, :CELLS]
 
     field = jax.ShapeDtypeStruct((CELLS, NX), F32)
     fields = lambda count: jax.ShapeDtypeStruct((count, CELLS, NX), F32)
     block = jax.ShapeDtypeStruct((DEV, 16, 128), F32)
     state = state.reshape(4, CELLS, NX)
 
-    y_side = jax.ShapeDtypeStruct((4, 96, NX), BF16)
-    z_side = jax.ShapeDtypeStruct((4, 24, NX), BF16)
-    y_low, y_high, z_low, z_high = _call(
-        edges_kernel, (y_side, y_side, z_side, z_side), [VMEM, VMEM], "edges", 250_000_000, 2 * MIB, 16
-    )(state, _exact(pick))
-    y_below = lax.ppermute(y_high, "gy", _ring(GY, 1))
-    y_above = lax.ppermute(y_low, "gy", _ring(GY, -1))
-    z_below = lax.ppermute(z_high, "gz", _ring(GZ, 1))
-    z_above = lax.ppermute(z_low, "gz", _ring(GZ, -1))
-
-    partial, carrier = _call(
-        local_kernel, (fields(4), field), [SMEM, SMEM] + [VMEM] * 5, "local", 1_000_000_000, 4 * MIB, 32
-    )(metric, strain, state, z_below, z_above, circulant, _exact(along_y[:, :CELLS]))
-
-    provisional, heat, sent = _call(
+    def sides(count):
+        y_side = jax.ShapeDtypeStruct((count, 96, NX), BF16)
+        z_side = jax.ShapeDtypeStruct((count, 24, NX), BF16)
+        return (y_side, y_side, z_side, z_side)
+
+    def exchange(y_low, y_high, z_low, z_high):
+        return (
+            lax.ppermute(y_high, "gy", _ring(GY, 1)),
+            lax.ppermute(y_low, "gy", _ring(GY, -1)),
+            lax.ppermute(z_high, "gz", _ring(GZ, 1)),
+            lax.ppermute(z_low, "gz", _ring(GZ, -1)),
+        )
+
+    beside = exchange(*_call(edges_kernel, sides(4), [VMEM], "edges", 200_000_000, 2 * MIB, 16)(state))
+    partial, carrier_y, carrier_z = _call(
+        local_kernel,
+        (fields(4), field, jax.ShapeDtypeStruct((48, NX), F32)),
+        [SMEM, SMEM, VMEM, VMEM],
+        "local",
+        1_000_000_000,
+        4 * MIB,
+        24,
+    )(metric, strain, state, _exact(local))
+
+    provisional, sent, heat = _call(
         forward_kernel,
-        (fields(3), field, block),
-        [SMEM] + [VMEM] * 8,
+        (fields(3), block, field),
+        [SMEM] + [VMEM] * 12,
         "forward",
         2_000_000_000,
         8 * MIB,
         40,
+        out_specs=(VMEM, VMEM, ANY),
+        scratch_shapes=[pltpu.VMEM((CELLS, NX), F32), pltpu.SemaphoreType.DMA],
     )(
         metric,
         partial,
-        carrier,
-        y_below,
-        y_above,
-        _exact(along_y[:, CELLS : CELLS + 192]),
+        carrier_y,
+        carrier_z,
+        *beside,
+        beside_y,
+        beside_z,
         spread,
-        circulant,
-        _pieces(forward, 2),
+        np.concatenate([circulant, circulant], axis=0),
+        np.concatenate(_pieces(forward, 2), axis=1),
     )
     got = lax.all_to_all(sent, ("gy", "gz"), split_axis=0, concat_axis=0, tiled=True)
     sent = _call(
-        plane_kernel, block, [SMEM, SMEM] + [VMEM] * 7, "plane", 3_600_000_000, 8 * MIB, 48
+        plane_kernel, block, [SMEM, SMEM] + [VMEM] * 7, "plane", 3_600_000_000, 8 * MIB, 40
     )(
         metric,
         wave_x,
         got,
-        _pieces(outer, 2),
-        _pieces(outer.T, 3),
+        np.concatenate(_pieces(outer, 2), axis=1),
+        np.concatenate(_pieces(outer.T, 3), axis=1),
         twist,
-        _pieces(inner, 2),
-        _pieces(inner.T, 3),
+        np.concatenate(_pieces(inner, 2), axis=0),
+        np.concatenate(_pieces(inner.T, 3), axis=0),
         waves,
     )
     got = lax.all_to_all(sent, ("gy", "gz"), split_axis=0, concat_axis=0, tiled=True)
     motion = _call(
         project_kernel, fields(3), [SMEM] + [VMEM] * 5, "project", 2_500_000_000, 8 * MIB, 40
-    )(metric, got, gather, _pieces(inverse, 2), _pieces(slope, 2), provisional)
+    )(
+        metric,
+        got,
+        gather,
+        np.concatenate(_pieces(inverse, 2), axis=0),
+        np.concatenate(_pieces(slope, 2), axis=0),
+        provisional,
+    )
     return motion.reshape(3, BZ, BY, NX), heat.reshape(BZ, BY, NX)
 
 

time: 102 us -> 92.2 us (0.904)
  waiting for transfers between devices: 13.1 us -> 6.59 us
  local copies, waits for them, and re-layouts: 6.74 us -> 5.03 us
  Pallas kernels: 18.9 us -> 17.5 us
    ppermute x4, waiting for transfers between devices: 13.1 us -> 6.59 us  [the longest x1 4.05 us: exchange(): lax.ppermute(z_low, 'gz', _ring(GZ, -1))]
    unnamed x42, local copies, waits for them, and re-layouts: 6.74 us -> 5.03 us
    pallas_call x1, Pallas kernels: 7.45 us -> 5.92 us  [_step(): _call(plane_kernel, block, [SMEM, SMEM] + [VMEM] * 7, 'plane', 3600000000...]
where the time goes in v2:
time: 92.2 us; the launch traced here: 91.9 us
  blocking collectives  50.5 us (55%)
  Pallas kernels  17.5 us (19%)
  starting transfers between devices  11.4 us (12%)
  waiting for transfers between devices  6.59 us (7%)
  local copies, waits for them, and re-layouts  5.03 us (5%)
    all_to_all x2, blocking collectives, _step(): lax.all_to_all(sent, ('gy', 'gz'), split_axis=0, concat_axis=0, tiled=True)  50.5 us
    ppermute x1, starting transfers between devices, exchange(): lax.ppermute(y_low, 'gy', _ring(GY, -1))  6.01 us
    pallas_call x1, Pallas kernels, _step(): _call(plane_kernel, block, [SMEM, SMEM] + [VMEM] * 7, 'plane', 3600000000...  5.92 us
    unnamed x42, local copies, waits for them, and re-layouts  5.03 us
    pallas_call x1, Pallas kernels, _step(): _call(project_kernel, fields(3), [SMEM] + [VMEM] * 5, 'project', 25000000...  4.97 us
    ppermute x1, waiting for transfers between devices, exchange(): lax.ppermute(z_low, 'gz', _ring(GZ, -1))  4.05 us
    pallas_call x1, Pallas kernels, _step(): _call(forward_kernel, (fields(3), block, field), [SMEM] + [VMEM] * 12, 'f...  3.41 us
    ppermute x1, starting transfers between devices, exchange(): lax.ppermute(z_high, 'gz', _ring(GZ, 1))  3.29 us
  transfers between devices with their start and end apart: 4, of which 2 were waited for; matrix products, arithmetic and copies ran while one was open for 0% of the time, Pallas kernels for 3%

profile of v2, /device:TPU:1, one launch (start us, length us, event | category | flops | bytes accessed | tf_op | source)
XLA Modules:
  0.0 91.9 jit_solution(6099200481067669650)
XLA Ops:
  0.6 0.0 copy-start
  0.6 1.2 %copy-done = bf16[4,32,8,512]{3,2,1,0:T(8,128)(2,1)S(1)} copy-done((bf16[4,32,8,512]{3,2,1,0:T(8,128)(2,1)S(1)}, bf16[4,32,8,512]{3,2,1,0:T(8,128)(2,1)}, u32[]{:S(2)}) %copy-start) | copy-done | bytes 1048600
  1.9 0.0 copy-start.10
  1.9 0.4 edges.1
  2.3 0.0 copy-start.4
  2.3 2.1 %collective-permute-start = (bf16[4,96,512]{2,1,0:T(8,128)(2,1)S(1)}, bf16[4,96,512]{2,1,0:T(8,128)(2,1)S(1)}, u32[]{:S(2)}, u32[]{:S(2)}) collective-permute-start(bf16[4,96,512]{2,1,0:T(8,128)(2,1)S(1)} %get-tuple-element.15), channel_id=1, source_target_pairs={{0,4},{4,8},{8,12},{12,16},{16,20},{20,24},{24,28},{28,32},{32,36}... | collective-permute-start | bytes 1179656 | tf_op jit(solution)/shard_map/ppermute | solution.py:399
  4.4 6.0 %collective-permute-start.1 = (bf16[4,96,512]{2,1,0:T(8,128)(2,1)S(1)}, bf16[4,96,512]{2,1,0:T(8,128)(2,1)S(1)}, u32[]{:S(2)}, u32[]{:S(2)}) collective-permute-start(bf16[4,96,512]{2,1,0:T(8,128)(2,1)S(1)} %get-tuple-element.16), channel_id=1, source_target_pairs={{0,124},{4,0},{8,4},{12,8},{16,12},{20,16},{24,20},{28,24},{32,28}... | collective-permute-start | bytes 1179656 | tf_op jit(solution)/shard_map/ppermute | solution.py:400
  10.4 3.3 %collective-permute-start.2 = (bf16[4,24,512]{2,1,0:T(8,128)(2,1)S(1)}, bf16[4,24,512]{2,1,0:T(8,128)(2,1)S(1)}, u32[]{:S(2)}, u32[]{:S(2)}) collective-permute-start(bf16[4,24,512]{2,1,0:T(8,128)(2,1)S(1)} %get-tuple-element.17), channel_id=1, source_target_pairs={{0,1},{1,2},{2,3},{3,0},{4,5},{5,6},{6,7},{7,4},{8,9},{9,10},{10,1... | collective-permute-start | bytes 294920 | tf_op jit(solution)/shard_map/ppermute | solution.py:401
  13.7 0.0 collective-permute-start.3
  13.7 0.0 copy-start.1
  13.7 1.2 %copy-done.1 = bf16[4,32,8,512]{3,2,1,0:T(8,128)(2,1)S(1)} copy-done((bf16[4,32,8,512]{3,2,1,0:T(8,128)(2,1)S(1)}, bf16[4,32,8,512]{3,2,1,0:T(8,128)(2,1)}, u32[]{:S(2)}) %copy-start.1) | copy-done | bytes 1048600
  14.9 0.0 copy-start.2
  14.9 0.7 copy-done.2
  15.6 0.0 copy-start.3
  15.6 0.7 copy-done.3
  16.3 0.0 copy-start.13
  16.3 1.1 %copy-done.13 = bf16[768,512]{1,0:T(8,128)(2,1)S(1)} copy-done((bf16[768,512]{1,0:T(8,128)(2,1)S(1)}, bf16[768,512]{1,0:T(8,128)(2,1)}, u32[]{:S(2)}) %copy-start.13) | copy-done | bytes 786456
  17.4 0.0 copy-start.11
  17.4 0.0 copy-start.12
  17.4 0.0 copy-start.18
  17.4 0.0 copy-start.19
  17.4 2.7 %local.1 = (f32[4,256,512]{2,1,0:T(8,128)S(1)}, f32[256,512]{1,0:T(8,128)S(1)}, f32[48,512]{1,0:T(8,128)S(1)}) custom-call(f32[3,3]{1,0:T(4,128)S(1)} %copy-done.3, f32[3,3]{1,0:T(4,128)S(1)} %copy-done.2, bf16[4,256,512]{2,1,0:T(8,128)(2,1)S(1)} %bitcast.4, bf16[768,512]{1,0:T(8,128)(2,1)S(1)} %copy-done.13), custom_call_target="tpu_custom_call" | custom-call | flops 1000000000 | bytes 4194304 | tf_op jit(solution)/shard_map/local/pallas_call | solution.py:406
  20.2 2.5 %collective-permute-done.2.z_below = bf16[4,24,512]{2,1,0:T(8,128)(2,1)S(1)} collective-permute-done((bf16[4,24,512]{2,1,0:T(8,128)(2,1)S(1)}, bf16[4,24,512]{2,1,0:T(8,128)(2,1)S(1)}, u32[]{:S(2)}, u32[]{:S(2)}) %collective-permute-start.2) | collective-permute-done | bytes 98336 | tf_op jit(solution)/shard_map/ppermute | solution.py:401
  22.7 4.0 %collective-permute-done.3.z_above = bf16[4,24,512]{2,1,0:T(8,128)(2,1)S(1)} collective-permute-done((bf16[4,24,512]{2,1,0:T(8,128)(2,1)S(1)}, bf16[4,24,512]{2,1,0:T(8,128)(2,1)S(1)}, u32[]{:S(2)}, u32[]{:S(2)}) %collective-permute-start.3) | collective-permute-done | bytes 98336 | tf_op jit(solution)/shard_map/ppermute | solution.py:402
  26.8 0.0 collective-permute-done.y_below
  26.8 0.0 collective-permute-done.1.y_above
  26.8 0.0 copy-done.10
  26.8 0.0 copy-done.4
  26.8 0.0 copy-done.11
  26.8 0.0 copy-done.12
  26.8 0.0 copy-done.18
  26.8 0.0 copy-done.19
  26.8 0.0 copy-start.5
  26.8 0.0 copy-start.14
  26.8 0.0 copy-start.15
  26.9 0.0 copy-start.16
  26.9 0.0 copy-start.17
  26.9 3.4 %forward.1 = (f32[3,256,512]{2,1,0:T(8,128)S(1)}, f32[128,16,128]{2,1,0:T(8,128)S(1)}, f32[256,512]{1,0:T(8,128)}) custom-call(f32[3,3]{1,0:T(4,128)S(1)} %copy-done.4, f32[4,256,512]{2,1,0:T(8,128)S(1)} %get-tuple-element.12.partial, f32[256,512]{1,0:T(8,128)S(1)} %get-tuple-element.13.carrier_y, f32[48,512]{1,0:T(8,128)S(1)} %get-tuple-element.14.carrier_z, ...), custom_call_target="tpu_custom_call" | custom-call | flops 2000000000 | bytes 8388608 | tf_op jit(solution)/shard_map/forward/pallas_call | solution.py:416
  30.3 0.0 copy-start.7
  30.3 0.0 copy-start.20
  30.3 27.3 %all_to_all.10.got = f32[128,16,128]{2,1,0:T(8,128)S(1)} all-to-all(f32[128,16,128]{2,1,0:T(8,128)S(1)} %get-tuple-element.19), channel_id=1, replica_groups=mesh['gy'=32,'gz'=4] {'gy','gz'}, dimensions={0} | all-to-all | bytes 2097152 | tf_op jit(solution)/shard_map/all_to_all | solution.py:438
  57.6 0.0 copy-done.5
  57.6 0.0 copy-done.14
  57.6 0.0 copy-done.15
  57.7 0.0 copy-done.16
  57.7 0.0 copy-done.17
  57.7 0.0 copy-done.7
  57.7 0.0 copy-done.20
  57.7 0.0 copy-start.6
  57.7 5.9 %plane.1 = f32[128,16,128]{2,1,0:T(8,128)S(1)} custom-call(f32[3,3]{1,0:T(4,128)S(1)} %copy-done.4, f32[256]{0:T(256)S(1)} %copy-done.20, f32[128,16,128]{2,1,0:T(8,128)S(1)} %all_to_all.10.got, bf16[256,512]{1,0:T(8,128)(2,1)S(1)} %copy-done.17, bf16[256,768]{1,0:T(8,128)(2,1)S(1)} %copy-done.16, f32[2,128,512]{2,1,0:T(8,128)S(1)} %copy-done.14, ...), custom_call_target="tpu_custom_call" | custom-call | flops 3600000000 | bytes 8388608 | tf_op jit(solution)/shard_map/plane/pallas_call | solution.py:439
  63.6 0.0 copy-start.8
  63.6 0.0 copy-start.9
  63.7 23.2 %all_to_all.11.got = f32[128,16,128]{2,1,0:T(8,128)S(1)} all-to-all(f32[128,16,128]{2,1,0:T(8,128)S(1)} %plane.1), channel_id=1, replica_groups=mesh['gy'=32,'gz'=4] {'gy','gz'}, dimensions={0} | all-to-all | bytes 2097152 | tf_op jit(solution)/shard_map/all_to_all | solution.py:452
  86.9 0.0 copy-done.6
  86.9 0.0 copy-done.8
  86.9 0.0 copy-done.9
  86.9 5.0 %project.1 = f32[3,256,512]{2,1,0:T(8,128)} custom-call(f32[3,3]{1,0:T(4,128)S(1)} %copy-done.4, f32[128,16,128]{2,1,0:T(8,128)S(1)} %all_to_all.11.got, bf16[768,1536]{1,0:T(8,128)(2,1)S(1)} %copy-done.6, bf16[1024,512]{1,0:T(8,128)(2,1)S(1)} %copy-done.9, bf16[1024,512]{1,0:T(8,128)(2,1)S(1)} %copy-done.8, f32[3,256,512]{2,1,0:T(8,128)S(1)} %get-tuple-element.20.provisional), custom_call_target="tpu_custom_call" | custom-call | flops 2500000000 | bytes 8388608 | tf_op jit(solution)/shard_map/project/pallas_call | solution.py:453
Async XLA Ops:
  0.6 1.2 %copy-start = (bf16[4,32,8,512]{3,2,1,0:T(8,128)(2,1)S(1)}, bf16[4,32,8,512]{3,2,1,0:T(8,128)(2,1)}, u32[]{:S(2)}) copy-start(bf16[4,32,8,512]{3,2,1,0:T(8,128)(2,1)} %param.19) | copy-start | bytes 3145732
  1.9 24.9 %copy-start.10 = (bf16[512,1024]{1,0:T(8,128)(2,1)S(1)}, bf16[512,1024]{1,0:T(8,128)(2,1)}, u32[]{:S(2)}) copy-start(bf16[512,1024]{1,0:T(8,128)(2,1)} %constant.37.clone.waves) | copy-start | bytes 3145732
  2.3 24.5 %copy-start.4 = (f32[3,3]{1,0:T(4,128)S(1)}, f32[3,3]{1,0:T(4,128)}, u32[]{:S(2)}) copy-start(f32[3,3]{1,0:T(4,128)} %metric.7) | copy-start | bytes 112
  2.3 24.5 %collective-permute-start = (bf16[4,96,512]{2,1,0:T(8,128)(2,1)S(1)}, bf16[4,96,512]{2,1,0:T(8,128)(2,1)S(1)}, u32[]{:S(2)}, u32[]{:S(2)}) collective-permute-start(bf16[4,96,512]{2,1,0:T(8,128)(2,1)S(1)} %get-tuple-element.15), channel_id=1, source_target_pairs={{0,4},{4,8},{8,12},{12,16},{16,20},{20,24},{24,28},{28,32},{32,36}... | collective-permute-start | bytes 1179656 | tf_op jit(solution)/shard_map/ppermute | solution.py:399
  4.4 22.4 %collective-permute-start.1 = (bf16[4,96,512]{2,1,0:T(8,128)(2,1)S(1)}, bf16[4,96,512]{2,1,0:T(8,128)(2,1)S(1)}, u32[]{:S(2)}, u32[]{:S(2)}) collective-permute-start(bf16[4,96,512]{2,1,0:T(8,128)(2,1)S(1)} %get-tuple-element.16), channel_id=1, source_target_pairs={{0,124},{4,0},{8,4},{12,8},{16,12},{20,16},{24,20},{28,24},{32,28}... | collective-permute-start | bytes 1179656 | tf_op jit(solution)/shard_map/ppermute | solution.py:400
  10.4 12.3 %collective-permute-start.2 = (bf16[4,24,512]{2,1,0:T(8,128)(2,1)S(1)}, bf16[4,24,512]{2,1,0:T(8,128)(2,1)S(1)}, u32[]{:S(2)}, u32[]{:S(2)}) collective-permute-start(bf16[4,24,512]{2,1,0:T(8,128)(2,1)S(1)} %get-tuple-element.17), channel_id=1, source_target_pairs={{0,1},{1,2},{2,3},{3,0},{4,5},{5,6},{6,7},{7,4},{8,9},{9,10},{10,1... | collective-permute-start | bytes 294920 | tf_op jit(solution)/shard_map/ppermute | solution.py:401
  13.7 13.1 %collective-permute-start.3 = (bf16[4,24,512]{2,1,0:T(8,128)(2,1)S(1)}, bf16[4,24,512]{2,1,0:T(8,128)(2,1)S(1)}, u32[]{:S(2)}, u32[]{:S(2)}) collective-permute-start(bf16[4,24,512]{2,1,0:T(8,128)(2,1)S(1)} %get-tuple-element.18), channel_id=1, source_target_pairs={{0,3},{1,0},{2,1},{3,2},{4,7},{5,4},{6,5},{7,6},{8,11},{9,8},{10,9... | collective-permute-start | bytes 294920 | tf_op jit(solution)/shard_map/ppermute | solution.py:402
  13.7 1.2 %copy-start.1 = (bf16[4,32,8,512]{3,2,1,0:T(8,128)(2,1)S(1)}, bf16[4,32,8,512]{3,2,1,0:T(8,128)(2,1)}, u32[]{:S(2)}) copy-start(bf16[4,32,8,512]{3,2,1,0:T(8,128)(2,1)} %param.19) | copy-start | bytes 3145732
  14.9 0.7 copy-start.2
  15.6 0.7 copy-start.3
  16.3 1.1 %copy-start.13 = (bf16[768,512]{1,0:T(8,128)(2,1)S(1)}, bf16[768,512]{1,0:T(8,128)(2,1)}, u32[]{:S(2)}) copy-start(bf16[768,512]{1,0:T(8,128)(2,1)} %constant.32.clone.along) | copy-start | bytes 2359300
  17.4 9.4 %copy-start.11 = (bf16[1024,512]{1,0:T(8,128)(2,1)S(1)}, bf16[1024,512]{1,0:T(8,128)(2,1)}, u32[]{:S(2)}) copy-start(bf16[1024,512]{1,0:T(8,128)(2,1)} %constant.36.clone.along_x) | copy-start | bytes 3145732
  17.4 9.4 %copy-start.12 = (bf16[512,1024]{1,0:T(8,128)(2,1)S(1)}, bf16[512,1024]{1,0:T(8,128)(2,1)}, u32[]{:S(2)}) copy-start(bf16[512,1024]{1,0:T(8,128)(2,1)} %constant.35.clone.spread) | copy-start | bytes 3145732
  17.4 9.4 %copy-start.18 = (bf16[256,192]{1,0:T(8,128)(2,1)S(1)}, bf16[256,192]{1,0:T(8,128)(2,1)}, u32[]{:S(2)}) copy-start(bf16[256,192]{1,0:T(8,128)(2,1)} %constant.33.clone.along_y) | copy-start | bytes 294916
  17.4 9.4 %copy-start.19 = (bf16[2,24,24]{2,1,0:T(8,128)(2,1)S(1)}, bf16[2,24,24]{2,1,0:T(8,128)(2,1)}, u32[]{:S(2)}) copy-start(bf16[2,24,24]{2,1,0:T(8,128)(2,1)} %constant.34.clone.along_z) | copy-start | bytes 6916
  26.8 30.8 %copy-start.5 = (bf16[1536,1024]{1,0:T(8,128)(2,1)S(1)}, bf16[1536,1024]{1,0:T(8,128)(2,1)}, u32[]{:S(2)}) copy-start(bf16[1536,1024]{1,0:T(8,128)(2,1)} %constant.43.clone.inner_back) | copy-start | bytes 9437188
  26.8 30.8 %copy-start.14 = (f32[2,128,512]{2,1,0:T(8,128)S(1)}, f32[2,128,512]{2,1,0:T(8,128)}, u32[]{:S(2)}) copy-start(f32[2,128,512]{2,1,0:T(8,128)} %constant.41.clone.twist) | copy-start | bytes 1572868
  26.8 30.8 %copy-start.15 = (f32[3,128,256]{2,1,0:T(8,128)S(1)}, f32[3,128,256]{2,1,0:T(8,128)}, u32[]{:S(2)}) copy-start(f32[3,128,256]{2,1,0:T(8,128)} %constant.44.clone.waves) | copy-start | bytes 1179652
  26.9 30.8 %copy-start.16 = (bf16[256,768]{1,0:T(8,128)(2,1)S(1)}, bf16[256,768]{1,0:T(8,128)(2,1)}, u32[]{:S(2)}) copy-start(bf16[256,768]{1,0:T(8,128)(2,1)} %constant.40.clone.outer_back) | copy-start | bytes 1179652
  26.9 30.8 %copy-start.17 = (bf16[256,512]{1,0:T(8,128)(2,1)S(1)}, bf16[256,512]{1,0:T(8,128)(2,1)}, u32[]{:S(2)}) copy-start(bf16[256,512]{1,0:T(8,128)(2,1)} %constant.39.clone.outer) | copy-start | bytes 786436
  30.3 27.4 %copy-start.7 = (bf16[2048,512]{1,0:T(8,128)(2,1)S(1)}, bf16[2048,512]{1,0:T(8,128)(2,1)}, u32[]{:S(2)}) copy-start(bf16[2048,512]{1,0:T(8,128)(2,1)} %constant.42.clone.inner) | copy-start | bytes 6291460
  30.3 27.4 %copy-start.20 = (f32[256]{0:T(256)S(1)}, f32[256]{0:T(256)}, u32[]{:S(2)}) copy-start(f32[256]{0:T(256)} %constant.38.clone.wave_x) | copy-start | bytes 3076
  57.7 29.2 %copy-start.6 = (bf16[768,1536]{1,0:T(8,128)(2,1)S(1)}, bf16[768,1536]{1,0:T(8,128)(2,1)}, u32[]{:S(2)}) copy-start(bf16[768,1536]{1,0:T(8,128)(2,1)} %constant.45.clone.gather) | copy-start | bytes 7077892
  63.6 23.2 %copy-start.8 = (bf16[1024,512]{1,0:T(8,128)(2,1)S(1)}, bf16[1024,512]{1,0:T(8,128)(2,1)}, u32[]{:S(2)}) copy-start(bf16[1024,512]{1,0:T(8,128)(2,1)} %constant.47.clone.slope) | copy-start | bytes 3145732
  63.6 23.2 %copy-start.9 = (bf16[1024,512]{1,0:T(8,128)(2,1)S(1)}, bf16[1024,512]{1,0:T(8,128)(2,1)}, u32[]{:S(2)}) copy-start(bf16[1024,512]{1,0:T(8,128)(2,1)} %constant.46.clone.inverse) | copy-start | bytes 3145732

commit v3 on v2

--- a/solution.py
+++ b/solution.py
@@ -173,29 +173,30 @@
     )
 
 
-def _picked(state):
+def _odd(axis):
+    return lax.rem(lax.axis_index(axis), 2)
+
+
+def edges_kernel(state, y_first, y_second, z_first, z_second):
+    odd_y, odd_z = _odd("gy"), _odd("gz")
     row = lax.broadcasted_iota(jnp.int32, (240, CELLS), 0)
     column = lax.broadcasted_iota(jnp.int32, (240, CELLS), 1)
-    high = row >= 96
-    within = jnp.where(high, row - 96, row)
+    second = row >= 96
+    within = jnp.where(second, row - 96, row)
     third = (within * 171) >> 9
-    along_y = BY * third + (within - 3 * third) + jnp.where(high, BY - 3, 0)
-    along_z = jnp.where(row >= 216, row - 216 + CELLS - 24, row - 192)
+    top_y = (BY - 3) * jnp.where(second, odd_y, 1 - odd_y)
+    along_y = BY * third + (within - 3 * third) + top_y
+    second = row >= 216
+    top_z = (CELLS - 24) * jnp.where(second, odd_z, 1 - odd_z)
+    along_z = jnp.where(second, row - 216, row - 192) + top_z
     source = jnp.where(row >= 192, along_z, along_y)
     pick = jnp.where(column == source, 1.0, 0.0).astype(BF16)
-    return [_dot(pick, value) for value in state]
-
-
-def _store_sides(q, rows, y_low, y_high, z_low, z_high):
-    y_low[q] = rows[0:96].astype(BF16)
-    y_high[q] = rows[96:192].astype(BF16)
-    z_low[q] = rows[192:216].astype(BF16)
-    z_high[q] = rows[216:240].astype(BF16)
-
-
-def edges_kernel(state, *sides):
-    for q, rows in enumerate(_picked([state[q] for q in range(4)])):
-        _store_sides(q, rows, *sides)
+    for q in range(4):
+        rows = _dot(pick, state[q])
+        y_first[q] = rows[0:96].astype(BF16)
+        y_second[q] = rows[96:192].astype(BF16)
+        z_first[q] = rows[192:216].astype(BF16)
+        z_second[q] = rows[216:240].astype(BF16)
 
 
 def local_kernel(
@@ -233,11 +234,15 @@
         partial[q] = speeds[q] + scale * carried - STEP * rest
 
 
-def _complete(q, partial, carrier_y, carrier_z, y_below, y_above, z_below, z_above, along_y, along_z):
-    beside = jnp.concatenate([y_below[q], y_above[q]], axis=0)
-    whole = partial + carrier_y[...] * _dot(along_y[...], beside)
-    low = whole[:24] + carrier_z[0:24] * _dot(along_z[0], z_below[q])
-    high = whole[CELLS - 24 :] + carrier_z[24:48] * _dot(along_z[1], z_above[q])
+def _complete(q, partial, carrier_y, carrier_z, y_first, y_second, z_first, z_second, along_y, along_z):
+    odd_y, odd_z = _odd("gy"), _odd("gz")
+    beside = jnp.concatenate([y_first[q], y_second[q]], axis=0)
+    whole = partial + carrier_y[...] * _dot(along_y[odd_y], beside)
+    first, second = _dot(along_z[odd_z], z_first[q]), _dot(along_z[1 - odd_z], z_second[q])
+    below = jnp.where(odd_z == 1, first, second)
+    above = jnp.where(odd_z == 1, second, first)
+    low = whole[:24] + carrier_z[0:24] * below
+    high = whole[CELLS - 24 :] + carrier_z[24:48] * above
     return jnp.concatenate([low, whole[24 : CELLS - 24], high], axis=0)
 
 
@@ -246,10 +251,10 @@
     partial,
     carrier_y,
     carrier_z,
-    y_below,
-    y_above,
-    z_below,
-    z_above,
+    y_first,
+    y_second,
+    z_first,
+    z_second,
     along_y,
     along_z,
     spread,
@@ -263,7 +268,7 @@
 ):
     fields = [
         _complete(
-            q, partial[q], carrier_y, carrier_z, y_below, y_above, z_below, z_above, along_y, along_z
+            q, partial[q], carrier_y, carrier_z, y_first, y_second, z_first, z_second, along_y, along_z
         )
         for q in range(4)
     ]
@@ -329,13 +334,20 @@
         factor = jnp.where(out, 0.0, -1.0 / (jnp.where(out, 1.0, symbol) * float(NX * NY * NZ)))
         block = modes[c * DEV : (c + 1) * DEV]
         solved.append(block * jnp.concatenate([factor, factor], axis=1))
-    cells = _by_table(_split(jnp.concatenate(solved, axis=0), 3), inner_back, 2 * CELLS)
+    high, low = _split(jnp.concatenate(solved, axis=0), 2)
+    cells = _dot(jnp.concatenate([low] * 2, axis=1), inner_back[: 4 * CELLS]) + _dot(
+        jnp.concatenate([high] * 3, axis=1), inner_back[...]
+    )
     columns = []
     for c in range(2):
         re = cells[c * DEV : (c + 1) * DEV, :EXT]
         im = cells[c * DEV : (c + 1) * DEV, EXT:]
         columns.append(jnp.concatenate([re * tr + im * ti, im * tr - re * ti], axis=0))
-    block = _table_by(outer_back, _split(jnp.concatenate(columns, axis=1), 3), 2 * DEV)
+    high, middle, low = _split(jnp.concatenate(columns, axis=1), 3)
+    block = _dot(outer_back[:, : 2 * DEV], low) + _dot(
+        outer_back[...], jnp.concatenate([middle] * 2, axis=0)
+    )
+    block = block + _dot(outer_back[...], jnp.concatenate([high] * 2, axis=0))
     for c in range(2):
         for part in range(2):
             for t in range(EXT // 128):
@@ -343,25 +355,39 @@
                 sent[:, 4 * t + 2 * c + part, :] = block[part * DEV : (part + 1) * DEV, at : at + 128]
 
 
-def project_kernel(metric, got, gather, inverse, slope, provisional, motion):
+def project_kernel(metric, got, gather, inverse, slope, provisional, motion, held, done):
     rows = [
         jnp.concatenate([got[:, 4 * t + r, :] for t in range(EXT // 128)], axis=1)
         for r in range(4)
     ]
     pieces = jnp.concatenate(_split(jnp.concatenate(rows, axis=0), 3), axis=1)
     fields = _dot_nt(gather[...], pieces)
-    pushes = []
-    for j, table in enumerate((slope, inverse, inverse)):
-        left = _split(fields[j * CELLS : (j + 1) * CELLS], 2)
-        pushes.append(_by_table(left, table, NX))
-    for i in range(3):
-        motion[i] = provisional[i] - (
-            metric[i, 0] * pushes[0] + metric[i, 1] * pushes[1] + metric[i, 2] * pushes[2]
-        )
-
-
-def _ring(count, shift):
-    return [(i, (i + shift) % count) for i in range(count)]
+    fields = [_split(fields[j * CELLS : (j + 1) * CELLS], 2) for j in range(3)]
+    half = NX // 2
+    copies = []
+    for h in range(2):
+        at = pl.ds(h * half, half)
+        pushes = [
+            _by_table(left, table[:, at], NX)
+            for left, table in zip(fields, (slope, inverse, inverse))
+        ]
+        for i in range(3):
+            held[i, :, at] = provisional[i, :, at] - (
+                metric[i, 0] * pushes[0] + metric[i, 1] * pushes[1] + metric[i, 2] * pushes[2]
+            )
+            copy = pltpu.make_async_copy(
+                held.at[i, :, at], motion.at[i, :, at], done.at[3 * h + i]
+            )
+            copy.start()
+            copies.append(copy)
+    for copy in copies:
+        copy.wait()
+
+
+def _swaps(count):
+    first = [(i, i ^ 1) for i in range(count)]
+    second = [(i, (i + 1 if i % 2 else i - 1) % count) for i in range(count)]
+    return first, second
 
 
 def _step(state, metric, strain):
@@ -376,9 +402,12 @@
     spread = np.concatenate([spread, spread], axis=1)
     gather = _exact(np.concatenate([np.eye(CELLS, EXT), along_y, along_z], axis=0))
     gather = np.concatenate([gather] * 3, axis=1)
-    beside_y = _exact(along_y[:, CELLS : CELLS + 192])
+    below, above = along_y[:, CELLS : CELLS + 96], along_y[:, CELLS + 96 : CELLS + 192]
+    beside_y = _exact(
+        np.stack([np.concatenate([above, below], axis=1), np.concatenate([below, above], axis=1)])
+    )
     beside_z = _exact(
-        np.stack([along_z[:24, CELLS + 192 : CELLS + 216], along_z[CELLS - 24 :, CELLS + 216 : CELLS + 240]])
+        np.stack([along_z[CELLS - 24 :, CELLS + 216 : CELLS + 240], along_z[:24, CELLS + 192 : CELLS + 216]])
     )
     local = np.zeros((NX + CELLS, NX))
     local[:NX] = _circulant_x()
@@ -394,12 +423,13 @@
         z_side = jax.ShapeDtypeStruct((count, 24, NX), BF16)
         return (y_side, y_side, z_side, z_side)
 
-    def exchange(y_low, y_high, z_low, z_high):
+    def exchange(y_first, y_second, z_first, z_second):
+        swaps_y, swaps_z = _swaps(GY), _swaps(GZ)
         return (
-            lax.ppermute(y_high, "gy", _ring(GY, 1)),
-            lax.ppermute(y_low, "gy", _ring(GY, -1)),
-            lax.ppermute(z_high, "gz", _ring(GZ, 1)),
-            lax.ppermute(z_low, "gz", _ring(GZ, -1)),
+            lax.ppermute(y_first, "gy", swaps_y[0]),
+            lax.ppermute(y_second, "gy", swaps_y[1]),
+            lax.ppermute(z_first, "gz", swaps_z[0]),
+            lax.ppermute(z_second, "gz", swaps_z[1]),
         )
 
     beside = exchange(*_call(edges_kernel, sides(4), [VMEM], "edges", 200_000_000, 2 * MIB, 16)(state))
@@ -443,7 +473,7 @@
         wave_x,
         got,
         np.concatenate(_pieces(outer, 2), axis=1),
-        np.concatenate(_pieces(outer.T, 3), axis=1),
+        np.concatenate(_pieces(outer.T, 2), axis=1),
         twist,
         np.concatenate(_pieces(inner, 2), axis=0),
         np.concatenate(_pieces(inner.T, 3), axis=0),
@@ -451,7 +481,15 @@
     )
     got = lax.all_to_all(sent, ("gy", "gz"), split_axis=0, concat_axis=0, tiled=True)
     motion = _call(
-        project_kernel, fields(3), [SMEM] + [VMEM] * 5, "project", 2_500_000_000, 8 * MIB, 40
+        project_kernel,
+        fields(3),
+        [SMEM] + [VMEM] * 5,
+        "project",
+        2_500_000_000,
+        8 * MIB,
+        40,
+        out_specs=ANY,
+        scratch_shapes=[pltpu.VMEM((3, CELLS, NX), F32), pltpu.SemaphoreType.DMA((6,))],
     )(
         metric,
         got,

time: 92.2 us -> 91.1 us (0.988)
  blocking collectives: 50.5 us -> 49.1 us
    all_to_all x2, blocking collectives: 50.5 us -> 49.1 us  [_step(): lax.all_to_all(sent, ('gy', 'gz'), split_axis=0, concat_axis=0, tiled=True)]
where the time goes in v3:
time: 91.1 us; the launch traced here: 90.8 us
  blocking collectives  49.1 us (54%)
  Pallas kernels  16.9 us (19%)
  starting transfers between devices  12.2 us (13%)
  waiting for transfers between devices  6.59 us (7%)
  local copies, waits for them, and re-layouts  5.03 us (6%)
  between operations  1 us (1%)
    all_to_all x2, blocking collectives, _step(): lax.all_to_all(sent, ('gy', 'gz'), split_axis=0, concat_axis=0, tiled=True)  49.1 us
    ppermute x1, starting transfers between devices, exchange(): lax.ppermute(y_second, 'gy', swaps_y[1])  6.18 us
    ppermute x1, waiting for transfers between devices, exchange(): lax.ppermute(z_second, 'gz', swaps_z[1])  6.12 us
    pallas_call x1, Pallas kernels, _step(): _call(plane_kernel, block, [SMEM, SMEM] + [VMEM] * 7, 'plane', 3600000000...  5.57 us
    unnamed x42, local copies, waits for them, and re-layouts  5.03 us
    pallas_call x1, Pallas kernels, _step(): _call(project_kernel, fields(3), [SMEM] + [VMEM] * 5, 'project', 25000000...  4.73 us
    pallas_call x1, Pallas kernels, _step(): _call(forward_kernel, (fields(3), block, field), [SMEM] + [VMEM] * 12, 'f...  3.42 us
    pallas_call x1, Pallas kernels, _step(): _call(local_kernel, (fields(4), field, jax.ShapeDtypeStruct((48, NX), F32...  2.73 us
  transfers between devices with their start and end apart: 4, of which 2 were waited for; matrix products, arithmetic and copies ran while one was open for 0% of the time, Pallas kernels for 3%

profile of v3, /device:TPU:1, one launch (start us, length us, event | category | flops | bytes accessed | tf_op | source)
XLA Modules:
  0.0 90.8 jit_solution(3876111829574490609)
XLA Ops:
  0.6 0.0 copy-start
  0.6 1.2 %copy-done = bf16[4,32,8,512]{3,2,1,0:T(8,128)(2,1)S(1)} copy-done((bf16[4,32,8,512]{3,2,1,0:T(8,128)(2,1)S(1)}, bf16[4,32,8,512]{3,2,1,0:T(8,128)(2,1)}, u32[]{:S(2)}) %copy-start) | copy-done | bytes 1048600
  1.9 0.0 copy-start.10
  1.9 0.4 edges.1
  2.3 0.0 copy-start.4
  2.3 2.1 %collective-permute-start = (bf16[4,96,512]{2,1,0:T(8,128)(2,1)S(1)}, bf16[4,96,512]{2,1,0:T(8,128)(2,1)S(1)}, u32[]{:S(2)}, u32[]{:S(2)}) collective-permute-start(bf16[4,96,512]{2,1,0:T(8,128)(2,1)S(1)} %get-tuple-element.15), channel_id=1, source_target_pairs={{0,4},{4,0},{8,12},{12,8},{16,20},{20,16},{24,28},{28,24},{32,36},... | collective-permute-start | bytes 1179656 | tf_op jit(solution)/shard_map/ppermute | solution.py:429
  4.4 6.2 %collective-permute-start.1 = (bf16[4,96,512]{2,1,0:T(8,128)(2,1)S(1)}, bf16[4,96,512]{2,1,0:T(8,128)(2,1)S(1)}, u32[]{:S(2)}, u32[]{:S(2)}) collective-permute-start(bf16[4,96,512]{2,1,0:T(8,128)(2,1)S(1)} %get-tuple-element.16), channel_id=1, source_target_pairs={{0,124},{4,8},{8,4},{12,16},{16,12},{20,24},{24,20},{28,32},{32,28... | collective-permute-start | bytes 1179656 | tf_op jit(solution)/shard_map/ppermute | solution.py:430
  10.6 1.2 %collective-permute-start.2 = (bf16[4,24,512]{2,1,0:T(8,128)(2,1)S(1)}, bf16[4,24,512]{2,1,0:T(8,128)(2,1)S(1)}, u32[]{:S(2)}, u32[]{:S(2)}) collective-permute-start(bf16[4,24,512]{2,1,0:T(8,128)(2,1)S(1)} %get-tuple-element.17), channel_id=1, source_target_pairs={{0,1},{1,0},{2,3},{3,2},{4,5},{5,4},{6,7},{7,6},{8,9},{9,8},{10,11... | collective-permute-start | bytes 294920 | tf_op jit(solution)/shard_map/ppermute | solution.py:431
  11.8 2.6 %collective-permute-start.3 = (bf16[4,24,512]{2,1,0:T(8,128)(2,1)S(1)}, bf16[4,24,512]{2,1,0:T(8,128)(2,1)S(1)}, u32[]{:S(2)}, u32[]{:S(2)}) collective-permute-start(bf16[4,24,512]{2,1,0:T(8,128)(2,1)S(1)} %get-tuple-element.18), channel_id=1, source_target_pairs={{0,3},{1,2},{2,1},{3,0},{4,7},{5,6},{6,5},{7,4},{8,11},{9,10},{10,... | collective-permute-start | bytes 294920 | tf_op jit(solution)/shard_map/ppermute | solution.py:432
  14.5 0.0 copy-start.1
  14.5 1.2 %copy-done.1 = bf16[4,32,8,512]{3,2,1,0:T(8,128)(2,1)S(1)} copy-done((bf16[4,32,8,512]{3,2,1,0:T(8,128)(2,1)S(1)}, bf16[4,32,8,512]{3,2,1,0:T(8,128)(2,1)}, u32[]{:S(2)}) %copy-start.1) | copy-done | bytes 1048600
  15.7 0.0 copy-start.2
  15.7 0.7 copy-done.2
  16.4 0.0 copy-start.3
  16.4 0.7 copy-done.3
  17.1 0.0 copy-start.13
  17.1 1.1 %copy-done.13 = bf16[768,512]{1,0:T(8,128)(2,1)S(1)} copy-done((bf16[768,512]{1,0:T(8,128)(2,1)S(1)}, bf16[768,512]{1,0:T(8,128)(2,1)}, u32[]{:S(2)}) %copy-start.13) | copy-done | bytes 786456
  18.2 0.0 copy-start.11
  18.2 0.0 copy-start.12
  18.2 0.0 copy-start.18
  18.2 0.0 copy-start.19
  18.2 2.7 %local.1 = (f32[4,256,512]{2,1,0:T(8,128)S(1)}, f32[256,512]{1,0:T(8,128)S(1)}, f32[48,512]{1,0:T(8,128)S(1)}) custom-call(f32[3,3]{1,0:T(4,128)S(1)} %copy-done.3, f32[3,3]{1,0:T(4,128)S(1)} %copy-done.2, bf16[4,256,512]{2,1,0:T(8,128)(2,1)S(1)} %bitcast.4, bf16[768,512]{1,0:T(8,128)(2,1)S(1)} %copy-done.13), custom_call_target="tpu_custom_call" | custom-call | flops 1000000000 | bytes 4194304 | tf_op jit(solution)/shard_map/local/pallas_call | solution.py:436
  20.9 0.0 collective-permute-done.2.z_first
  20.9 6.1 %collective-permute-done.3.z_second = bf16[4,24,512]{2,1,0:T(8,128)(2,1)S(1)} collective-permute-done((bf16[4,24,512]{2,1,0:T(8,128)(2,1)S(1)}, bf16[4,24,512]{2,1,0:T(8,128)(2,1)S(1)}, u32[]{:S(2)}, u32[]{:S(2)}) %collective-permute-start.3) | collective-permute-done | bytes 98336 | tf_op jit(solution)/shard_map/ppermute | solution.py:432
  27.1 0.0 collective-permute-done.y_first
  27.1 0.5 collective-permute-done.1.y_second
  27.5 0.0 copy-done.10
  27.5 0.0 copy-done.4
  27.5 0.0 copy-done.11
  27.5 0.0 copy-done.12
  27.6 0.0 copy-done.18
  27.6 0.0 copy-done.19
  27.6 0.0 copy-start.5
  27.6 0.0 copy-start.14
  27.6 0.0 copy-start.15
  27.6 0.0 copy-start.16
  27.6 0.0 copy-start.17
  27.6 3.4 %forward.1 = (f32[3,256,512]{2,1,0:T(8,128)S(1)}, f32[128,16,128]{2,1,0:T(8,128)S(1)}, f32[256,512]{1,0:T(8,128)}) custom-call(f32[3,3]{1,0:T(4,128)S(1)} %copy-done.4, f32[4,256,512]{2,1,0:T(8,128)S(1)} %get-tuple-element.12.partial, f32[256,512]{1,0:T(8,128)S(1)} %get-tuple-element.13.carrier_y, f32[48,512]{1,0:T(8,128)S(1)} %get-tuple-element.14.carrier_z, ...), custom_call_target="tpu_custom_call" | custom-call | flops 2000000000 | bytes 8388608 | tf_op jit(solution)/shard_map/forward/pallas_call | solution.py:446
  31.1 0.0 copy-start.7
  31.1 0.0 copy-start.20
  31.1 26.1 %all_to_all.10.got = f32[128,16,128]{2,1,0:T(8,128)S(1)} all-to-all(f32[128,16,128]{2,1,0:T(8,128)S(1)} %get-tuple-element.19), channel_id=1, replica_groups=mesh['gy'=32,'gz'=4] {'gy','gz'}, dimensions={0} | all-to-all | bytes 2097152 | tf_op jit(solution)/shard_map/all_to_all | solution.py:468
  57.2 0.0 copy-done.5
  57.2 0.0 copy-done.14
  57.2 0.0 copy-done.15
  57.2 0.0 copy-done.16
  57.2 0.0 copy-done.17
  57.2 0.0 copy-done.7
  57.3 0.0 copy-done.20
  57.3 0.0 copy-start.6
  57.3 5.6 %plane.1 = f32[128,16,128]{2,1,0:T(8,128)S(1)} custom-call(f32[3,3]{1,0:T(4,128)S(1)} %copy-done.4, f32[256]{0:T(256)S(1)} %copy-done.20, f32[128,16,128]{2,1,0:T(8,128)S(1)} %all_to_all.10.got, bf16[256,512]{1,0:T(8,128)(2,1)S(1)} %copy-done.17, bf16[256,512]{1,0:T(8,128)(2,1)S(1)} %copy-done.16, f32[2,128,512]{2,1,0:T(8,128)S(1)} %copy-done.14, ...), custom_call_target="tpu_custom_call" | custom-call | flops 3600000000 | bytes 8388608 | tf_op jit(solution)/shard_map/plane/pallas_call | solution.py:469
  62.9 0.0 copy-start.8
  62.9 0.0 copy-start.9
  62.9 23.0 %all_to_all.11.got = f32[128,16,128]{2,1,0:T(8,128)S(1)} all-to-all(f32[128,16,128]{2,1,0:T(8,128)S(1)} %plane.1), channel_id=1, replica_groups=mesh['gy'=32,'gz'=4] {'gy','gz'}, dimensions={0} | all-to-all | bytes 2097152 | tf_op jit(solution)/shard_map/all_to_all | solution.py:482
  85.9 0.0 copy-done.6
  85.9 0.0 copy-done.8
  85.9 0.0 copy-done.9
  85.9 4.7 %project.1 = f32[3,256,512]{2,1,0:T(8,128)} custom-call(f32[3,3]{1,0:T(4,128)S(1)} %copy-done.4, f32[128,16,128]{2,1,0:T(8,128)S(1)} %all_to_all.11.got, bf16[768,1536]{1,0:T(8,128)(2,1)S(1)} %copy-done.6, bf16[1024,512]{1,0:T(8,128)(2,1)S(1)} %copy-done.9, bf16[1024,512]{1,0:T(8,128)(2,1)S(1)} %copy-done.8, f32[3,256,512]{2,1,0:T(8,128)S(1)} %get-tuple-element.20.provisional), custom_call_target="tpu_custom_call" | custom-call | flops 2500000000 | bytes 8388608 | tf_op jit(solution)/shard_map/project/pallas_call | solution.py:483
Async XLA Ops:
  0.6 1.2 %copy-start = (bf16[4,32,8,512]{3,2,1,0:T(8,128)(2,1)S(1)}, bf16[4,32,8,512]{3,2,1,0:T(8,128)(2,1)}, u32[]{:S(2)}) copy-start(bf16[4,32,8,512]{3,2,1,0:T(8,128)(2,1)} %param.19) | copy-start | bytes 3145732
  1.9 25.7 %copy-start.10 = (bf16[512,1024]{1,0:T(8,128)(2,1)S(1)}, bf16[512,1024]{1,0:T(8,128)(2,1)}, u32[]{:S(2)}) copy-start(bf16[512,1024]{1,0:T(8,128)(2,1)} %constant.37.clone.waves) | copy-start | bytes 3145732
  2.3 25.3 %copy-start.4 = (f32[3,3]{1,0:T(4,128)S(1)}, f32[3,3]{1,0:T(4,128)}, u32[]{:S(2)}) copy-start(f32[3,3]{1,0:T(4,128)} %metric.7) | copy-start | bytes 112
  2.3 24.8 %collective-permute-start = (bf16[4,96,512]{2,1,0:T(8,128)(2,1)S(1)}, bf16[4,96,512]{2,1,0:T(8,128)(2,1)S(1)}, u32[]{:S(2)}, u32[]{:S(2)}) collective-permute-start(bf16[4,96,512]{2,1,0:T(8,128)(2,1)S(1)} %get-tuple-element.15), channel_id=1, source_target_pairs={{0,4},{4,0},{8,12},{12,8},{16,20},{20,16},{24,28},{28,24},{32,36},... | collective-permute-start | bytes 1179656 | tf_op jit(solution)/shard_map/ppermute | solution.py:429
  4.4 23.1 %collective-permute-start.1 = (bf16[4,96,512]{2,1,0:T(8,128)(2,1)S(1)}, bf16[4,96,512]{2,1,0:T(8,128)(2,1)S(1)}, u32[]{:S(2)}, u32[]{:S(2)}) collective-permute-start(bf16[4,96,512]{2,1,0:T(8,128)(2,1)S(1)} %get-tuple-element.16), channel_id=1, source_target_pairs={{0,124},{4,8},{8,4},{12,16},{16,12},{20,24},{24,20},{28,32},{32,28... | collective-permute-start | bytes 1179656 | tf_op jit(solution)/shard_map/ppermute | solution.py:430
  10.6 10.3 %collective-permute-start.2 = (bf16[4,24,512]{2,1,0:T(8,128)(2,1)S(1)}, bf16[4,24,512]{2,1,0:T(8,128)(2,1)S(1)}, u32[]{:S(2)}, u32[]{:S(2)}) collective-permute-start(bf16[4,24,512]{2,1,0:T(8,128)(2,1)S(1)} %get-tuple-element.17), channel_id=1, source_target_pairs={{0,1},{1,0},{2,3},{3,2},{4,5},{5,4},{6,7},{7,6},{8,9},{9,8},{10,11... | collective-permute-start | bytes 294920 | tf_op jit(solution)/shard_map/ppermute | solution.py:431
  11.8 15.2 %collective-permute-start.3 = (bf16[4,24,512]{2,1,0:T(8,128)(2,1)S(1)}, bf16[4,24,512]{2,1,0:T(8,128)(2,1)S(1)}, u32[]{:S(2)}, u32[]{:S(2)}) collective-permute-start(bf16[4,24,512]{2,1,0:T(8,128)(2,1)S(1)} %get-tuple-element.18), channel_id=1, source_target_pairs={{0,3},{1,2},{2,1},{3,0},{4,7},{5,6},{6,5},{7,4},{8,11},{9,10},{10,... | collective-permute-start | bytes 294920 | tf_op jit(solution)/shard_map/ppermute | solution.py:432
  14.5 1.2 %copy-start.1 = (bf16[4,32,8,512]{3,2,1,0:T(8,128)(2,1)S(1)}, bf16[4,32,8,512]{3,2,1,0:T(8,128)(2,1)}, u32[]{:S(2)}) copy-start(bf16[4,32,8,512]{3,2,1,0:T(8,128)(2,1)} %param.19) | copy-start | bytes 3145732
  15.7 0.7 copy-start.2
  16.4 0.7 copy-start.3
  17.1 1.1 %copy-start.13 = (bf16[768,512]{1,0:T(8,128)(2,1)S(1)}, bf16[768,512]{1,0:T(8,128)(2,1)}, u32[]{:S(2)}) copy-start(bf16[768,512]{1,0:T(8,128)(2,1)} %constant.32.clone.along) | copy-start | bytes 2359300
  18.2 9.4 %copy-start.11 = (bf16[1024,512]{1,0:T(8,128)(2,1)S(1)}, bf16[1024,512]{1,0:T(8,128)(2,1)}, u32[]{:S(2)}) copy-start(bf16[1024,512]{1,0:T(8,128)(2,1)} %constant.36.clone.along_x) | copy-start | bytes 3145732
  18.2 9.4 %copy-start.12 = (bf16[512,1024]{1,0:T(8,128)(2,1)S(1)}, bf16[512,1024]{1,0:T(8,128)(2,1)}, u32[]{:S(2)}) copy-start(bf16[512,1024]{1,0:T(8,128)(2,1)} %constant.35.clone.spread) | copy-start | bytes 3145732
  18.2 9.4 %copy-start.18 = (bf16[2,256,192]{2,1,0:T(8,128)(2,1)S(1)}, bf16[2,256,192]{2,1,0:T(8,128)(2,1)}, u32[]{:S(2)}) copy-start(bf16[2,256,192]{2,1,0:T(8,128)(2,1)} %constant.33.clone.along_y) | copy-start | bytes 589828
  18.2 9.4 %copy-start.19 = (bf16[2,24,24]{2,1,0:T(8,128)(2,1)S(1)}, bf16[2,24,24]{2,1,0:T(8,128)(2,1)}, u32[]{:S(2)}) copy-start(bf16[2,24,24]{2,1,0:T(8,128)(2,1)} %constant.34.clone.along_z) | copy-start | bytes 6916
  27.6 29.6 %copy-start.5 = (bf16[1536,1024]{1,0:T(8,128)(2,1)S(1)}, bf16[1536,1024]{1,0:T(8,128)(2,1)}, u32[]{:S(2)}) copy-start(bf16[1536,1024]{1,0:T(8,128)(2,1)} %constant.43.clone.inner_back) | copy-start | bytes 9437188
  27.6 29.6 %copy-start.14 = (f32[2,128,512]{2,1,0:T(8,128)S(1)}, f32[2,128,512]{2,1,0:T(8,128)}, u32[]{:S(2)}) copy-start(f32[2,128,512]{2,1,0:T(8,128)} %constant.41.clone.twist) | copy-start | bytes 1572868
  27.6 29.6 %copy-start.15 = (f32[3,128,256]{2,1,0:T(8,128)S(1)}, f32[3,128,256]{2,1,0:T(8,128)}, u32[]{:S(2)}) copy-start(f32[3,128,256]{2,1,0:T(8,128)} %constant.44.clone.waves) | copy-start | bytes 1179652
  27.6 29.6 %copy-start.16 = (bf16[256,512]{1,0:T(8,128)(2,1)S(1)}, bf16[256,512]{1,0:T(8,128)(2,1)}, u32[]{:S(2)}) copy-start(bf16[256,512]{1,0:T(8,128)(2,1)} %constant.40.clone.outer_back) | copy-start | bytes 786436
  27.6 29.6 %copy-start.17 = (bf16[256,512]{1,0:T(8,128)(2,1)S(1)}, bf16[256,512]{1,0:T(8,128)(2,1)}, u32[]{:S(2)}) copy-start(bf16[256,512]{1,0:T(8,128)(2,1)} %constant.39.clone.outer) | copy-start | bytes 786436
  31.1 26.2 %copy-start.7 = (bf16[2048,512]{1,0:T(8,128)(2,1)S(1)}, bf16[2048,512]{1,0:T(8,128)(2,1)}, u32[]{:S(2)}) copy-start(bf16[2048,512]{1,0:T(8,128)(2,1)} %constant.42.clone.inner) | copy-start | bytes 6291460
  31.1 26.2 %copy-start.20 = (f32[256]{0:T(256)S(1)}, f32[256]{0:T(256)}, u32[]{:S(2)}) copy-start(f32[256]{0:T(256)} %constant.38.clone.wave_x) | copy-start | bytes 3076
  57.3 28.6 %copy-start.6 = (bf16[768,1536]{1,0:T(8,128)(2,1)S(1)}, bf16[768,1536]{1,0:T(8,128)(2,1)}, u32[]{:S(2)}) copy-start(bf16[768,1536]{1,0:T(8,128)(2,1)} %constant.45.clone.gather) | copy-start | bytes 7077892
  62.9 23.0 %copy-start.8 = (bf16[1024,512]{1,0:T(8,128)(2,1)S(1)}, bf16[1024,512]{1,0:T(8,128)(2,1)}, u32[]{:S(2)}) copy-start(bf16[1024,512]{1,0:T(8,128)(2,1)} %constant.47.clone.slope) | copy-start | bytes 3145732
  62.9 23.0 %copy-start.9 = (bf16[1024,512]{1,0:T(8,128)(2,1)S(1)}, bf16[1024,512]{1,0:T(8,128)(2,1)}, u32[]{:S(2)}) copy-start(bf16[1024,512]{1,0:T(8,128)(2,1)} %constant.46.clone.inverse) | copy-start | bytes 3145732

commit v4 on v3

v4 whole, which is shorter than its diff:
```python
import numpy as np

import jax
import jax.numpy as jnp
import ml_dtypes
from jax import lax
from jax.experimental import pallas as pl
from jax.experimental.pallas import tpu as pltpu
from jax.sharding import PartitionSpec as P

F32 = jnp.float32
BF16 = jnp.bfloat16
NX, NY, NZ = 512, 256, 128
GY, GZ = 32, 4
BY, BZ = NY // GY, NZ // GZ
DEV = GY * GZ
CELLS = BY * BZ
EXT = 512
STEP = 0.4
COEF = {1: 45.0, -1: -45.0, 2: -9.0, -2: 9.0, 3: 1.0, -3: -1.0}
MIB = 1 << 20


def _pieces(table, count):
    rest = np.asarray(table, np.float64)
    out = []
    for _ in range(count):
        piece = rest.astype(np.float32).astype(ml_dtypes.bfloat16)
        out.append(piece)
        rest = rest - piece.astype(np.float64)
    return np.stack(out)


def _ext_cells():
    cells = [(w, y) for w in range(BZ) for y in range(BY)]
    cells += [(w, y) for w in range(BZ) for y in range(-3, 0)]
    cells += [(w, y) for w in range(BZ) for y in range(BY, BY + 3)]
    cells += [(w, y) for w in range(-3, 0) for y in range(BY)]
    cells += [(w, y) for w in range(BZ, BZ + 3) for y in range(BY)]
    return cells


def _difference_matrices():
    place = {cell: i for i, cell in enumerate(_ext_cells())}
    along_y = np.zeros((CELLS, EXT))
    along_z = np.zeros((CELLS, EXT))
    for w in range(BZ):
        for y in range(BY):
            row = place[(w, y)]
            for k, c in COEF.items():
                along_y[row, place[(w, y + k)]] = c
                along_z[row, place[(w + k, y)]] = c
    return along_y, along_z


def _circulant_x():
    table = np.zeros((NX, NX))
    for x in range(NX):
        for k, c in COEF.items():
            table[(x + k) % NX, x] = c
    return table


def _kt(modes, length):
    a = 2.0 * np.pi * modes / length
    return 1.5 * np.sin(a) - 0.3 * np.sin(2 * a) + np.sin(3 * a) / 30.0


def _x_tables():
    k = np.arange(NX // 2)[:, None]
    x = np.arange(NX)[None, :]
    angle = 2.0 * np.pi * ((k * x) % NX) / NX
    alternating = 1.0 - 2.0 * (np.arange(NX) % 2)
    forward = np.zeros((NX // 2, 2, NX))
    forward[:, 0], forward[:, 1] = np.cos(angle), -np.sin(angle)
    forward[0, 0], forward[0, 1] = 1.0, alternating
    inverse = 2.0 * forward
    inverse[0] = forward[0]
    inverse = inverse.reshape(DEV, 2, 2, NX).transpose(1, 2, 0, 3).reshape(2, 2 * DEV, NX)
    symbol = 60.0 * _kt(np.arange(NX // 2), NX)
    symbol[0] = 0.0
    symbol = symbol.reshape(DEV, 2).T.reshape(2, 1, DEV).astype(np.float32)
    inverse = _pieces(inverse / 60.0, 2)
    inverse = np.concatenate(
        [inverse[0, 0], inverse[1, 0], inverse[0, 1], inverse[1, 1], inverse[0, 0], inverse[0, 1]]
    )
    return forward.reshape(NX, NX) / 60.0, inverse, symbol


def _plane_tables():
    a = np.arange(DEV)
    m1, n1 = a // GZ, a % GZ
    gy, gz = a // GZ, a % GZ
    outer = np.exp(
        -2j * np.pi * (np.outer(m1, gy) / GY + np.outer(n1, gz) / GZ)
    )
    cells = np.array(_ext_cells())
    count = len(cells)
    w, y = cells[:, 0], cells[:, 1]
    twist = np.zeros((DEV, EXT), complex)
    twist[:, :count] = np.exp(-2j * np.pi * (np.outer(n1, w) / NZ + np.outer(m1, y) / NY))
    b = np.arange(CELLS)
    n2, m2 = b // BY, b % BY
    inner = np.zeros((EXT, CELLS), complex)
    inner[:count] = np.exp(-2j * np.pi * (np.outer(w, n2) / BZ + np.outer(y, m2) / BY))
    outer_real = np.block([[outer.real, -outer.imag], [outer.imag, outer.real]])
    inner_real = np.block([[inner.real, inner.imag], [-inner.imag, inner.real]])
    chunks = EXT // 128
    inner_back = _pieces(inner_real.T, 3)[[0, 1, 2, 0, 1]].reshape(5, 2 * CELLS, 2, chunks, 128)
    inner_back = inner_back.transpose(0, 1, 3, 2, 4).reshape(10 * CELLS, 1024)
    inner_real = _pieces(inner_real, 2)[[0, 1, 0]].reshape(3, 2, chunks, 128, 2 * CELLS)
    inner_real = inner_real.transpose(2, 0, 1, 3, 4).reshape(chunks * 768, 2 * CELLS)
    mode_y = m1[:, None] + GY * m2[None, :]
    mode_z = n1[:, None] + GZ * n2[None, :]
    edge = (((2 * mode_y) % NY == 0) & ((2 * mode_z) % NZ == 0)).astype(np.float32)
    waves = np.stack([_kt(mode_y, NY), _kt(mode_z, NZ), edge]).astype(np.float32)
    twist = np.stack([twist.real, twist.imag]).astype(np.float32)
    return outer_real, twist, inner_real, inner_back, waves


def _exact(table):
    return np.asarray(table, np.float32).astype(ml_dtypes.bfloat16)


def _dot(left, right):
    return lax.dot_general(left, right, (((1,), (0,)), ((), ())), preferred_element_type=F32)


def _dot_nt(left, right):
    return lax.dot_general(left, right, (((1,), (1,)), ((), ())), preferred_element_type=F32)


def _split(value, count):
    out = []
    for i in range(count):
        piece = value.astype(BF16)
        out.append(piece)
        if i + 1 < count:
            value = value - piece.astype(F32)
    return out


VMEM = pl.BlockSpec(memory_space=pltpu.VMEM)
SMEM = pl.BlockSpec(memory_space=pltpu.SMEM)
ANY = pl.BlockSpec(memory_space=pl.ANY)


def _call(kernel, out_shape, in_specs, name, flops, nbytes, vmem, scratch_shapes=(), out_specs=None):
    return pl.pallas_call(
        kernel,
        out_shape=out_shape,
        in_specs=in_specs,
        out_specs=out_specs or jax.tree.map(lambda _: VMEM, out_shape),
        scratch_shapes=scratch_shapes,
        compiler_params=pltpu.CompilerParams(vmem_limit_bytes=vmem * MIB),
        cost_estimate=pl.CostEstimate(flops=flops, bytes_accessed=nbytes, transcendentals=0),
        name=name,
    )


def _odd(axis):
    return lax.rem(lax.axis_index(axis), 2)


def edges_kernel(state, y_first, y_second, y_first_heat, y_second_heat, z_first, z_second):
    odd_y, odd_z = _odd("gy"), _odd("gz")
    row = lax.broadcasted_iota(jnp.int32, (240, CELLS), 0)
    column = lax.broadcasted_iota(jnp.int32, (240, CELLS), 1)
    second = row >= 96
    within = jnp.where(second, row - 96, row)
    third = (within * 171) >> 9
    top_y = (BY - 3) * jnp.where(second, odd_y, 1 - odd_y)
    along_y = BY * third + (within - 3 * third) + top_y
    second = row >= 216
    top_z = (CELLS - 24) * jnp.where(second, odd_z, 1 - odd_z)
    along_z = jnp.where(second, row - 216, row - 192) + top_z
    source = jnp.where(row >= 192, along_z, along_y)
    pick = jnp.where(column == source, 1.0, 0.0).astype(BF16)
    for q in range(4):
        rows = _dot(pick, state[q])
        first, second, at = (y_first, y_second, q) if q < 3 else (y_first_heat, y_second_heat, 0)
        first[at] = rows[0:96].astype(BF16)
        second[at] = rows[96:192].astype(BF16)
        z_first[q] = rows[192:216].astype(BF16)
        z_second[q] = rows[216:240].astype(BF16)


def local_kernel(
    metric, strain, wave_x, state, along, waves, partial, partial_heat, carrier_y, carrier_z, factors
):
    along_x, along_y = along[:NX], along[NX:, :CELLS]
    speeds = [state[q].astype(F32) for q in range(4)]
    contra = [
        metric[0, j] * speeds[0] + metric[1, j] * speeds[1] + metric[2, j] * speeds[2]
        for j in range(3)
    ]
    scale = -STEP / 60.0
    carrier_y[...] = scale * contra[1]
    carrier_z[0:24] = scale * contra[2][0:24]
    carrier_z[24:48] = scale * contra[2][CELLS - 24 :]
    nothing = jnp.zeros((24, NX), F32)
    for q in range(4):
        d_x = _dot(state[q], along_x)
        d_y = _dot(along_y, state[q])
        tall = jnp.concatenate([nothing, speeds[q], nothing], axis=0)

        def moved(k):
            return tall[(3 + k) * BY : (3 + k) * BY + CELLS]

        d_z = (
            45.0 * (moved(1) - moved(-1)) - 9.0 * (moved(2) - moved(-2)) + (moved(3) - moved(-3))
        )
        carried = contra[0] * d_x + contra[1] * d_y + contra[2] * d_z
        if q < 3:
            rest = strain[q, 0] * speeds[0] + strain[q, 1] * speeds[1] + strain[q, 2] * speeds[2]
            if q == 2:
                rest = rest - speeds[3]
        else:
            rest = speeds[2]
        value = speeds[q] + scale * carried - STEP * rest
        if q < 3:
            partial[q] = value
        else:
            partial_heat[...] = value
    here = lax.axis_index("gy") * GZ + lax.axis_index("gz")
    wave_y, wave_z, edge = waves[0], waves[1], waves[2]
    for c in range(2):
        wx = wave_x[2 * here + c]
        symbol = jnp.zeros((DEV, CELLS), F32)
        for i in range(3):
            mixed = metric[i, 0] * wx + metric[i, 1] * wave_y + metric[i, 2] * wave_z
            symbol = symbol + mixed * mixed
        out = (edge * jnp.where(2 * here + c == 0, 1.0, 0.0)) > 0.5
        factors[c] = jnp.where(
            out, 0.0, -1.0 / (jnp.where(out, 1.0, symbol) * float(NX * NY * NZ))
        )


def _complete(partial, carrier_y, carrier_z, y_first, y_second, z_first, z_second, along_y, along_z):
    odd_y, odd_z = _odd("gy"), _odd("gz")
    beside = jnp.concatenate([y_first, y_second], axis=0)
    whole = partial + carrier_y[...] * _dot(along_y[odd_y], beside)
    first, second = _dot(along_z[odd_z], z_first), _dot(along_z[1 - odd_z], z_second)
    below = jnp.where(odd_z == 1, first, second)
    above = jnp.where(odd_z == 1, second, first)
    low = whole[:24] + carrier_z[0:24] * below
    high = whole[CELLS - 24 :] + carrier_z[24:48] * above
    return jnp.concatenate([low, whole[24 : CELLS - 24], high], axis=0)


def forward_kernel(
    metric,
    partial,
    carrier_y,
    carrier_z,
    y_first,
    y_second,
    z_first,
    z_second,
    along_y,
    along_z,
    spread,
    along_x,
    waves,
    provisional,
    sent,
):
    fields = [
        _complete(
            partial[q],
            carrier_y,
            carrier_z,
            y_first[q],
            y_second[q],
            z_first[q],
            z_second[q],
            along_y,
            along_z,
        )
        for q in range(3)
    ]
    for q in range(3):
        provisional[q] = fields[q]
    flux = [
        metric[0, j] * fields[0] + metric[1, j] * fields[1] + metric[2, j] * fields[2]
        for j in range(3)
    ]
    flux = [_split(f, 2) for f in flux]
    stacked = jnp.concatenate([flux[1][0], flux[2][0], flux[1][1], flux[2][1]], axis=0)
    own = _dot(jnp.concatenate(flux[0], axis=1), along_x[...])
    for part in range(EXT // CELLS):
        block = _dot(spread[part * CELLS : (part + 1) * CELLS], stacked)
        if part == 0:
            block = block + own
        high, low = _split(block, 2)
        spectrum = _dot_nt(waves[...], jnp.concatenate([high, high, low], axis=1))
        for t in range(CELLS // 128):
            at = 4 * (part * (CELLS // 128) + t)
            sent[:, at : at + 4, :] = spectrum[:, 128 * t : 128 * t + 128].reshape(DEV, 4, 128)


def plane_kernel(factors, got, outer, outer_back, twist, inner, inner_back, sent):
    chunks = EXT // 128
    parts = []
    for t in range(chunks):
        tr, ti = twist[0, :, 128 * t : 128 * t + 128], twist[1, :, 128 * t : 128 * t + 128]
        block = jnp.concatenate(
            [
                jnp.concatenate([got[:, 4 * t + 2 * c + part, :] for c in range(2)], axis=1)
                for part in range(2)
            ],
            axis=0,
        )
        high, low = _split(block, 2)
        block = _dot(outer[...], jnp.concatenate([high, high, low], axis=0))
        rows = []
        for c in range(2):
            at = slice(128 * c, 128 * c + 128)
            re, im = block[:DEV, at], block[DEV:, at]
            rows.append(jnp.concatenate([re * tr - im * ti, re * ti + im * tr], axis=1))
        high, low = _split(jnp.concatenate(rows, axis=0), 2)
        parts += [high, high, low]
    modes = _dot(jnp.concatenate(parts, axis=1), inner[...])
    solved = []
    for c in range(2):
        factor = factors[c]
        solved.append(modes[c * DEV : (c + 1) * DEV] * jnp.concatenate([factor, factor], axis=1))
    high, low = _split(jnp.concatenate(solved, axis=0), 2)
    left = jnp.concatenate([high] * 3 + [low] * 2, axis=1)
    every = _dot(left, inner_back[...])
    for t in range(chunks):
        tr, ti = twist[0, :, 128 * t : 128 * t + 128], twist[1, :, 128 * t : 128 * t + 128]
        cells = every[:, 256 * t : 256 * t + 256]
        columns = []
        for c in range(2):
            re, im = cells[c * DEV : (c + 1) * DEV, :128], cells[c * DEV : (c + 1) * DEV, 128:]
            columns.append(jnp.concatenate([re * tr + im * ti, im * tr - re * ti], axis=0))
        high, middle, low = _split(jnp.concatenate(columns, axis=1), 3)
        block = _dot(
            outer_back[...], jnp.concatenate([high] * 2 + [middle] * 2 + [low], axis=0)
        )
        for c in range(2):
            for part in range(2):
                sent[:, 4 * t + 2 * c + part, :] = block[
                    part * DEV : (part + 1) * DEV, 128 * c : 128 * c + 128
                ]


def project_kernel(
    metric,
    got,
    gather,
    inverse,
    symbol,
    provisional,
    partial,
    carrier_y,
    carrier_z,
    y_first,
    y_second,
    z_first,
    z_second,
    along_y,
    along_z,
    motion,
    heat,
    held,
    held_heat,
    done,
):
    held_heat[...] = _complete(
        partial[...],
        carrier_y,
        carrier_z,
        y_first[0],
        y_second[0],
        z_first[3],
        z_second[3],
        along_y,
        along_z,
    )
    copies = [pltpu.make_async_copy(held_heat, heat, done.at[3])]
    copies[0].start()
    pushes = [[], [], []]
    for c in range(2):
        block = jnp.concatenate(
            [
                jnp.concatenate([got[:, 4 * t + 2 * c + part, :] for t in range(EXT // 128)], axis=1)
                for part in range(2)
            ],
            axis=0,
        )
        fields = _dot_nt(gather[...], jnp.concatenate(_split(block, 3), axis=1))
        own, along_y, along_z = (fields[j * CELLS : (j + 1) * CELLS] for j in range(3))
        along_x = jnp.concatenate([-symbol[c] * own[:, 128:], symbol[c] * own[:, :128]], axis=1)
        for i in range(3):
            push = metric[i, 0] * along_x + metric[i, 1] * along_y + metric[i, 2] * along_z
            pushes[i].append(_split(push, 2))
    for i in range(3):
        (h0, l0), (h1, l1) = pushes[i]
        value = _dot(jnp.concatenate([h0, h0, h1, h1, l0, l1], axis=1), inverse[...])
        held[i] = provisional[i] - value
        copies.append(pltpu.make_async_copy(held.at[i], motion.at[i], done.at[i]))
        copies[-1].start()
    for copy in copies:
        copy.wait()


def _swaps(count):
    first = [(i, i ^ 1) for i in range(count)]
    second = [(i, (i + 1 if i % 2 else i - 1) % count) for i in range(count)]
    return first, second


def _step(state, metric, strain):
    along_y, along_z = _difference_matrices()
    forward, inverse, symbol = _x_tables()
    outer, twist, inner, inner_back, waves = _plane_tables()
    k = np.arange(NX // 2)
    wave_x = _kt(k, NX).astype(np.float32)
    wave_x[0] = 0.0
    circulant = _exact(_circulant_x())
    spread = _exact(-np.concatenate([along_y, along_z], axis=0).T)
    spread = np.concatenate([spread, spread], axis=1)
    gather = _exact(np.concatenate([np.eye(CELLS, EXT), along_y, along_z], axis=0))
    gather = np.concatenate([gather] * 3, axis=1)
    below, above = along_y[:, CELLS : CELLS + 96], along_y[:, CELLS + 96 : CELLS + 192]
    beside_y = _exact(
        np.stack([np.concatenate([above, below], axis=1), np.concatenate([below, above], axis=1)])
    )
    beside_z = _exact(
        np.stack([along_z[CELLS - 24 :, CELLS + 216 : CELLS + 240], along_z[:24, CELLS + 192 : CELLS + 216]])
    )
    local = np.zeros((NX + CELLS, NX))
    local[:NX] = _circulant_x()
    local[NX:, :CELLS] = along_y[:, :CELLS]

    field = jax.ShapeDtypeStruct((CELLS, NX), F32)
    fields = lambda count: jax.ShapeDtypeStruct((count, CELLS, NX), F32)
    block = jax.ShapeDtypeStruct((DEV, 16, 128), F32)
    state = state.reshape(4, CELLS, NX)

    y_side = jax.ShapeDtypeStruct((3, 96, NX), BF16)
    y_side_heat = jax.ShapeDtypeStruct((1, 96, NX), BF16)
    z_side = jax.ShapeDtypeStruct((4, 24, NX), BF16)
    y_first, y_second, y_first_heat, y_second_heat, z_first, z_second = _call(
        edges_kernel,
        (y_side, y_side, y_side_heat, y_side_heat, z_side, z_side),
        [VMEM],
        "edges",
        20_000_000_000,
        64 * MIB,
        16,
    )(state)
    swaps_y, swaps_z = _swaps(GY), _swaps(GZ)
    y_first = lax.ppermute(y_first, "gy", swaps_y[0])
    y_second = lax.ppermute(y_second, "gy", swaps_y[1])
    z_first = lax.ppermute(z_first, "gz", swaps_z[0])
    z_second = lax.ppermute(z_second, "gz", swaps_z[1])
    y_first_heat = lax.ppermute(y_first_heat, "gy", swaps_y[0])
    y_second_heat = lax.ppermute(y_second_heat, "gy", swaps_y[1])
    partial, partial_heat, carrier_y, carrier_z, factors = _call(
        local_kernel,
        (
            fields(3),
            field,
            field,
            jax.ShapeDtypeStruct((48, NX), F32),
            jax.ShapeDtypeStruct((2, DEV, CELLS), F32),
        ),
        [SMEM, SMEM, SMEM, VMEM, VMEM, VMEM],
        "local",
        1_000_000_000,
        4 * MIB,
        24,
    )(metric, strain, wave_x, state, _exact(local), waves)

    provisional, sent = _call(
        forward_kernel,
        (fields(3), block),
        [SMEM] + [VMEM] * 12,
        "forward",
        2_000_000_000,
        8 * MIB,
        40,
    )(
        metric,
        partial,
        carrier_y,
        carrier_z,
        y_first,
        y_second,
        z_first,
        z_second,
        beside_y,
        beside_z,
        spread,
        np.concatenate([circulant, circulant], axis=0),
        np.concatenate(_pieces(forward, 2)[[0, 1, 0]], axis=1),
    )
    sent, y_first_heat, y_second_heat = lax.optimization_barrier(
        (sent, y_first_heat, y_second_heat)
    )
    got = lax.all_to_all(sent, ("gy", "gz"), split_axis=0, concat_axis=0, tiled=True)
    sent = _call(
        plane_kernel, block, [VMEM] * 7, "plane", 3_600_000_000, 8 * MIB, 40
    )(
        factors,
        got,
        np.concatenate(_pieces(outer, 2)[[0, 1, 0]], axis=1),
        np.concatenate(_pieces(outer.T, 2)[[0, 1, 0, 1, 0]], axis=1),
        twist,
        inner,
        inner_back,
    )
    got = lax.all_to_all(sent, ("gy", "gz"), split_axis=0, concat_axis=0, tiled=True)
    motion, heat = _call(
        project_kernel,
        (fields(3), field),
        [SMEM] + [VMEM] * 14,
        "project",
        2_500_000_000,
        8 * MIB,
        40,
        out_specs=(ANY, ANY),
        scratch_shapes=[
            pltpu.VMEM((3, CELLS, NX), F32),
            pltpu.VMEM((CELLS, NX), F32),
            pltpu.SemaphoreType.DMA((4,)),
        ],
    )(
        metric,
        got,
        gather,
        inverse,
        symbol,
        provisional,
        partial_heat,
        carrier_y,
        carrier_z,
        y_first_heat,
        y_second_heat,
        z_first,
        z_second,
        beside_y,
        beside_z,
    )
    return motion.reshape(3, BZ, BY, NX), heat.reshape(BZ, BY, NX)


def solution(mesh):
    return jax.shard_map(
        _step,
        mesh=mesh,
        in_specs=(P(None, "gz", "gy", None), P(), P()),
        out_specs=(P(None, "gz", "gy", None), P("gz", "gy", None)),
        check_vma=False,
    )
```

time: 91.1 us -> 87.7 us (0.963)
  local copies, waits for them, and re-layouts: 5.03 us -> 1.33 us
  starting transfers between devices: 12.2 us -> 13.6 us
    unnamed x42, local copies, waits for them, and re-layouts: 5.03 us -> 1.33 us
    ppermute x4 -> x6, starting transfers between devices: 12.2 us -> 13.6 us  [the longest x1 6.18 us: _step(): y_second = lax.ppermute(y_second, 'gy', swaps_y[1])]
    ppermute x4 -> x6, waiting for transfers between devices: 6.59 us -> 6.85 us  [the longest x1 5.39 us: _step(): z_second = lax.ppermute(z_second, 'gz', swaps_z[1])]
  transfers between devices with their start and end apart: 4 -> 6, of which waited for: 2 -> 2; matrix products, arithmetic and copies ran while one was open for 0% -> 0% of each run, Pallas kernels for 3% -> 7%
where the time goes in v4:
time: 87.7 us; the launch traced here: 87.5 us
  blocking collectives  48.4 us (55%)
  Pallas kernels  16.2 us (18%)
  starting transfers between devices  13.6 us (16%)
  waiting for transfers between devices  6.85 us (8%)
  local copies, waits for them, and re-layouts  1.33 us (2%)
  between operations  1.08 us (1%)
    all_to_all x2, blocking collectives, _step(): lax.all_to_all(sent, ('gy', 'gz'), split_axis=0, concat_axis=0, tiled=True)  48.4 us
    ppermute x1, starting transfers between devices, _step(): y_second = lax.ppermute(y_second, 'gy', swaps_y[1])  6.18 us
    ppermute x1, waiting for transfers between devices, _step(): z_second = lax.ppermute(z_second, 'gz', swaps_z[1])  5.39 us
    pallas_call x1, Pallas kernels, _step(): _call(project_kernel, (fields(3), field), [SMEM] + [VMEM] * 14, 'project'...  4.83 us
    pallas_call x1, Pallas kernels, _step(): _call(plane_kernel, block, [VMEM] * 7, 'plane', 3600000000, 8 * MIB, 40)  4.57 us
    pallas_call x1, Pallas kernels, _step(): _call(forward_kernel, (fields(3), block), [SMEM] + [VMEM] * 12, 'forward'...  3.29 us
    pallas_call x1, Pallas kernels, _step(): _call(local_kernel, (fields(3), field, field, jax.ShapeDtypeStruct((48, N...  3.09 us
    ppermute x1, starting transfers between devices, _step(): z_second = lax.ppermute(z_second, 'gz', swaps_z[1])  2.63 us
  transfers between devices with their start and end apart: 6, of which 2 were waited for; matrix products, arithmetic and copies ran while one was open for 0% of the time, Pallas kernels for 7%

profile of v4, /device:TPU:1, one launch (start us, length us, event | category | flops | bytes accessed | tf_op | source)
XLA Modules:
  0.0 87.5 jit_solution(16708401904489886110)
XLA Ops:
  0.6 0.0 copy-start
  0.6 1.2 %copy-done = bf16[4,32,8,512]{3,2,1,0:T(8,128)(2,1)S(1)} copy-done((bf16[4,32,8,512]{3,2,1,0:T(8,128)(2,1)S(1)}, bf16[4,32,8,512]{3,2,1,0:T(8,128)(2,1)}, u32[]{:S(2)}) %copy-start) | copy-done | bytes 1048600
  1.9 0.0 copy-start.1
  1.9 0.0 copy-start.2
  1.9 0.0 copy-start.3
  1.9 0.0 copy-start.10
  1.9 0.0 copy-start.14
  1.9 0.0 copy-start.18
  1.9 0.0 copy-start.15
  1.9 0.0 copy-start.12
  1.9 0.4 edges.1
  2.3 2.1 %collective-permute-start = (bf16[3,96,512]{2,1,0:T(8,128)(2,1)S(1)}, bf16[3,96,512]{2,1,0:T(8,128)(2,1)S(1)}, u32[]{:S(2)}, u32[]{:S(2)}) collective-permute-start(bf16[3,96,512]{2,1,0:T(8,128)(2,1)S(1)} %get-tuple-element.24), channel_id=1, source_target_pairs={{0,4},{4,0},{8,12},{12,8},{16,20},{20,16},{24,28},{28,24},{32,36},... | collective-permute-start | bytes 884744 | tf_op jit(solution)/shard_map/ppermute | solution.py:456
  4.5 6.2 %collective-permute-start.1 = (bf16[3,96,512]{2,1,0:T(8,128)(2,1)S(1)}, bf16[3,96,512]{2,1,0:T(8,128)(2,1)S(1)}, u32[]{:S(2)}, u32[]{:S(2)}) collective-permute-start(bf16[3,96,512]{2,1,0:T(8,128)(2,1)S(1)} %get-tuple-element.25), channel_id=1, source_target_pairs={{0,124},{4,8},{8,4},{12,16},{16,12},{20,24},{24,20},{28,32},{32,28... | collective-permute-start | bytes 884744 | tf_op jit(solution)/shard_map/ppermute | solution.py:457
  10.6 1.2 %collective-permute-start.2 = (bf16[4,24,512]{2,1,0:T(8,128)(2,1)S(1)}, bf16[4,24,512]{2,1,0:T(8,128)(2,1)S(1)}, u32[]{:S(2)}, u32[]{:S(2)}) collective-permute-start(bf16[4,24,512]{2,1,0:T(8,128)(2,1)S(1)} %get-tuple-element.26), channel_id=1, source_target_pairs={{0,1},{1,0},{2,3},{3,2},{4,5},{5,4},{6,7},{7,6},{8,9},{9,8},{10,11... | collective-permute-start | bytes 294920 | tf_op jit(solution)/shard_map/ppermute | solution.py:458
  11.9 2.6 %collective-permute-start.3 = (bf16[4,24,512]{2,1,0:T(8,128)(2,1)S(1)}, bf16[4,24,512]{2,1,0:T(8,128)(2,1)S(1)}, u32[]{:S(2)}, u32[]{:S(2)}) collective-permute-start(bf16[4,24,512]{2,1,0:T(8,128)(2,1)S(1)} %get-tuple-element.27), channel_id=1, source_target_pairs={{0,3},{1,2},{2,1},{3,0},{4,7},{5,6},{6,5},{7,4},{8,11},{9,10},{10,... | collective-permute-start | bytes 294920 | tf_op jit(solution)/shard_map/ppermute | solution.py:459
  14.5 0.0 copy-start.7
  14.5 0.0 copy-start.8
  14.5 0.0 copy-start.9
  14.5 0.0 copy-start.16
  14.5 0.1 collective-permute-start.4
  14.6 0.0 copy-done.1
  14.6 0.0 copy-done.2
  14.6 0.0 copy-done.3
  14.6 0.0 copy-done.10
  14.7 0.0 copy-done.14
  14.7 0.0 copy-done.18
  14.7 3.1 %local.1 = (f32[3,256,512]{2,1,0:T(8,128)S(1)}, f32[256,512]{1,0:T(8,128)S(1)}, f32[256,512]{1,0:T(8,128)S(1)}, f32[48,512]{1,0:T(8,128)S(1)}, f32[2,128,256]{2,1,0:T(8,128)S(1)}) custom-call(f32[3,3]{1,0:T(4,128)S(1)} %copy-done.3, f32[3,3]{1,0:T(4,128)S(1)} %copy-done.2, f32[256]{0:T(256)S(1)} %copy-done.18, bf16[4,256,512]{2,1,0:T(8,128)(2,1)S(1)} %bitcast.4, ...), custom_call_target="tpu_custom_call" | custom-call | flops 1000000000 | bytes 4194304 | tf_op jit(solution)/shard_map/local/pallas_call | solution.py:462
  17.8 0.0 collective-permute-done.2.z_first
  17.8 1.3 %collective-permute-start.5 = (bf16[1,96,512]{2,1,0:T(8,128)(2,1)S(1)}, bf16[1,96,512]{2,1,0:T(8,128)(2,1)S(1)}, u32[]{:S(2)}, u32[]{:S(2)}) collective-permute-start(bf16[1,96,512]{2,1,0:T(8,128)(2,1)S(1)} %get-tuple-element.30), channel_id=1, source_target_pairs={{0,124},{4,8},{8,4},{12,16},{16,12},{20,24},{24,20},{28,32},{32,28... | collective-permute-start | bytes 294920 | tf_op jit(solution)/shard_map/ppermute | solution.py:461
  19.1 5.4 %collective-permute-done.3.z_second = bf16[4,24,512]{2,1,0:T(8,128)(2,1)S(1)} collective-permute-done((bf16[4,24,512]{2,1,0:T(8,128)(2,1)S(1)}, bf16[4,24,512]{2,1,0:T(8,128)(2,1)S(1)}, u32[]{:S(2)}, u32[]{:S(2)}) %collective-permute-start.3) | collective-permute-done | bytes 98336 | tf_op jit(solution)/shard_map/ppermute | solution.py:459
  24.5 0.0 collective-permute-done.y_first
  24.5 0.0 collective-permute-done.1.y_second
  24.5 0.0 slice-start
  24.5 0.0 copy-done.15
  24.5 0.0 copy-done.7
  24.6 0.0 copy-done.8
  24.6 0.0 copy-done.9
  24.6 0.0 copy-done.16
  24.6 0.0 slice-start.1
  24.6 0.0 copy-start.4
  24.6 3.3 %forward.1 = (f32[3,256,512]{2,1,0:T(8,128)S(1)}, f32[128,16,128]{2,1,0:T(8,128)S(1)}) custom-call(f32[3,3]{1,0:T(4,128)S(1)} %copy-done.3, f32[3,256,512]{2,1,0:T(8,128)S(1)} %get-tuple-element.21.partial, f32[256,512]{1,0:T(8,128)S(1)} %get-tuple-element.22.carrier_y, f32[48,512]{1,0:T(8,128)S(1)} %get-tuple-element.23.carrier_z, ...), custom_call_target="tpu_custom_call" | custom-call | flops 2000000000 | bytes 8388608 | tf_op jit(solution)/shard_map/forward/pallas_call | solution.py:478
  27.9 0.0 copy-start.11
  27.9 0.0 copy-start.13
  27.9 0.0 collective-permute-done.4.y_first
  27.9 1.4 %collective-permute-done.5.y_second = bf16[1,96,512]{2,1,0:T(8,128)(2,1)S(1)} collective-permute-done((bf16[1,96,512]{2,1,0:T(8,128)(2,1)S(1)}, bf16[1,96,512]{2,1,0:T(8,128)(2,1)S(1)}, u32[]{:S(2)}, u32[]{:S(2)}) %collective-permute-start.5) | collective-permute-done | bytes 98336 | tf_op jit(solution)/shard_map/ppermute | solution.py:461
  29.4 25.4 %all_to_all.10.got = f32[128,16,128]{2,1,0:T(8,128)S(1)} all-to-all(f32[128,16,128]{2,1,0:T(8,128)S(1)} %get-tuple-element.31), channel_id=1, replica_groups=mesh['gy'=32,'gz'=4] {'gy','gz'}, dimensions={0} | all-to-all | bytes 2097152 | tf_op jit(solution)/shard_map/all_to_all | solution.py:504
  54.8 0.0 copy-done.12
  54.8 0.0 slice-done
  54.8 0.0 slice-done.1
  54.8 0.0 copy-done.4
  54.8 0.0 copy-done.11
  54.8 0.0 copy-done.13
  54.8 0.0 copy-start.5
  54.8 4.6 %plane.1 = f32[128,16,128]{2,1,0:T(8,128)S(1)} custom-call(f32[2,128,256]{2,1,0:T(8,128)S(1)} %get-tuple-element.20.factors, f32[128,16,128]{2,1,0:T(8,128)S(1)} %all_to_all.10.got, bf16[256,768]{1,0:T(8,128)(2,1)S(1)} %copy-done.13, bf16[256,1280]{1,0:T(8,128)(2,1)S(1)} %copy-done.11, f32[2,128,512]{2,1,0:T(8,128)S(1)} %copy-done.12, ...), custom_call_target="tpu_custom_call" | custom-call | flops 3600000000 | bytes 8388608 | tf_op jit(solution)/shard_map/plane/pallas_call | solution.py:505
  59.4 0.0 copy-start.6
  59.4 0.0 copy-start.17
  59.4 23.0 %all_to_all.11.got = f32[128,16,128]{2,1,0:T(8,128)S(1)} all-to-all(f32[128,16,128]{2,1,0:T(8,128)S(1)} %plane.1), channel_id=1, replica_groups=mesh['gy'=32,'gz'=4] {'gy','gz'}, dimensions={0} | all-to-all | bytes 2097152 | tf_op jit(solution)/shard_map/all_to_all | solution.py:516
  82.5 0.0 copy-done.5
  82.5 0.0 copy-done.6
  82.5 0.0 copy-done.17
  82.5 4.8 %project.1 = (f32[3,256,512]{2,1,0:T(8,128)}, f32[256,512]{1,0:T(8,128)}) custom-call(f32[3,3]{1,0:T(4,128)S(1)} %copy-done.3, f32[128,16,128]{2,1,0:T(8,128)S(1)} %all_to_all.11.got, bf16[768,1536]{1,0:T(8,128)(2,1)S(1)} %copy-done.5, bf16[1536,512]{1,0:T(8,128)(2,1)S(1)} %copy-done.6, f32[2,1,128]{2,1,0:T(1,128)S(1)} %copy-done.17, ...), custom_call_target="tpu_custom_call" | custom-call | flops 2500000000 | bytes 8388608 | tf_op jit(solution)/shard_map/project/pallas_call | solution.py:517
  (1 shorter events, 0.0 us)
Async XLA Ops:
  0.6 1.2 %copy-start = (bf16[4,32,8,512]{3,2,1,0:T(8,128)(2,1)S(1)}, bf16[4,32,8,512]{3,2,1,0:T(8,128)(2,1)}, u32[]{:S(2)}) copy-start(bf16[4,32,8,512]{3,2,1,0:T(8,128)(2,1)} %param.19) | copy-start | bytes 3145732
  1.9 12.8 %copy-start.1 = (bf16[4,32,8,512]{3,2,1,0:T(8,128)(2,1)S(1)}, bf16[4,32,8,512]{3,2,1,0:T(8,128)(2,1)}, u32[]{:S(2)}) copy-start(bf16[4,32,8,512]{3,2,1,0:T(8,128)(2,1)} %param.19) | copy-start | bytes 3145732
  1.9 12.8 %copy-start.2 = (f32[3,3]{1,0:T(4,128)S(1)}, f32[3,3]{1,0:T(4,128)}, u32[]{:S(2)}) copy-start(f32[3,3]{1,0:T(4,128)} %strain.1) | copy-start | bytes 112
  1.9 12.8 %copy-start.3 = (f32[3,3]{1,0:T(4,128)S(1)}, f32[3,3]{1,0:T(4,128)}, u32[]{:S(2)}) copy-start(f32[3,3]{1,0:T(4,128)} %metric.5) | copy-start | bytes 112
  1.9 12.8 %copy-start.10 = (bf16[768,512]{1,0:T(8,128)(2,1)S(1)}, bf16[768,512]{1,0:T(8,128)(2,1)}, u32[]{:S(2)}) copy-start(bf16[768,512]{1,0:T(8,128)(2,1)} %constant.33.clone.along) | copy-start | bytes 2359300
  1.9 12.8 %copy-start.14 = (f32[3,128,256]{2,1,0:T(8,128)S(1)}, f32[3,128,256]{2,1,0:T(8,128)}, u32[]{:S(2)}) copy-start(f32[3,128,256]{2,1,0:T(8,128)} %constant.34.clone.waves) | copy-start | bytes 1179652
  1.9 12.8 %copy-start.18 = (f32[256]{0:T(256)S(1)}, f32[256]{0:T(256)}, u32[]{:S(2)}) copy-start(f32[256]{0:T(256)} %constant.32.clone.wave_x) | copy-start | bytes 3076
  1.9 22.6 %copy-start.15 = (bf16[2,256,192]{2,1,0:T(8,128)(2,1)S(1)}, bf16[2,256,192]{2,1,0:T(8,128)(2,1)}, u32[]{:S(2)}) copy-start(bf16[2,256,192]{2,1,0:T(8,128)(2,1)} %constant.35.clone.along_y) | copy-start | bytes 589828
  1.9 52.9 %copy-start.12 = (f32[2,128,512]{2,1,0:T(8,128)S(1)}, f32[2,128,512]{2,1,0:T(8,128)}, u32[]{:S(2)}) copy-start(f32[2,128,512]{2,1,0:T(8,128)} %constant.42.clone.twist) | copy-start | bytes 1572868
  2.3 22.2 %collective-permute-start = (bf16[3,96,512]{2,1,0:T(8,128)(2,1)S(1)}, bf16[3,96,512]{2,1,0:T(8,128)(2,1)S(1)}, u32[]{:S(2)}, u32[]{:S(2)}) collective-permute-start(bf16[3,96,512]{2,1,0:T(8,128)(2,1)S(1)} %get-tuple-element.24), channel_id=1, source_target_pairs={{0,4},{4,0},{8,12},{12,8},{16,20},{20,16},{24,28},{28,24},{32,36},... | collective-permute-start | bytes 884744 | tf_op jit(solution)/shard_map/ppermute | solution.py:456
  4.5 20.1 %collective-permute-start.1 = (bf16[3,96,512]{2,1,0:T(8,128)(2,1)S(1)}, bf16[3,96,512]{2,1,0:T(8,128)(2,1)S(1)}, u32[]{:S(2)}, u32[]{:S(2)}) collective-permute-start(bf16[3,96,512]{2,1,0:T(8,128)(2,1)S(1)} %get-tuple-element.25), channel_id=1, source_target_pairs={{0,124},{4,8},{8,4},{12,16},{16,12},{20,24},{24,20},{28,32},{32,28... | collective-permute-start | bytes 884744 | tf_op jit(solution)/shard_map/ppermute | solution.py:457
  10.6 7.1 %collective-permute-start.2 = (bf16[4,24,512]{2,1,0:T(8,128)(2,1)S(1)}, bf16[4,24,512]{2,1,0:T(8,128)(2,1)S(1)}, u32[]{:S(2)}, u32[]{:S(2)}) collective-permute-start(bf16[4,24,512]{2,1,0:T(8,128)(2,1)S(1)} %get-tuple-element.26), channel_id=1, source_target_pairs={{0,1},{1,0},{2,3},{3,2},{4,5},{5,4},{6,7},{7,6},{8,9},{9,8},{10,11... | collective-permute-start | bytes 294920 | tf_op jit(solution)/shard_map/ppermute | solution.py:458
  11.9 12.6 %collective-permute-start.3 = (bf16[4,24,512]{2,1,0:T(8,128)(2,1)S(1)}, bf16[4,24,512]{2,1,0:T(8,128)(2,1)S(1)}, u32[]{:S(2)}, u32[]{:S(2)}) collective-permute-start(bf16[4,24,512]{2,1,0:T(8,128)(2,1)S(1)} %get-tuple-element.27), channel_id=1, source_target_pairs={{0,3},{1,2},{2,1},{3,0},{4,7},{5,6},{6,5},{7,4},{8,11},{9,10},{10,... | collective-permute-start | bytes 294920 | tf_op jit(solution)/shard_map/ppermute | solution.py:459
  14.5 10.0 %copy-start.7 = (bf16[512,1536]{1,0:T(8,128)(2,1)S(1)}, bf16[512,1536]{1,0:T(8,128)(2,1)}, u32[]{:S(2)}) copy-start(bf16[512,1536]{1,0:T(8,128)(2,1)} %constant.39.clone.waves) | copy-start | bytes 4718596
  14.5 10.0 %copy-start.8 = (bf16[1024,512]{1,0:T(8,128)(2,1)S(1)}, bf16[1024,512]{1,0:T(8,128)(2,1)}, u32[]{:S(2)}) copy-start(bf16[1024,512]{1,0:T(8,128)(2,1)} %constant.38.clone.along_x) | copy-start | bytes 3145732
  14.5 10.0 %copy-start.9 = (bf16[512,1024]{1,0:T(8,128)(2,1)S(1)}, bf16[512,1024]{1,0:T(8,128)(2,1)}, u32[]{:S(2)}) copy-start(bf16[512,1024]{1,0:T(8,128)(2,1)} %constant.37.clone.spread) | copy-start | bytes 3145732
  14.5 10.1 %copy-start.16 = (bf16[2,24,24]{2,1,0:T(8,128)(2,1)S(1)}, bf16[2,24,24]{2,1,0:T(8,128)(2,1)}, u32[]{:S(2)}) copy-start(bf16[2,24,24]{2,1,0:T(8,128)(2,1)} %constant.36.clone.along_z) | copy-start | bytes 6916
  14.5 13.4 %collective-permute-start.4 = (bf16[1,96,512]{2,1,0:T(8,128)(2,1)S(1)}, bf16[1,96,512]{2,1,0:T(8,128)(2,1)S(1)}, u32[]{:S(2)}, u32[]{:S(2)}) collective-permute-start(bf16[1,96,512]{2,1,0:T(8,128)(2,1)S(1)} %get-tuple-element.29), channel_id=1, source_target_pairs={{0,4},{4,0},{8,12},{12,8},{16,20},{20,16},{24,28},{28,24},{32,36},... | collective-permute-start | bytes 294920 | tf_op jit(solution)/shard_map/ppermute | solution.py:460
  17.8 11.6 %collective-permute-start.5 = (bf16[1,96,512]{2,1,0:T(8,128)(2,1)S(1)}, bf16[1,96,512]{2,1,0:T(8,128)(2,1)S(1)}, u32[]{:S(2)}, u32[]{:S(2)}) collective-permute-start(bf16[1,96,512]{2,1,0:T(8,128)(2,1)S(1)} %get-tuple-element.30), channel_id=1, source_target_pairs={{0,124},{4,8},{8,4},{12,16},{16,12},{20,24},{24,20},{28,32},{32,28... | collective-permute-start | bytes 294920 | tf_op jit(solution)/shard_map/ppermute | solution.py:461
  24.5 30.3 %slice-start = ((s8[5242880]{0:T(1024)(128)(4,1)}), s8[4194304]{0:T(1024)(128)(4,1)S(1)}, s32[]{:S(2)}) async-start(s8[5242880]{0:T(1024)(128)(4,1)} %bitcast.5), calls=%async_computation.2 | async-start | bytes 8388608
  24.6 30.2 %slice-start.1 = ((s8[5242880]{0:T(1024)(128)(4,1)}), s8[1048576]{0:T(1024)(128)(4,1)S(1)}, s32[]{:S(2)}) async-start(s8[5242880]{0:T(1024)(128)(4,1)} %bitcast.5), calls=%async_computation.3 | async-start | bytes 2097152
  24.6 30.2 %copy-start.4 = (bf16[3072,512]{1,0:T(8,128)(2,1)S(1)}, bf16[3072,512]{1,0:T(8,128)(2,1)}, u32[]{:S(2)}) copy-start(bf16[3072,512]{1,0:T(8,128)(2,1)} %constant.43.clone.inner) | copy-start | bytes 9437188
  27.9 26.9 %copy-start.11 = (bf16[256,1280]{1,0:T(8,128)(2,1)S(1)}, bf16[256,1280]{1,0:T(8,128)(2,1)}, u32[]{:S(2)}) copy-start(bf16[256,1280]{1,0:T(8,128)(2,1)} %constant.41.clone.outer_back) | copy-start | bytes 1966084
  27.9 26.9 %copy-start.13 = (bf16[256,768]{1,0:T(8,128)(2,1)S(1)}, bf16[256,768]{1,0:T(8,128)(2,1)}, u32[]{:S(2)}) copy-start(bf16[256,768]{1,0:T(8,128)(2,1)} %constant.40.clone.outer) | copy-start | bytes 1179652
  54.8 27.6 %copy-start.5 = (bf16[768,1536]{1,0:T(8,128)(2,1)S(1)}, bf16[768,1536]{1,0:T(8,128)(2,1)}, u32[]{:S(2)}) copy-start(bf16[768,1536]{1,0:T(8,128)(2,1)} %constant.45.clone.gather) | copy-start | bytes 7077892
  59.4 23.0 %copy-start.6 = (bf16[1536,512]{1,0:T(8,128)(2,1)S(1)}, bf16[1536,512]{1,0:T(8,128)(2,1)}, u32[]{:S(2)}) copy-start(bf16[1536,512]{1,0:T(8,128)(2,1)} %constant.46.clone.inverse) | copy-start | bytes 4718596
  59.4 23.0 %copy-start.17 = (f32[2,1,128]{2,1,0:T(1,128)S(1)}, f32[2,1,128]{2,1,0:T(1,128)}, u32[]{:S(2)}) copy-start(f32[2,1,128]{2,1,0:T(1,128)} %constant.47.clone.symbol) | copy-start | bytes 3076

commit v5 on v4

--- a/solution.py
+++ b/solution.py
@@ -286,12 +286,15 @@
         for j in range(3)
     ]
     flux = [_split(f, 2) for f in flux]
-    stacked = jnp.concatenate([flux[1][0], flux[2][0], flux[1][1], flux[2][1]], axis=0)
+    stacked = [jnp.concatenate(flux[j], axis=0) for j in (1, 2)]
     own = _dot(jnp.concatenate(flux[0], axis=1), along_x[...])
     for part in range(EXT // CELLS):
-        block = _dot(spread[part * CELLS : (part + 1) * CELLS], stacked)
         if part == 0:
-            block = block + own
+            block = own + _dot(spread[:CELLS], jnp.concatenate(stacked, axis=0))
+        else:
+            beside_y = _dot(spread[CELLS : CELLS + 192, :NX], stacked[0])
+            beside_z = _dot(spread[CELLS + 192 :, NX:], stacked[1])
+            block = jnp.concatenate([beside_y, beside_z], axis=0)
         high, low = _split(block, 2)
         spectrum = _dot_nt(waves[...], jnp.concatenate([high, high, low], axis=1))
         for t in range(CELLS // 128):
@@ -350,6 +353,7 @@
     metric,
     got,
     gather,
+    keep,
     inverse,
     symbol,
     provisional,
@@ -390,8 +394,10 @@
             ],
             axis=0,
         )
-        fields = _dot_nt(gather[...], jnp.concatenate(_split(block, 3), axis=1))
-        own, along_y, along_z = (fields[j * CELLS : (j + 1) * CELLS] for j in range(3))
+        split = _split(block, 3)
+        fields = _dot_nt(gather[...], jnp.concatenate(split, axis=1))
+        along_y, along_z = fields[:CELLS], fields[CELLS:]
+        own = _dot_nt(keep[...], jnp.concatenate([p[:, :CELLS] for p in split[:2]], axis=1))
         along_x = jnp.concatenate([-symbol[c] * own[:, 128:], symbol[c] * own[:, :128]], axis=1)
         for i in range(3):
             push = metric[i, 0] * along_x + metric[i, 1] * along_y + metric[i, 2] * along_z
@@ -420,9 +426,9 @@
     wave_x = _kt(k, NX).astype(np.float32)
     wave_x[0] = 0.0
     circulant = _exact(_circulant_x())
-    spread = _exact(-np.concatenate([along_y, along_z], axis=0).T)
-    spread = np.concatenate([spread, spread], axis=1)
-    gather = _exact(np.concatenate([np.eye(CELLS, EXT), along_y, along_z], axis=0))
+    spread = _exact(-np.concatenate([along_y, along_y, along_z, along_z], axis=0).T)
+    gather = _exact(np.concatenate([along_y, along_z], axis=0))
+    keep = _exact(np.concatenate([np.eye(CELLS)] * 2, axis=1))
     gather = np.concatenate([gather] * 3, axis=1)
     below, above = along_y[:, CELLS : CELLS + 96], along_y[:, CELLS + 96 : CELLS + 192]
     beside_y = _exact(
@@ -457,8 +463,6 @@
     y_second = lax.ppermute(y_second, "gy", swaps_y[1])
     z_first = lax.ppermute(z_first, "gz", swaps_z[0])
     z_second = lax.ppermute(z_second, "gz", swaps_z[1])
-    y_first_heat = lax.ppermute(y_first_heat, "gy", swaps_y[0])
-    y_second_heat = lax.ppermute(y_second_heat, "gy", swaps_y[1])
     partial, partial_heat, carrier_y, carrier_z, factors = _call(
         local_kernel,
         (
@@ -475,6 +479,11 @@
         24,
     )(metric, strain, wave_x, state, _exact(local), waves)
 
+    y_first_heat, y_second_heat, carrier_z = lax.optimization_barrier(
+        (y_first_heat, y_second_heat, carrier_z)
+    )
+    y_first_heat = lax.ppermute(y_first_heat, "gy", swaps_y[0])
+    y_second_heat = lax.ppermute(y_second_heat, "gy", swaps_y[1])
     provisional, sent = _call(
         forward_kernel,
         (fields(3), block),
@@ -517,7 +526,7 @@
     motion, heat = _call(
         project_kernel,
         (fields(3), field),
-        [SMEM] + [VMEM] * 14,
+        [SMEM] + [VMEM] * 15,
         "project",
         2_500_000_000,
         8 * MIB,
@@ -532,6 +541,7 @@
         metric,
         got,
         gather,
+        keep,
         inverse,
         symbol,
         provisional,

time: 87.7 us -> 87.2 us (level)
  no operation moved by 1% of the time
where the time goes in v5:
time: 87.2 us; the launch traced here: 87 us
  blocking collectives  48.4 us (56%)
  Pallas kernels  15.6 us (18%)
  starting transfers between devices  13.6 us (16%)
  waiting for transfers between devices  7 us (8%)
  local copies, waits for them, and re-layouts  1.33 us (2%)
  between operations  1.07 us (1%)
    all_to_all x2, blocking collectives, _step(): lax.all_to_all(sent, ('gy', 'gz'), split_axis=0, concat_axis=0, tiled=True)  48.4 us
    ppermute x1, starting transfers between devices, _step(): y_second = lax.ppermute(y_second, 'gy', swaps_y[1])  6.18 us
    ppermute x1, waiting for transfers between devices, _step(): z_second = lax.ppermute(z_second, 'gz', swaps_z[1])  5.38 us
    pallas_call x1, Pallas kernels, _step(): _call(plane_kernel, block, [VMEM] * 7, 'plane', 3600000000, 8 * MIB, 40)  4.58 us
    pallas_call x1, Pallas kernels, _step(): _call(project_kernel, (fields(3), field), [SMEM] + [VMEM] * 15, 'project'...  4.35 us
    pallas_call x1, Pallas kernels, _step(): _call(forward_kernel, (fields(3), block), [SMEM] + [VMEM] * 12, 'forward'...  3.14 us
    pallas_call x1, Pallas kernels, _step(): _call(local_kernel, (fields(3), field, field, jax.ShapeDtypeStruct((48, N...  3.08 us
    ppermute x1, starting transfers between devices, _step(): z_second = lax.ppermute(z_second, 'gz', swaps_z[1])  2.72 us
  transfers between devices with their start and end apart: 6, of which 2 were waited for; matrix products, arithmetic and copies ran while one was open for 0% of the time, Pallas kernels for 7%

profile of v5, /device:TPU:1, one launch (start us, length us, event | category | flops | bytes accessed | tf_op | source)
XLA Modules:
  0.0 87.0 jit_solution(9070597420094097207)
XLA Ops:
  0.6 0.0 copy-start
  0.6 1.2 %copy-done = bf16[4,32,8,512]{3,2,1,0:T(8,128)(2,1)S(1)} copy-done((bf16[4,32,8,512]{3,2,1,0:T(8,128)(2,1)S(1)}, bf16[4,32,8,512]{3,2,1,0:T(8,128)(2,1)}, u32[]{:S(2)}) %copy-start) | copy-done | bytes 1048600
  1.9 0.0 copy-start.1
  1.9 0.0 copy-start.2
  1.9 0.0 copy-start.3
  1.9 0.0 copy-start.10
  1.9 0.0 copy-start.14
  1.9 0.0 copy-start.19
  1.9 0.0 copy-start.15
  1.9 0.0 copy-start.12
  1.9 0.4 edges.1
  2.3 2.1 %collective-permute-start = (bf16[3,96,512]{2,1,0:T(8,128)(2,1)S(1)}, bf16[3,96,512]{2,1,0:T(8,128)(2,1)S(1)}, u32[]{:S(2)}, u32[]{:S(2)}) collective-permute-start(bf16[3,96,512]{2,1,0:T(8,128)(2,1)S(1)} %get-tuple-element.30), channel_id=1, source_target_pairs={{0,4},{4,0},{8,12},{12,8},{16,20},{20,16},{24,28},{28,24},{32,36},... | collective-permute-start | bytes 884744 | tf_op jit(solution)/shard_map/ppermute | solution.py:462
  4.5 6.2 %collective-permute-start.1 = (bf16[3,96,512]{2,1,0:T(8,128)(2,1)S(1)}, bf16[3,96,512]{2,1,0:T(8,128)(2,1)S(1)}, u32[]{:S(2)}, u32[]{:S(2)}) collective-permute-start(bf16[3,96,512]{2,1,0:T(8,128)(2,1)S(1)} %get-tuple-element.31), channel_id=1, source_target_pairs={{0,124},{4,8},{8,4},{12,16},{16,12},{20,24},{24,20},{28,32},{32,28... | collective-permute-start | bytes 884744 | tf_op jit(solution)/shard_map/ppermute | solution.py:463
  10.6 1.2 %collective-permute-start.2 = (bf16[4,24,512]{2,1,0:T(8,128)(2,1)S(1)}, bf16[4,24,512]{2,1,0:T(8,128)(2,1)S(1)}, u32[]{:S(2)}, u32[]{:S(2)}) collective-permute-start(bf16[4,24,512]{2,1,0:T(8,128)(2,1)S(1)} %get-tuple-element.32), channel_id=1, source_target_pairs={{0,1},{1,0},{2,3},{3,2},{4,5},{5,4},{6,7},{7,6},{8,9},{9,8},{10,11... | collective-permute-start | bytes 294920 | tf_op jit(solution)/shard_map/ppermute | solution.py:464
  11.9 0.0 copy-start.7
  11.9 0.0 copy-start.8
  11.9 0.0 copy-start.9
  11.9 0.0 copy-start.17
  11.9 2.7 %collective-permute-start.3 = (bf16[4,24,512]{2,1,0:T(8,128)(2,1)S(1)}, bf16[4,24,512]{2,1,0:T(8,128)(2,1)S(1)}, u32[]{:S(2)}, u32[]{:S(2)}) collective-permute-start(bf16[4,24,512]{2,1,0:T(8,128)(2,1)S(1)} %get-tuple-element.33), channel_id=1, source_target_pairs={{0,3},{1,2},{2,1},{3,0},{4,7},{5,6},{6,5},{7,4},{8,11},{9,10},{10,... | collective-permute-start | bytes 294920 | tf_op jit(solution)/shard_map/ppermute | solution.py:465
  14.6 0.0 copy-done.1
  14.6 0.0 copy-done.2
  14.6 0.0 copy-done.3
  14.6 0.0 copy-done.10
  14.6 0.0 copy-done.14
  14.6 0.0 copy-done.19
  14.6 3.1 %local.1 = (f32[3,256,512]{2,1,0:T(8,128)S(1)}, f32[256,512]{1,0:T(8,128)S(1)}, f32[256,512]{1,0:T(8,128)S(1)}, f32[48,512]{1,0:T(8,128)S(1)}, f32[2,128,256]{2,1,0:T(8,128)S(1)}) custom-call(f32[3,3]{1,0:T(4,128)S(1)} %copy-done.3, f32[3,3]{1,0:T(4,128)S(1)} %copy-done.2, f32[256]{0:T(256)S(1)} %copy-done.19, bf16[4,256,512]{2,1,0:T(8,128)(2,1)S(1)} %bitcast.4, ...), custom_call_target="tpu_custom_call" | custom-call | flops 1000000000 | bytes 4194304 | tf_op jit(solution)/shard_map/local/pallas_call | solution.py:466
  17.7 0.1 collective-permute-start.4
  17.8 0.0 collective-permute-done.2.z_first
  17.8 1.3 %collective-permute-start.5 = (bf16[1,96,512]{2,1,0:T(8,128)(2,1)S(1)}, bf16[1,96,512]{2,1,0:T(8,128)(2,1)S(1)}, u32[]{:S(2)}, u32[]{:S(2)}) collective-permute-start(bf16[1,96,512]{2,1,0:T(8,128)(2,1)S(1)} %get-tuple-element.36), channel_id=1, source_target_pairs={{0,124},{4,8},{8,4},{12,16},{16,12},{20,24},{24,20},{28,32},{32,28... | collective-permute-start | bytes 294920 | tf_op jit(solution)/shard_map/ppermute | solution.py:486
  19.1 5.4 %collective-permute-done.3.z_second = bf16[4,24,512]{2,1,0:T(8,128)(2,1)S(1)} collective-permute-done((bf16[4,24,512]{2,1,0:T(8,128)(2,1)S(1)}, bf16[4,24,512]{2,1,0:T(8,128)(2,1)S(1)}, u32[]{:S(2)}, u32[]{:S(2)}) %collective-permute-start.3) | collective-permute-done | bytes 98336 | tf_op jit(solution)/shard_map/ppermute | solution.py:465
  24.5 0.0 collective-permute-done.y_first
  24.5 0.0 collective-permute-done.1.y_second
  24.5 0.0 slice-start
  24.5 0.0 copy-done.15
  24.5 0.0 copy-done.7
  24.6 0.0 copy-done.8
  24.6 0.0 copy-done.9
  24.6 0.0 copy-done.17
  24.6 0.0 slice-start.1
  24.6 0.0 copy-start.4
  24.6 3.1 %forward.1 = (f32[3,256,512]{2,1,0:T(8,128)S(1)}, f32[128,16,128]{2,1,0:T(8,128)S(1)}) custom-call(f32[3,3]{1,0:T(4,128)S(1)} %copy-done.3, f32[3,256,512]{2,1,0:T(8,128)S(1)} %get-tuple-element.24.partial, f32[256,512]{1,0:T(8,128)S(1)} %get-tuple-element.25.carrier_y, f32[48,512]{1,0:T(8,128)S(1)} %get-tuple-element.29.carrier_z, ...), custom_call_target="tpu_custom_call" | custom-call | flops 2000000000 | bytes 8388608 | tf_op jit(solution)/shard_map/forward/pallas_call | solution.py:487
  27.8 0.0 copy-start.11
  27.8 0.0 copy-start.13
  27.8 0.0 collective-permute-done.4.y_first
  27.8 1.6 %collective-permute-done.5.y_second = bf16[1,96,512]{2,1,0:T(8,128)(2,1)S(1)} collective-permute-done((bf16[1,96,512]{2,1,0:T(8,128)(2,1)S(1)}, bf16[1,96,512]{2,1,0:T(8,128)(2,1)S(1)}, u32[]{:S(2)}, u32[]{:S(2)}) %collective-permute-start.5) | collective-permute-done | bytes 98336 | tf_op jit(solution)/shard_map/ppermute | solution.py:486
  29.4 25.4 %all_to_all.10.got = f32[128,16,128]{2,1,0:T(8,128)S(1)} all-to-all(f32[128,16,128]{2,1,0:T(8,128)S(1)} %get-tuple-element.37), channel_id=1, replica_groups=mesh['gy'=32,'gz'=4] {'gy','gz'}, dimensions={0} | all-to-all | bytes 2097152 | tf_op jit(solution)/shard_map/all_to_all | solution.py:513
  54.8 0.0 copy-done.12
  54.8 0.0 slice-done
  54.8 0.0 slice-done.1
  54.8 0.0 copy-done.4
  54.8 0.0 copy-done.11
  54.8 0.0 copy-done.13
  54.8 0.0 copy-start.6
  54.8 4.6 %plane.1 = f32[128,16,128]{2,1,0:T(8,128)S(1)} custom-call(f32[2,128,256]{2,1,0:T(8,128)S(1)} %get-tuple-element.23.factors, f32[128,16,128]{2,1,0:T(8,128)S(1)} %all_to_all.10.got, bf16[256,768]{1,0:T(8,128)(2,1)S(1)} %copy-done.13, bf16[256,1280]{1,0:T(8,128)(2,1)S(1)} %copy-done.11, f32[2,128,512]{2,1,0:T(8,128)S(1)} %copy-done.12, ...), custom_call_target="tpu_custom_call" | custom-call | flops 3600000000 | bytes 8388608 | tf_op jit(solution)/shard_map/plane/pallas_call | solution.py:514
  59.4 0.0 copy-start.5
  59.4 0.0 copy-start.16
  59.4 0.0 copy-start.18
  59.5 23.0 %all_to_all.11.got = f32[128,16,128]{2,1,0:T(8,128)S(1)} all-to-all(f32[128,16,128]{2,1,0:T(8,128)S(1)} %plane.1), channel_id=1, replica_groups=mesh['gy'=32,'gz'=4] {'gy','gz'}, dimensions={0} | all-to-all | bytes 2097152 | tf_op jit(solution)/shard_map/all_to_all | solution.py:525
  82.5 0.0 copy-done.6
  82.5 0.0 copy-done.5
  82.5 0.0 copy-done.16
  82.5 0.0 copy-done.18
  82.5 4.3 %project.1 = (f32[3,256,512]{2,1,0:T(8,128)}, f32[256,512]{1,0:T(8,128)}) custom-call(f32[3,3]{1,0:T(4,128)S(1)} %copy-done.3, f32[128,16,128]{2,1,0:T(8,128)S(1)} %all_to_all.11.got, bf16[512,1536]{1,0:T(8,128)(2,1)S(1)} %copy-done.6, bf16[256,512]{1,0:T(8,128)(2,1)S(1)} %copy-done.16, bf16[1536,512]{1,0:T(8,128)(2,1)S(1)} %copy-done.5, ...), custom_call_target="tpu_custom_call" | custom-call | flops 2500000000 | bytes 8388608 | tf_op jit(solution)/shard_map/project/pallas_call | solution.py:526
  (1 shorter events, 0.0 us)
Async XLA Ops:
  0.6 1.2 %copy-start = (bf16[4,32,8,512]{3,2,1,0:T(8,128)(2,1)S(1)}, bf16[4,32,8,512]{3,2,1,0:T(8,128)(2,1)}, u32[]{:S(2)}) copy-start(bf16[4,32,8,512]{3,2,1,0:T(8,128)(2,1)} %param.20) | copy-start | bytes 3145732
  1.9 12.8 %copy-start.1 = (bf16[4,32,8,512]{3,2,1,0:T(8,128)(2,1)S(1)}, bf16[4,32,8,512]{3,2,1,0:T(8,128)(2,1)}, u32[]{:S(2)}) copy-start(bf16[4,32,8,512]{3,2,1,0:T(8,128)(2,1)} %param.20) | copy-start | bytes 3145732
  1.9 12.8 %copy-start.2 = (f32[3,3]{1,0:T(4,128)S(1)}, f32[3,3]{1,0:T(4,128)}, u32[]{:S(2)}) copy-start(f32[3,3]{1,0:T(4,128)} %strain.1) | copy-start | bytes 112
  1.9 12.8 %copy-start.3 = (f32[3,3]{1,0:T(4,128)S(1)}, f32[3,3]{1,0:T(4,128)}, u32[]{:S(2)}) copy-start(f32[3,3]{1,0:T(4,128)} %metric.5) | copy-start | bytes 112
  1.9 12.8 %copy-start.10 = (bf16[768,512]{1,0:T(8,128)(2,1)S(1)}, bf16[768,512]{1,0:T(8,128)(2,1)}, u32[]{:S(2)}) copy-start(bf16[768,512]{1,0:T(8,128)(2,1)} %constant.35.clone.along) | copy-start | bytes 2359300
  1.9 12.8 %copy-start.14 = (f32[3,128,256]{2,1,0:T(8,128)S(1)}, f32[3,128,256]{2,1,0:T(8,128)}, u32[]{:S(2)}) copy-start(f32[3,128,256]{2,1,0:T(8,128)} %constant.36.clone.waves) | copy-start | bytes 1179652
  1.9 12.8 %copy-start.19 = (f32[256]{0:T(256)S(1)}, f32[256]{0:T(256)}, u32[]{:S(2)}) copy-start(f32[256]{0:T(256)} %constant.34.clone.wave_x) | copy-start | bytes 3076
  1.9 22.6 %copy-start.15 = (bf16[2,256,192]{2,1,0:T(8,128)(2,1)S(1)}, bf16[2,256,192]{2,1,0:T(8,128)(2,1)}, u32[]{:S(2)}) copy-start(bf16[2,256,192]{2,1,0:T(8,128)(2,1)} %constant.37.clone.along_y) | copy-start | bytes 589828
  1.9 52.9 %copy-start.12 = (f32[2,128,512]{2,1,0:T(8,128)S(1)}, f32[2,128,512]{2,1,0:T(8,128)}, u32[]{:S(2)}) copy-start(f32[2,128,512]{2,1,0:T(8,128)} %constant.44.clone.twist) | copy-start | bytes 1572868
  2.3 22.2 %collective-permute-start = (bf16[3,96,512]{2,1,0:T(8,128)(2,1)S(1)}, bf16[3,96,512]{2,1,0:T(8,128)(2,1)S(1)}, u32[]{:S(2)}, u32[]{:S(2)}) collective-permute-start(bf16[3,96,512]{2,1,0:T(8,128)(2,1)S(1)} %get-tuple-element.30), channel_id=1, source_target_pairs={{0,4},{4,0},{8,12},{12,8},{16,20},{20,16},{24,28},{28,24},{32,36},... | collective-permute-start | bytes 884744 | tf_op jit(solution)/shard_map/ppermute | solution.py:462
  4.5 20.1 %collective-permute-start.1 = (bf16[3,96,512]{2,1,0:T(8,128)(2,1)S(1)}, bf16[3,96,512]{2,1,0:T(8,128)(2,1)S(1)}, u32[]{:S(2)}, u32[]{:S(2)}) collective-permute-start(bf16[3,96,512]{2,1,0:T(8,128)(2,1)S(1)} %get-tuple-element.31), channel_id=1, source_target_pairs={{0,124},{4,8},{8,4},{12,16},{16,12},{20,24},{24,20},{28,32},{32,28... | collective-permute-start | bytes 884744 | tf_op jit(solution)/shard_map/ppermute | solution.py:463
  10.6 7.2 %collective-permute-start.2 = (bf16[4,24,512]{2,1,0:T(8,128)(2,1)S(1)}, bf16[4,24,512]{2,1,0:T(8,128)(2,1)S(1)}, u32[]{:S(2)}, u32[]{:S(2)}) collective-permute-start(bf16[4,24,512]{2,1,0:T(8,128)(2,1)S(1)} %get-tuple-element.32), channel_id=1, source_target_pairs={{0,1},{1,0},{2,3},{3,2},{4,5},{5,4},{6,7},{7,6},{8,9},{9,8},{10,11... | collective-permute-start | bytes 294920 | tf_op jit(solution)/shard_map/ppermute | solution.py:464
  11.9 12.7 %copy-start.7 = (bf16[512,1536]{1,0:T(8,128)(2,1)S(1)}, bf16[512,1536]{1,0:T(8,128)(2,1)}, u32[]{:S(2)}) copy-start(bf16[512,1536]{1,0:T(8,128)(2,1)} %constant.41.clone.waves) | copy-start | bytes 4718596
  11.9 12.7 %copy-start.8 = (bf16[1024,512]{1,0:T(8,128)(2,1)S(1)}, bf16[1024,512]{1,0:T(8,128)(2,1)}, u32[]{:S(2)}) copy-start(bf16[1024,512]{1,0:T(8,128)(2,1)} %constant.40.clone.along_x) | copy-start | bytes 3145732
  11.9 12.7 %copy-start.9 = (bf16[512,1024]{1,0:T(8,128)(2,1)S(1)}, bf16[512,1024]{1,0:T(8,128)(2,1)}, u32[]{:S(2)}) copy-start(bf16[512,1024]{1,0:T(8,128)(2,1)} %constant.39.clone.spread) | copy-start | bytes 3145732
  11.9 12.7 %copy-start.17 = (bf16[2,24,24]{2,1,0:T(8,128)(2,1)S(1)}, bf16[2,24,24]{2,1,0:T(8,128)(2,1)}, u32[]{:S(2)}) copy-start(bf16[2,24,24]{2,1,0:T(8,128)(2,1)} %constant.38.clone.along_z) | copy-start | bytes 6916
  11.9 12.6 %collective-permute-start.3 = (bf16[4,24,512]{2,1,0:T(8,128)(2,1)S(1)}, bf16[4,24,512]{2,1,0:T(8,128)(2,1)S(1)}, u32[]{:S(2)}, u32[]{:S(2)}) collective-permute-start(bf16[4,24,512]{2,1,0:T(8,128)(2,1)S(1)} %get-tuple-element.33), channel_id=1, source_target_pairs={{0,3},{1,2},{2,1},{3,0},{4,7},{5,6},{6,5},{7,4},{8,11},{9,10},{10,... | collective-permute-start | bytes 294920 | tf_op jit(solution)/shard_map/ppermute | solution.py:465
  17.7 10.0 %collective-permute-start.4 = (bf16[1,96,512]{2,1,0:T(8,128)(2,1)S(1)}, bf16[1,96,512]{2,1,0:T(8,128)(2,1)S(1)}, u32[]{:S(2)}, u32[]{:S(2)}) collective-permute-start(bf16[1,96,512]{2,1,0:T(8,128)(2,1)S(1)} %get-tuple-element.35), channel_id=1, source_target_pairs={{0,4},{4,0},{8,12},{12,8},{16,20},{20,16},{24,28},{28,24},{32,36},... | collective-permute-start | bytes 294920 | tf_op jit(solution)/shard_map/ppermute | solution.py:485
  17.8 11.5 %collective-permute-start.5 = (bf16[1,96,512]{2,1,0:T(8,128)(2,1)S(1)}, bf16[1,96,512]{2,1,0:T(8,128)(2,1)S(1)}, u32[]{:S(2)}, u32[]{:S(2)}) collective-permute-start(bf16[1,96,512]{2,1,0:T(8,128)(2,1)S(1)} %get-tuple-element.36), channel_id=1, source_target_pairs={{0,124},{4,8},{8,4},{12,16},{16,12},{20,24},{24,20},{28,32},{32,28... | collective-permute-start | bytes 294920 | tf_op jit(solution)/shard_map/ppermute | solution.py:486
  24.5 30.3 %slice-start = ((s8[5242880]{0:T(1024)(128)(4,1)}), s8[4194304]{0:T(1024)(128)(4,1)S(1)}, s32[]{:S(2)}) async-start(s8[5242880]{0:T(1024)(128)(4,1)} %bitcast.5), calls=%async_computation.2 | async-start | bytes 8388608
  24.6 30.2 %slice-start.1 = ((s8[5242880]{0:T(1024)(128)(4,1)}), s8[1048576]{0:T(1024)(128)(4,1)S(1)}, s32[]{:S(2)}) async-start(s8[5242880]{0:T(1024)(128)(4,1)} %bitcast.5), calls=%async_computation.3 | async-start | bytes 2097152
  24.6 30.2 %copy-start.4 = (bf16[3072,512]{1,0:T(8,128)(2,1)S(1)}, bf16[3072,512]{1,0:T(8,128)(2,1)}, u32[]{:S(2)}) copy-start(bf16[3072,512]{1,0:T(8,128)(2,1)} %constant.45.clone.inner) | copy-start | bytes 9437188
  27.8 27.0 %copy-start.11 = (bf16[256,1280]{1,0:T(8,128)(2,1)S(1)}, bf16[256,1280]{1,0:T(8,128)(2,1)}, u32[]{:S(2)}) copy-start(bf16[256,1280]{1,0:T(8,128)(2,1)} %constant.43.clone.outer_back) | copy-start | bytes 1966084
  27.8 27.0 %copy-start.13 = (bf16[256,768]{1,0:T(8,128)(2,1)S(1)}, bf16[256,768]{1,0:T(8,128)(2,1)}, u32[]{:S(2)}) copy-start(bf16[256,768]{1,0:T(8,128)(2,1)} %constant.42.clone.outer) | copy-start | bytes 1179652
  54.8 27.6 %copy-start.6 = (bf16[512,1536]{1,0:T(8,128)(2,1)S(1)}, bf16[512,1536]{1,0:T(8,128)(2,1)}, u32[]{:S(2)}) copy-start(bf16[512,1536]{1,0:T(8,128)(2,1)} %constant.47.clone.gather) | copy-start | bytes 4718596
  59.4 23.1 %copy-start.5 = (bf16[1536,512]{1,0:T(8,128)(2,1)S(1)}, bf16[1536,512]{1,0:T(8,128)(2,1)}, u32[]{:S(2)}) copy-start(bf16[1536,512]{1,0:T(8,128)(2,1)} %constant.49.clone.inverse) | copy-start | bytes 4718596
  59.4 23.0 %copy-start.16 = (bf16[256,512]{1,0:T(8,128)(2,1)S(1)}, bf16[256,512]{1,0:T(8,128)(2,1)}, u32[]{:S(2)}) copy-start(bf16[256,512]{1,0:T(8,128)(2,1)} %constant.48.clone.keep) | copy-start | bytes 786436
  59.4 23.0 %copy-start.18 = (f32[2,1,128]{2,1,0:T(1,128)S(1)}, f32[2,1,128]{2,1,0:T(1,128)}, u32[]{:S(2)}) copy-start(f32[2,1,128]{2,1,0:T(1,128)} %constant.50.clone.symbol) | copy-start | bytes 3076

commit v6 on v5

--- a/solution.py
+++ b/solution.py
@@ -186,7 +186,7 @@
 
 
 def local_kernel(
-    metric, strain, wave_x, state, along, waves, partial, partial_heat, carrier_y, carrier_z, factors
+    metric, strain, wave_x, state, along, waves, partial, partial_heat, carrier_y, carrier_z, carrier_second, factors
 ):
     along_x, along_y = along[:NX], along[NX:, :CELLS]
     speeds = [state[q].astype(F32) for q in range(4)]
@@ -196,6 +196,13 @@
     ]
     scale = -STEP / 60.0
     carrier_y[...] = scale * contra[1]
+    row = lax.broadcasted_iota(jnp.int32, (96, CELLS), 0)
+    column = lax.broadcasted_iota(jnp.int32, (96, CELLS), 1)
+    third = (row * 171) >> 9
+    source = BY * third + (row - 3 * third) + (BY - 3) * _odd("gy")
+    pick = jnp.where(column == source, 1.0, 0.0).astype(BF16)
+    high, middle, low = _split(scale * contra[1], 3)
+    carrier_second[...] = (_dot(pick, low) + _dot(pick, middle)) + _dot(pick, high)
     carrier_z[0:24] = scale * contra[2][0:24]
     carrier_z[24:48] = scale * contra[2][CELLS - 24 :]
     nothing = jnp.zeros((24, NX), F32)
@@ -236,56 +243,48 @@
         )
 
 
-def _complete(partial, carrier_y, carrier_z, y_first, y_second, z_first, z_second, along_y, along_z):
-    odd_y, odd_z = _odd("gy"), _odd("gz")
-    beside = jnp.concatenate([y_first, y_second], axis=0)
-    whole = partial + carrier_y[...] * _dot(along_y[odd_y], beside)
-    first, second = _dot(along_z[odd_z], z_first), _dot(along_z[1 - odd_z], z_second)
-    below = jnp.where(odd_z == 1, first, second)
-    above = jnp.where(odd_z == 1, second, first)
+def _with_z(whole, carrier_z, z_first, z_second, along_z):
+    odd = _odd("gz")
+    first, second = _dot(along_z[odd], z_first), _dot(along_z[1 - odd], z_second)
+    below = jnp.where(odd == 1, first, second)
+    above = jnp.where(odd == 1, second, first)
     low = whole[:24] + carrier_z[0:24] * below
     high = whole[CELLS - 24 :] + carrier_z[24:48] * above
     return jnp.concatenate([low, whole[24 : CELLS - 24], high], axis=0)
 
 
-def forward_kernel(
+def _flux(metric, fields):
+    return [
+        metric[0, j] * fields[0] + metric[1, j] * fields[1] + metric[2, j] * fields[2]
+        for j in range(3)
+    ]
+
+
+def early_kernel(
     metric,
     partial,
     carrier_y,
     carrier_z,
     y_first,
-    y_second,
     z_first,
-    z_second,
-    along_y,
+    along_first,
     along_z,
     spread,
     along_x,
     waves,
     provisional,
-    sent,
+    spectrum,
 ):
-    fields = [
-        _complete(
-            partial[q],
-            carrier_y,
-            carrier_z,
-            y_first[q],
-            y_second[q],
-            z_first[q],
-            z_second[q],
-            along_y,
-            along_z,
-        )
-        for q in range(3)
-    ]
+    odd, odd_z = _odd("gy"), _odd("gz")
+    fields = []
     for q in range(3):
+        whole = partial[q] + carrier_y[...] * _dot(along_first[odd], y_first[q])
+        first = _dot(along_z[odd_z], z_first[q])
+        low = whole[:24] + carrier_z[0:24] * jnp.where(odd_z == 1, first, 0.0)
+        high = whole[CELLS - 24 :] + carrier_z[24:48] * jnp.where(odd_z == 1, 0.0, first)
+        fields.append(jnp.concatenate([low, whole[24 : CELLS - 24], high], axis=0))
         provisional[q] = fields[q]
-    flux = [
-        metric[0, j] * fields[0] + metric[1, j] * fields[1] + metric[2, j] * fields[2]
-        for j in range(3)
-    ]
-    flux = [_split(f, 2) for f in flux]
+    flux = [_split(f, 2) for f in _flux(metric, fields)]
     stacked = [jnp.concatenate(flux[j], axis=0) for j in (1, 2)]
     own = _dot(jnp.concatenate(flux[0], axis=1), along_x[...])
     for part in range(EXT // CELLS):
@@ -296,10 +295,56 @@
             beside_z = _dot(spread[CELLS + 192 :, NX:], stacked[1])
             block = jnp.concatenate([beside_y, beside_z], axis=0)
         high, low = _split(block, 2)
-        spectrum = _dot_nt(waves[...], jnp.concatenate([high, high, low], axis=1))
-        for t in range(CELLS // 128):
-            at = 4 * (part * (CELLS // 128) + t)
-            sent[:, at : at + 4, :] = spectrum[:, 128 * t : 128 * t + 128].reshape(DEV, 4, 128)
+        spectrum[:, part * CELLS : (part + 1) * CELLS] = _dot_nt(
+            waves[...], jnp.concatenate([high, high, low], axis=1)
+        )
+
+
+def forward_kernel(
+    metric,
+    partial,
+    spectrum,
+    carrier_y,
+    carrier_z,
+    carrier_second,
+    y_second,
+    z_second,
+    along_second,
+    along_rows,
+    along_z,
+    spread_rows,
+    along_x,
+    waves,
+    provisional,
+    sent,
+):
+    odd, odd_z = _odd("gy"), _odd("gz")
+    carrier = jnp.where(odd_z == 1, carrier_z[24:48], carrier_z[0:24])
+    nothing = jnp.zeros((8, NX), F32)
+    fields = []
+    for q in range(3):
+        layers = carrier * _dot(along_z[1 - odd_z], z_second[q])
+        whole = partial[q] + carrier_y[...] * _dot(along_second[odd], y_second[q])
+        low = whole[:24] + jnp.where(odd_z == 1, 0.0, layers)
+        high = whole[CELLS - 24 :] + jnp.where(odd_z == 1, layers, 0.0)
+        provisional[q] = jnp.concatenate([low, whole[24 : CELLS - 24], high], axis=0)
+        rows = carrier_second[...] * _dot(along_rows[odd], y_second[q])
+        fields.append(jnp.concatenate([rows, layers, nothing], axis=0))
+    flux = [_split(f, 2) for f in _flux(metric, fields)]
+    slope = _split(_dot(jnp.concatenate(flux[0], axis=1), along_x[...]), 2)
+    high, low = (
+        jnp.concatenate([flux[1][i], flux[2][i], slope[i]], axis=0) for i in range(2)
+    )
+    rows = _dot_nt(jnp.concatenate([high, high, low], axis=1), waves[...])
+    more = lax.dot_general(
+        jnp.concatenate(_split(rows, 2), axis=0),
+        spread_rows[2 * odd + odd_z],
+        (((0,), (0,)), ((), ())),
+        preferred_element_type=F32,
+    )
+    for t in range(EXT // 128):
+        at = slice(128 * t, 128 * t + 128)
+        sent[:, 4 * t : 4 * t + 4, :] = (spectrum[:, at] + more[:, at]).reshape(DEV, 4, 128)
 
 
 def plane_kernel(factors, got, outer, outer_back, twist, inner, inner_back, sent):
@@ -364,7 +409,8 @@
     y_second,
     z_first,
     z_second,
-    along_y,
+    along_first,
+    along_second,
     along_z,
     motion,
     heat,
@@ -372,16 +418,10 @@
     held_heat,
     done,
 ):
-    held_heat[...] = _complete(
-        partial[...],
-        carrier_y,
-        carrier_z,
-        y_first[0],
-        y_second[0],
-        z_first[3],
-        z_second[3],
-        along_y,
-        along_z,
+    odd = _odd("gy")
+    slopes = _dot(along_first[odd], y_first[0]) + _dot(along_second[odd], y_second[0])
+    held_heat[...] = _with_z(
+        partial[...] + carrier_y[...] * slopes, carrier_z, z_first[3], z_second[3], along_z
     )
     copies = [pltpu.make_async_copy(held_heat, heat, done.at[3])]
     copies[0].start()
@@ -431,9 +471,19 @@
     keep = _exact(np.concatenate([np.eye(CELLS)] * 2, axis=1))
     gather = np.concatenate([gather] * 3, axis=1)
     below, above = along_y[:, CELLS : CELLS + 96], along_y[:, CELLS + 96 : CELLS + 192]
-    beside_y = _exact(
-        np.stack([np.concatenate([above, below], axis=1), np.concatenate([below, above], axis=1)])
-    )
+    beside_first = _exact(np.stack([above, below]))
+    beside_second = _exact(np.stack([below, above]))
+    rows = [[BY * w + y + i for w in range(BZ) for y in range(3)] for i in (0, BY - 3)]
+    beside_rows = np.stack([beside_second[i][rows[i]] for i in range(2)])
+    layers = [list(range(24)), list(range(CELLS - 24, CELLS))]
+    spread_rows = []
+    for i in range(4):
+        chosen = rows[i // 2] + layers[i % 2]
+        part = np.zeros((3, 128, EXT))
+        for j, table in enumerate((-along_y, -along_z, np.eye(CELLS, EXT))):
+            part[j, : len(chosen)] = table[chosen]
+        spread_rows.append(np.concatenate([part.reshape(384, EXT)] * 2, axis=0))
+    spread_rows = _exact(np.stack(spread_rows))
     beside_z = _exact(
         np.stack([along_z[CELLS - 24 :, CELLS + 216 : CELLS + 240], along_z[:24, CELLS + 192 : CELLS + 216]])
     )
@@ -463,13 +513,14 @@
     y_second = lax.ppermute(y_second, "gy", swaps_y[1])
     z_first = lax.ppermute(z_first, "gz", swaps_z[0])
     z_second = lax.ppermute(z_second, "gz", swaps_z[1])
-    partial, partial_heat, carrier_y, carrier_z, factors = _call(
+    partial, partial_heat, carrier_y, carrier_z, carrier_second, factors = _call(
         local_kernel,
         (
             fields(3),
             field,
             field,
             jax.ShapeDtypeStruct((48, NX), F32),
+            jax.ShapeDtypeStruct((96, NX), F32),
             jax.ShapeDtypeStruct((2, DEV, CELLS), F32),
         ),
         [SMEM, SMEM, SMEM, VMEM, VMEM, VMEM],
@@ -484,28 +535,52 @@
     )
     y_first_heat = lax.ppermute(y_first_heat, "gy", swaps_y[0])
     y_second_heat = lax.ppermute(y_second_heat, "gy", swaps_y[1])
-    provisional, sent = _call(
-        forward_kernel,
-        (fields(3), block),
-        [SMEM] + [VMEM] * 12,
-        "forward",
-        2_000_000_000,
+    circulant = np.concatenate([circulant, circulant], axis=0)
+    forward = np.concatenate(_pieces(forward, 2)[[0, 1, 0]], axis=1)
+    early, spectrum = _call(
+        early_kernel,
+        (fields(3), jax.ShapeDtypeStruct((NX, EXT), F32)),
+        [SMEM] + [VMEM] * 10,
+        "early",
+        3_000_000_000,
         8 * MIB,
-        40,
+        20,
     )(
         metric,
         partial,
         carrier_y,
         carrier_z,
         y_first,
-        y_second,
         z_first,
-        z_second,
-        beside_y,
+        beside_first,
         beside_z,
         spread,
-        np.concatenate([circulant, circulant], axis=0),
-        np.concatenate(_pieces(forward, 2)[[0, 1, 0]], axis=1),
+        circulant,
+        forward,
+    )
+    provisional, sent = _call(
+        forward_kernel,
+        (fields(3), block),
+        [SMEM] + [VMEM] * 13,
+        "forward",
+        2_000_000_000,
+        8 * MIB,
+        20,
+    )(
+        metric,
+        early,
+        spectrum,
+        carrier_y,
+        carrier_z,
+        carrier_second,
+        y_second,
+        z_second,
+        beside_second,
+        beside_rows,
+        beside_z,
+        spread_rows,
+        circulant,
+        forward,
     )
     sent, y_first_heat, y_second_heat = lax.optimization_barrier(
         (sent, y_first_heat, y_second_heat)
@@ -526,7 +601,7 @@
     motion, heat = _call(
         project_kernel,
         (fields(3), field),
-        [SMEM] + [VMEM] * 15,
+        [SMEM] + [VMEM] * 16,
         "project",
         2_500_000_000,
         8 * MIB,
@@ -552,7 +627,8 @@
         y_second_heat,
         z_first,
         z_second,
-        beside_y,
+        beside_first,
+        beside_second,
         beside_z,
     )
     return motion.reshape(3, BZ, BY, NX), heat.reshape(BZ, BY, NX)

time: 87.2 us -> 87.1 us (level)
  Pallas kernels: 15.6 us -> 18.2 us
  waiting for transfers between devices: 7 us -> 4.88 us
    ppermute x1, waiting for transfers between devices: 5.38 us -> 0.01 us  [_step(): z_second = lax.ppermute(z_second, 'gz', swaps_z[1])]
    ppermute x1, waiting for transfers between devices: 0.01 us -> 3.68 us  [_step(): y_second = lax.ppermute(y_second, 'gy', swaps_y[1])]
    pallas_call x2 -> x3, Pallas kernels: 7.48 us -> 9.95 us  [the longest x1 4.35 us: _step(): _call(project_kernel, (fields(3), field), [SMEM] + [VMEM] * 16, 'project'...]
  transfers between devices with their start and end apart: 6 -> 6, of which waited for: 2 -> 2; matrix products, arithmetic and copies ran while one was open for 0% -> 0% of each run, Pallas kernels for 7% -> 10%
where the time goes in v6:
time: 87.1 us; the launch traced here: 86.9 us
  blocking collectives  48.4 us (56%)
  Pallas kernels  18.2 us (21%)
  starting transfers between devices  13 us (15%)
  waiting for transfers between devices  4.88 us (6%)
  local copies, waits for them, and re-layouts  1.35 us (2%)
  between operations  1.1 us (1%)
    all_to_all x2, blocking collectives, _step(): lax.all_to_all(sent, ('gy', 'gz'), split_axis=0, concat_axis=0, tiled=True)  48.4 us
    ppermute x1, starting transfers between devices, _step(): y_second = lax.ppermute(y_second, 'gy', swaps_y[1])  5.95 us
    pallas_call x1, Pallas kernels, _step(): _call(plane_kernel, block, [VMEM] * 7, 'plane', 3600000000, 8 * MIB, 40)  4.48 us
    pallas_call x1, Pallas kernels, _step(): _call(project_kernel, (fields(3), field), [SMEM] + [VMEM] * 16, 'project'...  4.35 us
    ppermute x1, waiting for transfers between devices, _step(): y_second = lax.ppermute(y_second, 'gy', swaps_y[1])  3.68 us
    pallas_call x1, Pallas kernels, _step(): _call(local_kernel, (fields(3), field, field, jax.ShapeDtypeStruct((48, N...  3.34 us
    pallas_call x1, Pallas kernels, _step(): _call(early_kernel, (fields(3), jax.ShapeDtypeStruct((NX, EXT), F32)), [S...  2.96 us
    pallas_call x1, Pallas kernels, _step(): _call(forward_kernel, (fields(3), block), [SMEM] + [VMEM] * 13, 'forward'...  2.64 us
  transfers between devices with their start and end apart: 6, of which 2 were waited for; matrix products, arithmetic and copies ran while one was open for 0% of the time, Pallas kernels for 10%

profile of v6, /device:TPU:1, one launch (start us, length us, event | category | flops | bytes accessed | tf_op | source)
XLA Modules:
  0.0 86.9 jit_solution(8179617186291609717)
XLA Ops:
  0.6 0.0 copy-start.7
  0.6 1.2 %copy-done.7 = bf16[4,32,8,512]{3,2,1,0:T(8,128)(2,1)S(1)} copy-done((bf16[4,32,8,512]{3,2,1,0:T(8,128)(2,1)S(1)}, bf16[4,32,8,512]{3,2,1,0:T(8,128)(2,1)}, u32[]{:S(2)}) %copy-start.7) | copy-done | bytes 1048600
  1.9 0.0 copy-start.6
  1.9 0.0 copy-start.8
  1.9 0.0 copy-start.9
  1.9 0.0 copy-start.18
  1.9 0.0 copy-start.22
  1.9 0.0 copy-start.20
  1.9 0.4 edges.1
  2.3 2.1 %collective-permute-start = (bf16[3,96,512]{2,1,0:T(8,128)(2,1)S(1)}, bf16[3,96,512]{2,1,0:T(8,128)(2,1)S(1)}, u32[]{:S(2)}, u32[]{:S(2)}) collective-permute-start(bf16[3,96,512]{2,1,0:T(8,128)(2,1)S(1)} %get-tuple-element.33), channel_id=1, source_target_pairs={{0,4},{4,0},{8,12},{12,8},{16,20},{20,16},{24,28},{28,24},{32,36},... | collective-permute-start | bytes 884744 | tf_op jit(solution)/shard_map/ppermute | solution.py:512
  4.5 1.0 %collective-permute-start.1 = (bf16[4,24,512]{2,1,0:T(8,128)(2,1)S(1)}, bf16[4,24,512]{2,1,0:T(8,128)(2,1)S(1)}, u32[]{:S(2)}, u32[]{:S(2)}) collective-permute-start(bf16[4,24,512]{2,1,0:T(8,128)(2,1)S(1)} %get-tuple-element.34), channel_id=1, source_target_pairs={{0,1},{1,0},{2,3},{3,2},{4,5},{5,4},{6,7},{7,6},{8,9},{9,8},{10,11... | collective-permute-start | bytes 294920 | tf_op jit(solution)/shard_map/ppermute | solution.py:514
  5.4 2.3 %collective-permute-start.3 = (bf16[4,24,512]{2,1,0:T(8,128)(2,1)S(1)}, bf16[4,24,512]{2,1,0:T(8,128)(2,1)S(1)}, u32[]{:S(2)}, u32[]{:S(2)}) collective-permute-start(bf16[4,24,512]{2,1,0:T(8,128)(2,1)S(1)} %get-tuple-element.39), channel_id=1, source_target_pairs={{0,3},{1,2},{2,1},{3,0},{4,7},{5,6},{6,5},{7,4},{8,11},{9,10},{10,... | collective-permute-start | bytes 294920 | tf_op jit(solution)/shard_map/ppermute | solution.py:515
  7.8 5.9 %collective-permute-start.2 = (bf16[3,96,512]{2,1,0:T(8,128)(2,1)S(1)}, bf16[3,96,512]{2,1,0:T(8,128)(2,1)S(1)}, u32[]{:S(2)}, u32[]{:S(2)}) collective-permute-start(bf16[3,96,512]{2,1,0:T(8,128)(2,1)S(1)} %get-tuple-element.38), channel_id=1, source_target_pairs={{0,124},{4,8},{8,4},{12,16},{16,12},{20,24},{24,20},{28,32},{32,28... | collective-permute-start | bytes 884744 | tf_op jit(solution)/shard_map/ppermute | solution.py:513
  13.7 0.0 copy-done.6
  13.7 0.0 copy-done.8
  13.7 0.0 copy-done.9
  13.7 0.0 copy-done.14
  13.7 0.0 copy-done.18
  13.7 0.0 copy-done.22
  13.7 3.3 %local.1 = (f32[3,256,512]{2,1,0:T(8,128)S(1)}, f32[256,512]{1,0:T(8,128)S(1)}, f32[256,512]{1,0:T(8,128)S(1)}, f32[48,512]{1,0:T(8,128)S(1)}, f32[96,512]{1,0:T(8,128)S(1)}, /*index=5*/f32[2,128,256]{2,1,0:T(8,128)S(1)}) custom-call(f32[3,3]{1,0:T(4,128)S(1)} %copy-done.6, f32[3,3]{1,0:T(4,128)S(1)} %copy-done.9, f32[256]{0:T(256)S(1)} %copy-done.22, ...), custom_call_target="tpu_custom_call" | custom-call | flops 1000000000 | bytes 4194304 | tf_op jit(solution)/shard_map/local/pallas_call | solution.py:516
  17.1 0.1 collective-permute-start.4
  17.2 0.0 collective-permute-done.1.z_first
  17.2 1.5 %collective-permute-start.5 = (bf16[1,96,512]{2,1,0:T(8,128)(2,1)S(1)}, bf16[1,96,512]{2,1,0:T(8,128)(2,1)S(1)}, u32[]{:S(2)}, u32[]{:S(2)}) collective-permute-start(bf16[1,96,512]{2,1,0:T(8,128)(2,1)S(1)} %get-tuple-element.42), channel_id=1, source_target_pairs={{0,124},{4,8},{8,4},{12,16},{16,12},{20,24},{24,20},{28,32},{32,28... | collective-permute-start | bytes 294920 | tf_op jit(solution)/shard_map/ppermute | solution.py:537
  18.7 0.0 collective-permute-done.y_first
  18.7 0.0 copy-done.20
  18.7 0.0 copy-done.1
  18.7 0.0 copy-done.2
  18.8 0.0 copy-done.5
  18.8 0.0 copy-done.13
  18.8 0.0 copy-start
  18.8 0.0 copy-start.3
  18.8 0.0 copy-start.4
  18.8 3.0 %early.1 = (f32[3,256,512]{2,1,0:T(8,128)S(1)}, f32[512,512]{1,0:T(8,128)S(1)}) custom-call(f32[3,3]{1,0:T(4,128)S(1)} %copy-done.6, f32[3,256,512]{2,1,0:T(8,128)S(1)} %get-tuple-element.27.partial, f32[256,512]{1,0:T(8,128)S(1)} %get-tuple-element.28.carrier_y, f32[48,512]{1,0:T(8,128)S(1)} %get-tuple-element.32.carrier_z, ...), custom_call_target="tpu_custom_call" | custom-call | flops 3000000000 | bytes 8388608 | tf_op jit(solution)/shard_map/early/pallas_call | solution.py:540
  21.8 0.0 collective-permute-done.3.z_second
  21.8 3.7 %collective-permute-done.2.y_second = bf16[3,96,512]{2,1,0:T(8,128)(2,1)S(1)} collective-permute-done((bf16[3,96,512]{2,1,0:T(8,128)(2,1)S(1)}, bf16[3,96,512]{2,1,0:T(8,128)(2,1)S(1)}, u32[]{:S(2)}, u32[]{:S(2)}) %collective-permute-start.2) | collective-permute-done | bytes 294944 | tf_op jit(solution)/shard_map/ppermute | solution.py:513
  25.5 0.0 copy-done
  25.5 0.0 copy-done.3
  25.5 0.0 copy-done.4
  25.5 0.0 slice-start.1
  25.5 0.0 copy-start.10
  25.5 2.6 %forward.1 = (f32[3,256,512]{2,1,0:T(8,128)S(1)}, f32[128,16,128]{2,1,0:T(8,128)S(1)}) custom-call(f32[3,3]{1,0:T(4,128)S(1)} %copy-done.6, f32[3,256,512]{2,1,0:T(8,128)S(1)} %get-tuple-element.35.partial, f32[512,512]{1,0:T(8,128)S(1)} %get-tuple-element.36.spectrum, f32[256,512]{1,0:T(8,128)S(1)} %get-tuple-element.28.carrier_y, ...), custom_call_target="tpu_custom_call" | custom-call | flops 2000000000 | bytes 8388608 | tf_op jit(solution)/shard_map/forward/pallas_call | solution.py:561
  28.1 0.0 copy-start.15
  28.2 0.0 copy-start.16
  28.2 0.0 copy-start.17
  28.2 0.0 collective-permute-done.4.y_first
  28.2 1.2 %collective-permute-done.5.y_second = bf16[1,96,512]{2,1,0:T(8,128)(2,1)S(1)} collective-permute-done((bf16[1,96,512]{2,1,0:T(8,128)(2,1)S(1)}, bf16[1,96,512]{2,1,0:T(8,128)(2,1)S(1)}, u32[]{:S(2)}, u32[]{:S(2)}) %collective-permute-start.5) | collective-permute-done | bytes 98336 | tf_op jit(solution)/shard_map/ppermute | solution.py:537
  29.4 25.4 %all_to_all.10.got = f32[128,16,128]{2,1,0:T(8,128)S(1)} all-to-all(f32[128,16,128]{2,1,0:T(8,128)S(1)} %get-tuple-element.43), channel_id=1, replica_groups=mesh['gy'=32,'gz'=4] {'gy','gz'}, dimensions={0} | all-to-all | bytes 2097152 | tf_op jit(solution)/shard_map/all_to_all | solution.py:588
  54.8 0.0 slice-done
  54.8 0.0 slice-done.1
  54.8 0.0 copy-done.10
  54.8 0.0 copy-done.15
  54.8 0.0 copy-done.16
  54.8 0.0 copy-done.17
  54.8 0.0 copy-start.12
  54.8 4.5 %plane.1 = f32[128,16,128]{2,1,0:T(8,128)S(1)} custom-call(f32[2,128,256]{2,1,0:T(8,128)S(1)} %get-tuple-element.26.factors, f32[128,16,128]{2,1,0:T(8,128)S(1)} %all_to_all.10.got, bf16[256,768]{1,0:T(8,128)(2,1)S(1)} %copy-done.17, bf16[256,1280]{1,0:T(8,128)(2,1)S(1)} %copy-done.15, f32[2,128,512]{2,1,0:T(8,128)S(1)} %copy-done.16, ...), custom_call_target="tpu_custom_call" | custom-call | flops 3600000000 | bytes 8388608 | tf_op jit(solution)/shard_map/plane/pallas_call | solution.py:589
  59.3 0.0 copy-start.11
  59.3 0.0 copy-start.19
  59.3 0.0 copy-start.21
  59.4 23.0 %all_to_all.11.got = f32[128,16,128]{2,1,0:T(8,128)S(1)} all-to-all(f32[128,16,128]{2,1,0:T(8,128)S(1)} %plane.1), channel_id=1, replica_groups=mesh['gy'=32,'gz'=4] {'gy','gz'}, dimensions={0} | all-to-all | bytes 2097152 | tf_op jit(solution)/shard_map/all_to_all | solution.py:600
  82.4 0.0 copy-done.12
  82.4 0.0 copy-done.11
  82.4 0.0 copy-done.19
  82.4 0.0 copy-done.21
  82.4 4.4 %project.1 = (f32[3,256,512]{2,1,0:T(8,128)}, f32[256,512]{1,0:T(8,128)}) custom-call(f32[3,3]{1,0:T(4,128)S(1)} %copy-done.6, f32[128,16,128]{2,1,0:T(8,128)S(1)} %all_to_all.11.got, bf16[512,1536]{1,0:T(8,128)(2,1)S(1)} %copy-done.12, bf16[256,512]{1,0:T(8,128)(2,1)S(1)} %copy-done.19, bf16[1536,512]{1,0:T(8,128)(2,1)S(1)} %copy-done.11, ...), custom_call_target="tpu_custom_call" | custom-call | flops 2500000000 | bytes 8388608 | tf_op jit(solution)/shard_map/project/pallas_call | solution.py:601
  (7 shorter events, 0.0 us)
Async XLA Ops:
  0.6 1.2 %copy-start.7 = (bf16[4,32,8,512]{3,2,1,0:T(8,128)(2,1)S(1)}, bf16[4,32,8,512]{3,2,1,0:T(8,128)(2,1)}, u32[]{:S(2)}) copy-start(bf16[4,32,8,512]{3,2,1,0:T(8,128)(2,1)} %param.23) | copy-start | bytes 3145732
  1.9 11.9 %copy-start.6 = (f32[3,3]{1,0:T(4,128)S(1)}, f32[3,3]{1,0:T(4,128)}, u32[]{:S(2)}) copy-start(f32[3,3]{1,0:T(4,128)} %metric.7) | copy-start | bytes 112
  1.9 11.9 %copy-start.8 = (bf16[4,32,8,512]{3,2,1,0:T(8,128)(2,1)S(1)}, bf16[4,32,8,512]{3,2,1,0:T(8,128)(2,1)}, u32[]{:S(2)}) copy-start(bf16[4,32,8,512]{3,2,1,0:T(8,128)(2,1)} %param.23) | copy-start | bytes 3145732
  1.9 11.9 %copy-start.9 = (f32[3,3]{1,0:T(4,128)S(1)}, f32[3,3]{1,0:T(4,128)}, u32[]{:S(2)}) copy-start(f32[3,3]{1,0:T(4,128)} %strain.1) | copy-start | bytes 112
  1.9 11.9 %copy-start.14 = (bf16[768,512]{1,0:T(8,128)(2,1)S(1)}, bf16[768,512]{1,0:T(8,128)(2,1)}, u32[]{:S(2)}) copy-start(bf16[768,512]{1,0:T(8,128)(2,1)} %constant.41.clone.along) | copy-start | bytes 2359300
  1.9 11.9 %copy-start.18 = (f32[3,128,256]{2,1,0:T(8,128)S(1)}, f32[3,128,256]{2,1,0:T(8,128)}, u32[]{:S(2)}) copy-start(f32[3,128,256]{2,1,0:T(8,128)} %constant.42.clone.waves) | copy-start | bytes 1179652
  1.9 11.8 %copy-start.22 = (f32[256]{0:T(256)S(1)}, f32[256]{0:T(256)}, u32[]{:S(2)}) copy-start(f32[256]{0:T(256)} %constant.40.clone.wave_x) | copy-start | bytes 3076
  1.9 16.8 %copy-start.20 = (bf16[2,256,96]{2,1,0:T(8,128)(2,1)S(1)}, bf16[2,256,96]{2,1,0:T(8,128)(2,1)}, u32[]{:S(2)}) copy-start(bf16[2,256,96]{2,1,0:T(8,128)(2,1)} %constant.43.clone.along_first) | copy-start | bytes 294916
  2.3 16.4 %collective-permute-start = (bf16[3,96,512]{2,1,0:T(8,128)(2,1)S(1)}, bf16[3,96,512]{2,1,0:T(8,128)(2,1)S(1)}, u32[]{:S(2)}, u32[]{:S(2)}) collective-permute-start(bf16[3,96,512]{2,1,0:T(8,128)(2,1)S(1)} %get-tuple-element.33), channel_id=1, source_target_pairs={{0,4},{4,0},{8,12},{12,8},{16,20},{20,16},{24,28},{28,24},{32,36},... | collective-permute-start | bytes 884744 | tf_op jit(solution)/shard_map/ppermute | solution.py:512
  4.5 12.7 %collective-permute-start.1 = (bf16[4,24,512]{2,1,0:T(8,128)(2,1)S(1)}, bf16[4,24,512]{2,1,0:T(8,128)(2,1)S(1)}, u32[]{:S(2)}, u32[]{:S(2)}) collective-permute-start(bf16[4,24,512]{2,1,0:T(8,128)(2,1)S(1)} %get-tuple-element.34), channel_id=1, source_target_pairs={{0,1},{1,0},{2,3},{3,2},{4,5},{5,4},{6,7},{7,6},{8,9},{9,8},{10,11... | collective-permute-start | bytes 294920 | tf_op jit(solution)/shard_map/ppermute | solution.py:514
  5.4 16.4 %collective-permute-start.3 = (bf16[4,24,512]{2,1,0:T(8,128)(2,1)S(1)}, bf16[4,24,512]{2,1,0:T(8,128)(2,1)S(1)}, u32[]{:S(2)}, u32[]{:S(2)}) collective-permute-start(bf16[4,24,512]{2,1,0:T(8,128)(2,1)S(1)} %get-tuple-element.39), channel_id=1, source_target_pairs={{0,3},{1,2},{2,1},{3,0},{4,7},{5,6},{6,5},{7,4},{8,11},{9,10},{10,... | collective-permute-start | bytes 294920 | tf_op jit(solution)/shard_map/ppermute | solution.py:515
  7.7 11.0 %copy-start.1 = (bf16[512,1536]{1,0:T(8,128)(2,1)S(1)}, bf16[512,1536]{1,0:T(8,128)(2,1)}, u32[]{:S(2)}) copy-start(bf16[512,1536]{1,0:T(8,128)(2,1)} %constant.47.clone.waves) | copy-start | bytes 4718596
  7.7 11.0 %copy-start.2 = (bf16[1024,512]{1,0:T(8,128)(2,1)S(1)}, bf16[1024,512]{1,0:T(8,128)(2,1)}, u32[]{:S(2)}) copy-start(bf16[1024,512]{1,0:T(8,128)(2,1)} %constant.46.clone.along_x) | copy-start | bytes 3145732
  7.8 11.0 %copy-start.5 = (bf16[2,24,24]{2,1,0:T(8,128)(2,1)S(1)}, bf16[2,24,24]{2,1,0:T(8,128)(2,1)}, u32[]{:S(2)}) copy-start(bf16[2,24,24]{2,1,0:T(8,128)(2,1)} %constant.44.clone.along_z) | copy-start | bytes 6916
  7.8 11.0 %copy-start.13 = (bf16[512,1024]{1,0:T(8,128)(2,1)S(1)}, bf16[512,1024]{1,0:T(8,128)(2,1)}, u32[]{:S(2)}) copy-start(bf16[512,1024]{1,0:T(8,128)(2,1)} %constant.45.clone.spread) | copy-start | bytes 3145732
  7.8 17.7 %collective-permute-start.2 = (bf16[3,96,512]{2,1,0:T(8,128)(2,1)S(1)}, bf16[3,96,512]{2,1,0:T(8,128)(2,1)S(1)}, u32[]{:S(2)}, u32[]{:S(2)}) collective-permute-start(bf16[3,96,512]{2,1,0:T(8,128)(2,1)S(1)} %get-tuple-element.38), channel_id=1, source_target_pairs={{0,124},{4,8},{8,4},{12,16},{16,12},{20,24},{24,20},{28,32},{32,28... | collective-permute-start | bytes 884744 | tf_op jit(solution)/shard_map/ppermute | solution.py:513
  17.1 11.1 %collective-permute-start.4 = (bf16[1,96,512]{2,1,0:T(8,128)(2,1)S(1)}, bf16[1,96,512]{2,1,0:T(8,128)(2,1)S(1)}, u32[]{:S(2)}, u32[]{:S(2)}) collective-permute-start(bf16[1,96,512]{2,1,0:T(8,128)(2,1)S(1)} %get-tuple-element.41), channel_id=1, source_target_pairs={{0,4},{4,0},{8,12},{12,8},{16,20},{20,16},{24,28},{28,24},{32,36},... | collective-permute-start | bytes 294920 | tf_op jit(solution)/shard_map/ppermute | solution.py:536
  17.2 12.2 %collective-permute-start.5 = (bf16[1,96,512]{2,1,0:T(8,128)(2,1)S(1)}, bf16[1,96,512]{2,1,0:T(8,128)(2,1)S(1)}, u32[]{:S(2)}, u32[]{:S(2)}) collective-permute-start(bf16[1,96,512]{2,1,0:T(8,128)(2,1)S(1)} %get-tuple-element.42), channel_id=1, source_target_pairs={{0,124},{4,8},{8,4},{12,16},{16,12},{20,24},{24,20},{28,32},{32,28... | collective-permute-start | bytes 294920 | tf_op jit(solution)/shard_map/ppermute | solution.py:537
  18.8 6.7 %copy-start = (bf16[4,768,512]{2,1,0:T(8,128)(2,1)S(1)}, bf16[4,768,512]{2,1,0:T(8,128)(2,1)}, u32[]{:S(2)}) copy-start(bf16[4,768,512]{2,1,0:T(8,128)(2,1)} %constant.50.clone.spread_rows) | copy-start | bytes 9437188
  18.8 6.7 %copy-start.3 = (bf16[2,256,96]{2,1,0:T(8,128)(2,1)S(1)}, bf16[2,256,96]{2,1,0:T(8,128)(2,1)}, u32[]{:S(2)}) copy-start(bf16[2,256,96]{2,1,0:T(8,128)(2,1)} %constant.48.clone.along_second) | copy-start | bytes 294916
  18.8 6.7 %copy-start.4 = (bf16[2,96,96]{2,1,0:T(8,128)(2,1)S(1)}, bf16[2,96,96]{2,1,0:T(8,128)(2,1)}, u32[]{:S(2)}) copy-start(bf16[2,96,96]{2,1,0:T(8,128)(2,1)} %constant.49.clone.along_rows) | copy-start | bytes 110596
  25.5 29.3 %slice-start = ((s8[5242880]{0:T(1024)(128)(4,1)}), s8[4194304]{0:T(1024)(128)(4,1)S(1)}, s32[]{:S(2)}) async-start(s8[5242880]{0:T(1024)(128)(4,1)} %bitcast.5), calls=%async_computation.2 | async-start | bytes 8388608
  25.5 29.3 %slice-start.1 = ((s8[5242880]{0:T(1024)(128)(4,1)}), s8[1048576]{0:T(1024)(128)(4,1)S(1)}, s32[]{:S(2)}) async-start(s8[5242880]{0:T(1024)(128)(4,1)} %bitcast.5), calls=%async_computation.3 | async-start | bytes 2097152
  25.5 29.3 %copy-start.10 = (bf16[3072,512]{1,0:T(8,128)(2,1)S(1)}, bf16[3072,512]{1,0:T(8,128)(2,1)}, u32[]{:S(2)}) copy-start(bf16[3072,512]{1,0:T(8,128)(2,1)} %constant.54.clone.inner) | copy-start | bytes 9437188
  28.1 26.6 %copy-start.15 = (bf16[256,1280]{1,0:T(8,128)(2,1)S(1)}, bf16[256,1280]{1,0:T(8,128)(2,1)}, u32[]{:S(2)}) copy-start(bf16[256,1280]{1,0:T(8,128)(2,1)} %constant.52.clone.outer_back) | copy-start | bytes 1966084
  28.2 26.6 %copy-start.16 = (f32[2,128,512]{2,1,0:T(8,128)S(1)}, f32[2,128,512]{2,1,0:T(8,128)}, u32[]{:S(2)}) copy-start(f32[2,128,512]{2,1,0:T(8,128)} %constant.53.clone.twist) | copy-start | bytes 1572868
  28.2 26.6 %copy-start.17 = (bf16[256,768]{1,0:T(8,128)(2,1)S(1)}, bf16[256,768]{1,0:T(8,128)(2,1)}, u32[]{:S(2)}) copy-start(bf16[256,768]{1,0:T(8,128)(2,1)} %constant.51.clone.outer) | copy-start | bytes 1179652
  54.8 27.6 %copy-start.12 = (bf16[512,1536]{1,0:T(8,128)(2,1)S(1)}, bf16[512,1536]{1,0:T(8,128)(2,1)}, u32[]{:S(2)}) copy-start(bf16[512,1536]{1,0:T(8,128)(2,1)} %constant.56.clone.gather) | copy-start | bytes 4718596
  59.3 23.1 %copy-start.11 = (bf16[1536,512]{1,0:T(8,128)(2,1)S(1)}, bf16[1536,512]{1,0:T(8,128)(2,1)}, u32[]{:S(2)}) copy-start(bf16[1536,512]{1,0:T(8,128)(2,1)} %constant.58.clone.inverse) | copy-start | bytes 4718596
  59.3 23.0 %copy-start.19 = (bf16[256,512]{1,0:T(8,128)(2,1)S(1)}, bf16[256,512]{1,0:T(8,128)(2,1)}, u32[]{:S(2)}) copy-start(bf16[256,512]{1,0:T(8,128)(2,1)} %constant.57.clone.keep) | copy-start | bytes 786436
  59.3 23.0 %copy-start.21 = (f32[2,1,128]{2,1,0:T(1,128)S(1)}, f32[2,1,128]{2,1,0:T(1,128)}, u32[]{:S(2)}) copy-start(f32[2,1,128]{2,1,0:T(1,128)} %constant.59.clone.symbol) | copy-start | bytes 3076

commit v7 on v6

--- a/solution.py
+++ b/solution.py
@@ -512,7 +512,6 @@
     y_first = lax.ppermute(y_first, "gy", swaps_y[0])
     y_second = lax.ppermute(y_second, "gy", swaps_y[1])
     z_first = lax.ppermute(z_first, "gz", swaps_z[0])
-    z_second = lax.ppermute(z_second, "gz", swaps_z[1])
     partial, partial_heat, carrier_y, carrier_z, carrier_second, factors = _call(
         local_kernel,
         (
@@ -530,9 +529,10 @@
         24,
     )(metric, strain, wave_x, state, _exact(local), waves)
 
-    y_first_heat, y_second_heat, carrier_z = lax.optimization_barrier(
-        (y_first_heat, y_second_heat, carrier_z)
-    )
+    z_second, y_first_heat, y_second_heat, carrier_z = lax.optimization_barrier(
+        (z_second, y_first_heat, y_second_heat, carrier_z)
+    )
+    z_second = lax.ppermute(z_second, "gz", swaps_z[1])
     y_first_heat = lax.ppermute(y_first_heat, "gy", swaps_y[0])
     y_second_heat = lax.ppermute(y_second_heat, "gy", swaps_y[1])
     circulant = np.concatenate([circulant, circulant], axis=0)

time: 87.1 us -> 87.1 us (level)
    ppermute x1, waiting for transfers between devices: 3.68 us -> 0.01 us  [_step(): y_second = lax.ppermute(y_second, 'gy', swaps_y[1])]
    ppermute x1, waiting for transfers between devices: 0.01 us -> 2.07 us  [_step(): z_second = lax.ppermute(z_second, 'gz', swaps_z[1])]
    ppermute x1, waiting for transfers between devices: 1.19 us -> 2.13 us  [_step(): y_second_heat = lax.ppermute(y_second_heat, 'gy', swaps_y[1])]
where the time goes in v7:
time: 87.1 us; the launch traced here: 86.9 us
  blocking collectives  48.4 us (56%)
  Pallas kernels  18.2 us (21%)
  starting transfers between devices  13.6 us (16%)
  waiting for transfers between devices  4.21 us (5%)
  local copies, waits for them, and re-layouts  1.35 us (2%)
  between operations  1.09 us (1%)
    all_to_all x2, blocking collectives, _step(): lax.all_to_all(sent, ('gy', 'gz'), split_axis=0, concat_axis=0, tiled=True)  48.4 us
    ppermute x1, starting transfers between devices, _step(): y_second = lax.ppermute(y_second, 'gy', swaps_y[1])  6.26 us
    pallas_call x1, Pallas kernels, _step(): _call(plane_kernel, block, [VMEM] * 7, 'plane', 3600000000, 8 * MIB, 40)  4.48 us
    pallas_call x1, Pallas kernels, _step(): _call(project_kernel, (fields(3), field), [SMEM] + [VMEM] * 16, 'project'...  4.35 us
    pallas_call x1, Pallas kernels, _step(): _call(local_kernel, (fields(3), field, field, jax.ShapeDtypeStruct((48, N...  3.34 us
    ppermute x1, starting transfers between devices, _step(): z_second = lax.ppermute(z_second, 'gz', swaps_z[1])  3.01 us
    pallas_call x1, Pallas kernels, _step(): _call(early_kernel, (fields(3), jax.ShapeDtypeStruct((NX, EXT), F32)), [S...  2.96 us
    pallas_call x1, Pallas kernels, _step(): _call(forward_kernel, (fields(3), block), [SMEM] + [VMEM] * 13, 'forward'...  2.66 us
  transfers between devices with their start and end apart: 6, of which 2 were waited for; matrix products, arithmetic and copies ran while one was open for 0% of the time, Pallas kernels for 10%

profile of v7, /device:TPU:1, one launch (start us, length us, event | category | flops | bytes accessed | tf_op | source)
XLA Modules:
  0.0 86.9 jit_solution(1988688587368100325)
XLA Ops:
  0.6 0.0 copy-start.7
  0.6 1.2 %copy-done.7 = bf16[4,32,8,512]{3,2,1,0:T(8,128)(2,1)S(1)} copy-done((bf16[4,32,8,512]{3,2,1,0:T(8,128)(2,1)S(1)}, bf16[4,32,8,512]{3,2,1,0:T(8,128)(2,1)}, u32[]{:S(2)}) %copy-start.7) | copy-done | bytes 1048600
  1.9 0.0 copy-start.6
  1.9 0.0 copy-start.8
  1.9 0.0 copy-start.9
  1.9 0.0 copy-start.18
  1.9 0.0 copy-start.22
  1.9 0.0 copy-start.20
  1.9 0.4 edges.1
  2.3 2.1 %collective-permute-start = (bf16[3,96,512]{2,1,0:T(8,128)(2,1)S(1)}, bf16[3,96,512]{2,1,0:T(8,128)(2,1)S(1)}, u32[]{:S(2)}, u32[]{:S(2)}) collective-permute-start(bf16[3,96,512]{2,1,0:T(8,128)(2,1)S(1)} %get-tuple-element.35), channel_id=1, source_target_pairs={{0,4},{4,0},{8,12},{12,8},{16,20},{20,16},{24,28},{28,24},{32,36},... | collective-permute-start | bytes 884744 | tf_op jit(solution)/shard_map/ppermute | solution.py:512
  4.5 1.0 %collective-permute-start.1 = (bf16[4,24,512]{2,1,0:T(8,128)(2,1)S(1)}, bf16[4,24,512]{2,1,0:T(8,128)(2,1)S(1)}, u32[]{:S(2)}, u32[]{:S(2)}) collective-permute-start(bf16[4,24,512]{2,1,0:T(8,128)(2,1)S(1)} %get-tuple-element.36), channel_id=1, source_target_pairs={{0,1},{1,0},{2,3},{3,2},{4,5},{5,4},{6,7},{7,6},{8,9},{9,8},{10,11... | collective-permute-start | bytes 294920 | tf_op jit(solution)/shard_map/ppermute | solution.py:514
  5.4 6.3 %collective-permute-start.2 = (bf16[3,96,512]{2,1,0:T(8,128)(2,1)S(1)}, bf16[3,96,512]{2,1,0:T(8,128)(2,1)S(1)}, u32[]{:S(2)}, u32[]{:S(2)}) collective-permute-start(bf16[3,96,512]{2,1,0:T(8,128)(2,1)S(1)} %get-tuple-element.40), channel_id=1, source_target_pairs={{0,124},{4,8},{8,4},{12,16},{16,12},{20,24},{24,20},{28,32},{32,28... | collective-permute-start | bytes 884744 | tf_op jit(solution)/shard_map/ppermute | solution.py:513
  11.7 0.0 copy-done.6
  11.7 0.0 copy-done.8
  11.7 0.0 copy-done.9
  11.7 0.0 copy-done.14
  11.7 0.0 copy-done.18
  11.7 0.0 copy-done.22
  11.7 3.3 %local.1 = (f32[3,256,512]{2,1,0:T(8,128)S(1)}, f32[256,512]{1,0:T(8,128)S(1)}, f32[256,512]{1,0:T(8,128)S(1)}, f32[48,512]{1,0:T(8,128)S(1)}, f32[96,512]{1,0:T(8,128)S(1)}, /*index=5*/f32[2,128,256]{2,1,0:T(8,128)S(1)}) custom-call(f32[3,3]{1,0:T(4,128)S(1)} %copy-done.6, f32[3,3]{1,0:T(4,128)S(1)} %copy-done.9, f32[256]{0:T(256)S(1)} %copy-done.22, ...), custom_call_target="tpu_custom_call" | custom-call | flops 1000000000 | bytes 4194304 | tf_op jit(solution)/shard_map/local/pallas_call | solution.py:515
  15.1 3.0 %collective-permute-start.3 = (bf16[4,24,512]{2,1,0:T(8,128)(2,1)S(1)}, bf16[4,24,512]{2,1,0:T(8,128)(2,1)S(1)}, u32[]{:S(2)}, u32[]{:S(2)}) collective-permute-start(bf16[4,24,512]{2,1,0:T(8,128)(2,1)S(1)} %get-tuple-element.41), channel_id=1, source_target_pairs={{0,3},{1,2},{2,1},{3,0},{4,7},{5,6},{6,5},{7,4},{8,11},{9,10},{10,... | collective-permute-start | bytes 294920 | tf_op jit(solution)/shard_map/ppermute | solution.py:535
  18.1 0.0 collective-permute-start.4
  18.1 0.0 collective-permute-done.1.z_first
  18.1 1.3 %collective-permute-start.5 = (bf16[1,96,512]{2,1,0:T(8,128)(2,1)S(1)}, bf16[1,96,512]{2,1,0:T(8,128)(2,1)S(1)}, u32[]{:S(2)}, u32[]{:S(2)}) collective-permute-start(bf16[1,96,512]{2,1,0:T(8,128)(2,1)S(1)} %get-tuple-element.44), channel_id=1, source_target_pairs={{0,124},{4,8},{8,4},{12,16},{16,12},{20,24},{24,20},{28,32},{32,28... | collective-permute-start | bytes 294920 | tf_op jit(solution)/shard_map/ppermute | solution.py:537
  19.4 0.0 collective-permute-done.y_first
  19.4 0.0 copy-done.20
  19.4 0.0 copy-done.1
  19.4 0.0 copy-done.2
  19.4 0.0 copy-done.5
  19.4 0.0 copy-done.13
  19.4 0.0 copy-start
  19.4 0.0 copy-start.3
  19.4 0.0 copy-start.4
  19.4 3.0 %early.1 = (f32[3,256,512]{2,1,0:T(8,128)S(1)}, f32[512,512]{1,0:T(8,128)S(1)}) custom-call(f32[3,3]{1,0:T(4,128)S(1)} %copy-done.6, f32[3,256,512]{2,1,0:T(8,128)S(1)} %get-tuple-element.28.partial, f32[256,512]{1,0:T(8,128)S(1)} %get-tuple-element.29.carrier_y, f32[48,512]{1,0:T(8,128)S(1)} %get-tuple-element.34.carrier_z, ...), custom_call_target="tpu_custom_call" | custom-call | flops 3000000000 | bytes 8388608 | tf_op jit(solution)/shard_map/early/pallas_call | solution.py:540
  22.4 2.1 %collective-permute-done.3.z_second = bf16[4,24,512]{2,1,0:T(8,128)(2,1)S(1)} collective-permute-done((bf16[4,24,512]{2,1,0:T(8,128)(2,1)S(1)}, bf16[4,24,512]{2,1,0:T(8,128)(2,1)S(1)}, u32[]{:S(2)}, u32[]{:S(2)}) %collective-permute-start.3) | collective-permute-done | bytes 98336 | tf_op jit(solution)/shard_map/ppermute | solution.py:535
  24.5 0.0 collective-permute-done.2.y_second
  24.5 0.0 copy-done
  24.5 0.0 copy-done.3
  24.5 0.0 copy-done.4
  24.5 0.0 slice-start.1
  24.5 0.0 copy-start.10
  24.5 2.7 %forward.1 = (f32[3,256,512]{2,1,0:T(8,128)S(1)}, f32[128,16,128]{2,1,0:T(8,128)S(1)}) custom-call(f32[3,3]{1,0:T(4,128)S(1)} %copy-done.6, f32[3,256,512]{2,1,0:T(8,128)S(1)} %get-tuple-element.37.partial, f32[512,512]{1,0:T(8,128)S(1)} %get-tuple-element.38.spectrum, f32[256,512]{1,0:T(8,128)S(1)} %get-tuple-element.29.carrier_y, ...), custom_call_target="tpu_custom_call" | custom-call | flops 2000000000 | bytes 8388608 | tf_op jit(solution)/shard_map/forward/pallas_call | solution.py:561
  27.2 0.0 copy-start.15
  27.2 0.0 copy-start.16
  27.2 0.0 copy-start.17
  27.2 0.0 collective-permute-done.4.y_first
  27.3 2.1 %collective-permute-done.5.y_second = bf16[1,96,512]{2,1,0:T(8,128)(2,1)S(1)} collective-permute-done((bf16[1,96,512]{2,1,0:T(8,128)(2,1)S(1)}, bf16[1,96,512]{2,1,0:T(8,128)(2,1)S(1)}, u32[]{:S(2)}, u32[]{:S(2)}) %collective-permute-start.5) | collective-permute-done | bytes 98336 | tf_op jit(solution)/shard_map/ppermute | solution.py:537
  29.4 25.4 %all_to_all.10.got = f32[128,16,128]{2,1,0:T(8,128)S(1)} all-to-all(f32[128,16,128]{2,1,0:T(8,128)S(1)} %get-tuple-element.45), channel_id=1, replica_groups=mesh['gy'=32,'gz'=4] {'gy','gz'}, dimensions={0} | all-to-all | bytes 2097152 | tf_op jit(solution)/shard_map/all_to_all | solution.py:588
  54.8 0.0 slice-done
  54.8 0.0 slice-done.1
  54.8 0.0 copy-done.10
  54.8 0.0 copy-done.15
  54.8 0.0 copy-done.16
  54.8 0.0 copy-done.17
  54.8 0.0 copy-start.12
  54.8 4.5 %plane.1 = f32[128,16,128]{2,1,0:T(8,128)S(1)} custom-call(f32[2,128,256]{2,1,0:T(8,128)S(1)} %get-tuple-element.27.factors, f32[128,16,128]{2,1,0:T(8,128)S(1)} %all_to_all.10.got, bf16[256,768]{1,0:T(8,128)(2,1)S(1)} %copy-done.17, bf16[256,1280]{1,0:T(8,128)(2,1)S(1)} %copy-done.15, f32[2,128,512]{2,1,0:T(8,128)S(1)} %copy-done.16, ...), custom_call_target="tpu_custom_call" | custom-call | flops 3600000000 | bytes 8388608 | tf_op jit(solution)/shard_map/plane/pallas_call | solution.py:589
  59.3 0.0 copy-start.11
  59.3 0.0 copy-start.19
  59.3 0.0 copy-start.21
  59.4 23.0 %all_to_all.11.got = f32[128,16,128]{2,1,0:T(8,128)S(1)} all-to-all(f32[128,16,128]{2,1,0:T(8,128)S(1)} %plane.1), channel_id=1, replica_groups=mesh['gy'=32,'gz'=4] {'gy','gz'}, dimensions={0} | all-to-all | bytes 2097152 | tf_op jit(solution)/shard_map/all_to_all | solution.py:600
  82.4 0.0 copy-done.12
  82.4 0.0 copy-done.11
  82.4 0.0 copy-done.19
  82.4 0.0 copy-done.21
  82.4 4.4 %project.1 = (f32[3,256,512]{2,1,0:T(8,128)}, f32[256,512]{1,0:T(8,128)}) custom-call(f32[3,3]{1,0:T(4,128)S(1)} %copy-done.6, f32[128,16,128]{2,1,0:T(8,128)S(1)} %all_to_all.11.got, bf16[512,1536]{1,0:T(8,128)(2,1)S(1)} %copy-done.12, bf16[256,512]{1,0:T(8,128)(2,1)S(1)} %copy-done.19, bf16[1536,512]{1,0:T(8,128)(2,1)S(1)} %copy-done.11, ...), custom_call_target="tpu_custom_call" | custom-call | flops 2500000000 | bytes 8388608 | tf_op jit(solution)/shard_map/project/pallas_call | solution.py:601
  (7 shorter events, 0.0 us)
Async XLA Ops:
  0.6 1.2 %copy-start.7 = (bf16[4,32,8,512]{3,2,1,0:T(8,128)(2,1)S(1)}, bf16[4,32,8,512]{3,2,1,0:T(8,128)(2,1)}, u32[]{:S(2)}) copy-start(bf16[4,32,8,512]{3,2,1,0:T(8,128)(2,1)} %param.23) | copy-start | bytes 3145732
  1.9 9.8 %copy-start.6 = (f32[3,3]{1,0:T(4,128)S(1)}, f32[3,3]{1,0:T(4,128)}, u32[]{:S(2)}) copy-start(f32[3,3]{1,0:T(4,128)} %metric.7) | copy-start | bytes 112
  1.9 9.8 %copy-start.8 = (bf16[4,32,8,512]{3,2,1,0:T(8,128)(2,1)S(1)}, bf16[4,32,8,512]{3,2,1,0:T(8,128)(2,1)}, u32[]{:S(2)}) copy-start(bf16[4,32,8,512]{3,2,1,0:T(8,128)(2,1)} %param.23) | copy-start | bytes 3145732
  1.9 9.8 %copy-start.9 = (f32[3,3]{1,0:T(4,128)S(1)}, f32[3,3]{1,0:T(4,128)}, u32[]{:S(2)}) copy-start(f32[3,3]{1,0:T(4,128)} %strain.1) | copy-start | bytes 112
  1.9 9.8 %copy-start.14 = (bf16[768,512]{1,0:T(8,128)(2,1)S(1)}, bf16[768,512]{1,0:T(8,128)(2,1)}, u32[]{:S(2)}) copy-start(bf16[768,512]{1,0:T(8,128)(2,1)} %constant.41.clone.along) | copy-start | bytes 2359300
  1.9 9.8 %copy-start.18 = (f32[3,128,256]{2,1,0:T(8,128)S(1)}, f32[3,128,256]{2,1,0:T(8,128)}, u32[]{:S(2)}) copy-start(f32[3,128,256]{2,1,0:T(8,128)} %constant.42.clone.waves) | copy-start | bytes 1179652
  1.9 9.8 %copy-start.22 = (f32[256]{0:T(256)S(1)}, f32[256]{0:T(256)}, u32[]{:S(2)}) copy-start(f32[256]{0:T(256)} %constant.40.clone.wave_x) | copy-start | bytes 3076
  1.9 17.5 %copy-start.20 = (bf16[2,256,96]{2,1,0:T(8,128)(2,1)S(1)}, bf16[2,256,96]{2,1,0:T(8,128)(2,1)}, u32[]{:S(2)}) copy-start(bf16[2,256,96]{2,1,0:T(8,128)(2,1)} %constant.43.clone.along_first) | copy-start | bytes 294916
  2.3 17.0 %collective-permute-start = (bf16[3,96,512]{2,1,0:T(8,128)(2,1)S(1)}, bf16[3,96,512]{2,1,0:T(8,128)(2,1)S(1)}, u32[]{:S(2)}, u32[]{:S(2)}) collective-permute-start(bf16[3,96,512]{2,1,0:T(8,128)(2,1)S(1)} %get-tuple-element.35), channel_id=1, source_target_pairs={{0,4},{4,0},{8,12},{12,8},{16,20},{20,16},{24,28},{28,24},{32,36},... | collective-permute-start | bytes 884744 | tf_op jit(solution)/shard_map/ppermute | solution.py:512
  4.5 13.6 %collective-permute-start.1 = (bf16[4,24,512]{2,1,0:T(8,128)(2,1)S(1)}, bf16[4,24,512]{2,1,0:T(8,128)(2,1)S(1)}, u32[]{:S(2)}, u32[]{:S(2)}) collective-permute-start(bf16[4,24,512]{2,1,0:T(8,128)(2,1)S(1)} %get-tuple-element.36), channel_id=1, source_target_pairs={{0,1},{1,0},{2,3},{3,2},{4,5},{5,4},{6,7},{7,6},{8,9},{9,8},{10,11... | collective-permute-start | bytes 294920 | tf_op jit(solution)/shard_map/ppermute | solution.py:514
  5.4 14.0 %copy-start.1 = (bf16[512,1536]{1,0:T(8,128)(2,1)S(1)}, bf16[512,1536]{1,0:T(8,128)(2,1)}, u32[]{:S(2)}) copy-start(bf16[512,1536]{1,0:T(8,128)(2,1)} %constant.47.clone.waves) | copy-start | bytes 4718596
  5.4 14.0 %copy-start.2 = (bf16[1024,512]{1,0:T(8,128)(2,1)S(1)}, bf16[1024,512]{1,0:T(8,128)(2,1)}, u32[]{:S(2)}) copy-start(bf16[1024,512]{1,0:T(8,128)(2,1)} %constant.46.clone.along_x) | copy-start | bytes 3145732
  5.4 14.0 %copy-start.5 = (bf16[2,24,24]{2,1,0:T(8,128)(2,1)S(1)}, bf16[2,24,24]{2,1,0:T(8,128)(2,1)}, u32[]{:S(2)}) copy-start(bf16[2,24,24]{2,1,0:T(8,128)(2,1)} %constant.44.clone.along_z) | copy-start | bytes 6916
  5.4 14.0 %copy-start.13 = (bf16[512,1024]{1,0:T(8,128)(2,1)S(1)}, bf16[512,1024]{1,0:T(8,128)(2,1)}, u32[]{:S(2)}) copy-start(bf16[512,1024]{1,0:T(8,128)(2,1)} %constant.45.clone.spread) | copy-start | bytes 3145732
  5.4 19.1 %collective-permute-start.2 = (bf16[3,96,512]{2,1,0:T(8,128)(2,1)S(1)}, bf16[3,96,512]{2,1,0:T(8,128)(2,1)S(1)}, u32[]{:S(2)}, u32[]{:S(2)}) collective-permute-start(bf16[3,96,512]{2,1,0:T(8,128)(2,1)S(1)} %get-tuple-element.40), channel_id=1, source_target_pairs={{0,124},{4,8},{8,4},{12,16},{16,12},{20,24},{24,20},{28,32},{32,28... | collective-permute-start | bytes 884744 | tf_op jit(solution)/shard_map/ppermute | solution.py:513
  15.1 9.4 %collective-permute-start.3 = (bf16[4,24,512]{2,1,0:T(8,128)(2,1)S(1)}, bf16[4,24,512]{2,1,0:T(8,128)(2,1)S(1)}, u32[]{:S(2)}, u32[]{:S(2)}) collective-permute-start(bf16[4,24,512]{2,1,0:T(8,128)(2,1)S(1)} %get-tuple-element.41), channel_id=1, source_target_pairs={{0,3},{1,2},{2,1},{3,0},{4,7},{5,6},{6,5},{7,4},{8,11},{9,10},{10,... | collective-permute-start | bytes 294920 | tf_op jit(solution)/shard_map/ppermute | solution.py:535
  18.1 9.2 %collective-permute-start.4 = (bf16[1,96,512]{2,1,0:T(8,128)(2,1)S(1)}, bf16[1,96,512]{2,1,0:T(8,128)(2,1)S(1)}, u32[]{:S(2)}, u32[]{:S(2)}) collective-permute-start(bf16[1,96,512]{2,1,0:T(8,128)(2,1)S(1)} %get-tuple-element.43), channel_id=1, source_target_pairs={{0,4},{4,0},{8,12},{12,8},{16,20},{20,16},{24,28},{28,24},{32,36},... | collective-permute-start | bytes 294920 | tf_op jit(solution)/shard_map/ppermute | solution.py:536
  18.1 11.3 %collective-permute-start.5 = (bf16[1,96,512]{2,1,0:T(8,128)(2,1)S(1)}, bf16[1,96,512]{2,1,0:T(8,128)(2,1)S(1)}, u32[]{:S(2)}, u32[]{:S(2)}) collective-permute-start(bf16[1,96,512]{2,1,0:T(8,128)(2,1)S(1)} %get-tuple-element.44), channel_id=1, source_target_pairs={{0,124},{4,8},{8,4},{12,16},{16,12},{20,24},{24,20},{28,32},{32,28... | collective-permute-start | bytes 294920 | tf_op jit(solution)/shard_map/ppermute | solution.py:537
  19.4 5.1 %copy-start = (bf16[4,768,512]{2,1,0:T(8,128)(2,1)S(1)}, bf16[4,768,512]{2,1,0:T(8,128)(2,1)}, u32[]{:S(2)}) copy-start(bf16[4,768,512]{2,1,0:T(8,128)(2,1)} %constant.50.clone.spread_rows) | copy-start | bytes 9437188
  19.4 5.1 %copy-start.3 = (bf16[2,256,96]{2,1,0:T(8,128)(2,1)S(1)}, bf16[2,256,96]{2,1,0:T(8,128)(2,1)}, u32[]{:S(2)}) copy-start(bf16[2,256,96]{2,1,0:T(8,128)(2,1)} %constant.48.clone.along_second) | copy-start | bytes 294916
  19.4 5.1 %copy-start.4 = (bf16[2,96,96]{2,1,0:T(8,128)(2,1)S(1)}, bf16[2,96,96]{2,1,0:T(8,128)(2,1)}, u32[]{:S(2)}) copy-start(bf16[2,96,96]{2,1,0:T(8,128)(2,1)} %constant.49.clone.along_rows) | copy-start | bytes 110596
  24.5 30.3 %slice-start = ((s8[5242880]{0:T(1024)(128)(4,1)}), s8[4194304]{0:T(1024)(128)(4,1)S(1)}, s32[]{:S(2)}) async-start(s8[5242880]{0:T(1024)(128)(4,1)} %bitcast.5), calls=%async_computation.2 | async-start | bytes 8388608
  24.5 30.3 %slice-start.1 = ((s8[5242880]{0:T(1024)(128)(4,1)}), s8[1048576]{0:T(1024)(128)(4,1)S(1)}, s32[]{:S(2)}) async-start(s8[5242880]{0:T(1024)(128)(4,1)} %bitcast.5), calls=%async_computation.3 | async-start | bytes 2097152
  24.5 30.2 %copy-start.10 = (bf16[3072,512]{1,0:T(8,128)(2,1)S(1)}, bf16[3072,512]{1,0:T(8,128)(2,1)}, u32[]{:S(2)}) copy-start(bf16[3072,512]{1,0:T(8,128)(2,1)} %constant.54.clone.inner) | copy-start | bytes 9437188
  27.2 27.6 %copy-start.15 = (bf16[256,1280]{1,0:T(8,128)(2,1)S(1)}, bf16[256,1280]{1,0:T(8,128)(2,1)}, u32[]{:S(2)}) copy-start(bf16[256,1280]{1,0:T(8,128)(2,1)} %constant.52.clone.outer_back) | copy-start | bytes 1966084
  27.2 27.6 %copy-start.16 = (f32[2,128,512]{2,1,0:T(8,128)S(1)}, f32[2,128,512]{2,1,0:T(8,128)}, u32[]{:S(2)}) copy-start(f32[2,128,512]{2,1,0:T(8,128)} %constant.53.clone.twist) | copy-start | bytes 1572868
  27.2 27.6 %copy-start.17 = (bf16[256,768]{1,0:T(8,128)(2,1)S(1)}, bf16[256,768]{1,0:T(8,128)(2,1)}, u32[]{:S(2)}) copy-start(bf16[256,768]{1,0:T(8,128)(2,1)} %constant.51.clone.outer) | copy-start | bytes 1179652
  54.8 27.6 %copy-start.12 = (bf16[512,1536]{1,0:T(8,128)(2,1)S(1)}, bf16[512,1536]{1,0:T(8,128)(2,1)}, u32[]{:S(2)}) copy-start(bf16[512,1536]{1,0:T(8,128)(2,1)} %constant.56.clone.gather) | copy-start | bytes 4718596
  59.3 23.1 %copy-start.11 = (bf16[1536,512]{1,0:T(8,128)(2,1)S(1)}, bf16[1536,512]{1,0:T(8,128)(2,1)}, u32[]{:S(2)}) copy-start(bf16[1536,512]{1,0:T(8,128)(2,1)} %constant.58.clone.inverse) | copy-start | bytes 4718596
  59.3 23.0 %copy-start.19 = (bf16[256,512]{1,0:T(8,128)(2,1)S(1)}, bf16[256,512]{1,0:T(8,128)(2,1)}, u32[]{:S(2)}) copy-start(bf16[256,512]{1,0:T(8,128)(2,1)} %constant.57.clone.keep) | copy-start | bytes 786436
  59.3 23.0 %copy-start.21 = (f32[2,1,128]{2,1,0:T(1,128)S(1)}, f32[2,1,128]{2,1,0:T(1,128)}, u32[]{:S(2)}) copy-start(f32[2,1,128]{2,1,0:T(1,128)} %constant.59.clone.symbol) | copy-start | bytes 3076

commit v8 on v6

--- a/solution.py
+++ b/solution.py
@@ -162,7 +162,17 @@
     return lax.rem(lax.axis_index(axis), 2)
 
 
-def edges_kernel(state, y_first, y_second, y_first_heat, y_second_heat, z_first, z_second):
+def first_kernel(state, y_first):
+    row = lax.broadcasted_iota(jnp.int32, (96, CELLS), 0)
+    column = lax.broadcasted_iota(jnp.int32, (96, CELLS), 1)
+    third = (row * 171) >> 9
+    source = BY * third + (row - 3 * third) + (BY - 3) * (1 - _odd("gy"))
+    pick = jnp.where(column == source, 1.0, 0.0).astype(BF16)
+    for q in range(3):
+        y_first[q] = _dot(pick, state[q]).astype(BF16)
+
+
+def edges_kernel(state, y_second, y_first_heat, y_second_heat, z_first, z_second):
     odd_y, odd_z = _odd("gy"), _odd("gz")
     row = lax.broadcasted_iota(jnp.int32, (240, CELLS), 0)
     column = lax.broadcasted_iota(jnp.int32, (240, CELLS), 1)
@@ -178,9 +188,11 @@
     pick = jnp.where(column == source, 1.0, 0.0).astype(BF16)
     for q in range(4):
         rows = _dot(pick, state[q])
-        first, second, at = (y_first, y_second, q) if q < 3 else (y_first_heat, y_second_heat, 0)
-        first[at] = rows[0:96].astype(BF16)
-        second[at] = rows[96:192].astype(BF16)
+        if q < 3:
+            y_second[q] = rows[96:192].astype(BF16)
+        else:
+            y_first_heat[0] = rows[0:96].astype(BF16)
+            y_second_heat[0] = rows[96:192].astype(BF16)
         z_first[q] = rows[192:216].astype(BF16)
         z_second[q] = rows[216:240].astype(BF16)
 
@@ -499,9 +511,10 @@
     y_side = jax.ShapeDtypeStruct((3, 96, NX), BF16)
     y_side_heat = jax.ShapeDtypeStruct((1, 96, NX), BF16)
     z_side = jax.ShapeDtypeStruct((4, 24, NX), BF16)
-    y_first, y_second, y_first_heat, y_second_heat, z_first, z_second = _call(
+    y_first = _call(first_kernel, y_side, [VMEM], "first", 100_000_000, 2 * MIB, 16)(state)
+    y_second, y_first_heat, y_second_heat, z_first, z_second = _call(
         edges_kernel,
-        (y_side, y_side, y_side_heat, y_side_heat, z_side, z_side),
+        (y_side, y_side_heat, y_side_heat, z_side, z_side),
         [VMEM],
         "edges",
         20_000_000_000,

time: 87.1 us -> 87 us (level)
  transfers between devices with their start and end apart: 6 -> 6, of which waited for: 2 -> 2; matrix products, arithmetic and copies ran while one was open for 0% -> 0% of each run, Pallas kernels for 10% -> 11%
where the time goes in v8:
time: 87 us; the launch traced here: 86.8 us
  blocking collectives  48.4 us (56%)
  Pallas kernels  18.5 us (21%)
  starting transfers between devices  13.2 us (15%)
  waiting for transfers between devices  4.27 us (5%)
  local copies, waits for them, and re-layouts  1.36 us (2%)
  between operations  1.12 us (1%)
    all_to_all x2, blocking collectives, _step(): lax.all_to_all(sent, ('gy', 'gz'), split_axis=0, concat_axis=0, tiled=True)  48.4 us
    ppermute x1, starting transfers between devices, _step(): y_second = lax.ppermute(y_second, 'gy', swaps_y[1])  5.95 us
    pallas_call x1, Pallas kernels, _step(): _call(plane_kernel, block, [VMEM] * 7, 'plane', 3600000000, 8 * MIB, 40)  4.48 us
    pallas_call x1, Pallas kernels, _step(): _call(project_kernel, (fields(3), field), [SMEM] + [VMEM] * 16, 'project'...  4.36 us
    pallas_call x1, Pallas kernels, _step(): _call(local_kernel, (fields(3), field, field, jax.ShapeDtypeStruct((48, N...  3.34 us
    ppermute x1, waiting for transfers between devices, _step(): y_second = lax.ppermute(y_second, 'gy', swaps_y[1])  3.09 us
    pallas_call x1, Pallas kernels, _step(): _call(early_kernel, (fields(3), jax.ShapeDtypeStruct((NX, EXT), F32)), [S...  2.96 us
    pallas_call x1, Pallas kernels, _step(): _call(forward_kernel, (fields(3), block), [SMEM] + [VMEM] * 13, 'forward'...  2.65 us
  transfers between devices with their start and end apart: 6, of which 2 were waited for; matrix products, arithmetic and copies ran while one was open for 0% of the time, Pallas kernels for 11%

profile of v8, /device:TPU:1, one launch (start us, length us, event | category | flops | bytes accessed | tf_op | source)
XLA Modules:
  0.0 86.8 jit_solution(12481366536484458593)
XLA Ops:
  0.6 0.0 copy-start.3
  0.6 1.2 %copy-done.3 = bf16[4,32,8,512]{3,2,1,0:T(8,128)(2,1)S(1)} copy-done((bf16[4,32,8,512]{3,2,1,0:T(8,128)(2,1)S(1)}, bf16[4,32,8,512]{3,2,1,0:T(8,128)(2,1)}, u32[]{:S(2)}) %copy-start.3) | copy-done | bytes 1048600
  1.9 0.3 first.1
  2.1 0.0 copy-start.4
  2.1 0.0 copy-start.8
  2.1 0.0 copy-start.9
  2.2 0.0 copy-start.14
  2.2 0.0 copy-start.18
  2.2 0.0 copy-start.22
  2.2 2.1 %collective-permute-start = (bf16[3,96,512]{2,1,0:T(8,128)(2,1)S(1)}, bf16[3,96,512]{2,1,0:T(8,128)(2,1)S(1)}, u32[]{:S(2)}, u32[]{:S(2)}) collective-permute-start(bf16[3,96,512]{2,1,0:T(8,128)(2,1)S(1)} %first.1), channel_id=1, source_target_pairs={{0,4},{4,0},{8,12},{12,8},{16,20},{20,16},{24,28},{28,24},{32,36},... | collective-permute-start | bytes 884744 | tf_op jit(solution)/shard_map/ppermute | solution.py:525
  4.3 0.4 edges.1
  4.7 1.0 %collective-permute-start.1 = (bf16[4,24,512]{2,1,0:T(8,128)(2,1)S(1)}, bf16[4,24,512]{2,1,0:T(8,128)(2,1)S(1)}, u32[]{:S(2)}, u32[]{:S(2)}) collective-permute-start(bf16[4,24,512]{2,1,0:T(8,128)(2,1)S(1)} %get-tuple-element.32), channel_id=1, source_target_pairs={{0,1},{1,0},{2,3},{3,2},{4,5},{5,4},{6,7},{7,6},{8,9},{9,8},{10,11... | collective-permute-start | bytes 294920 | tf_op jit(solution)/shard_map/ppermute | solution.py:527
  5.8 2.4 %collective-permute-start.3 = (bf16[4,24,512]{2,1,0:T(8,128)(2,1)S(1)}, bf16[4,24,512]{2,1,0:T(8,128)(2,1)S(1)}, u32[]{:S(2)}, u32[]{:S(2)}) collective-permute-start(bf16[4,24,512]{2,1,0:T(8,128)(2,1)S(1)} %get-tuple-element.37), channel_id=1, source_target_pairs={{0,3},{1,2},{2,1},{3,0},{4,7},{5,6},{6,5},{7,4},{8,11},{9,10},{10,... | collective-permute-start | bytes 294920 | tf_op jit(solution)/shard_map/ppermute | solution.py:528
  8.2 5.9 %collective-permute-start.2 = (bf16[3,96,512]{2,1,0:T(8,128)(2,1)S(1)}, bf16[3,96,512]{2,1,0:T(8,128)(2,1)S(1)}, u32[]{:S(2)}, u32[]{:S(2)}) collective-permute-start(bf16[3,96,512]{2,1,0:T(8,128)(2,1)S(1)} %get-tuple-element.36), channel_id=1, source_target_pairs={{0,124},{4,8},{8,4},{12,16},{16,12},{20,24},{24,20},{28,32},{32,28... | collective-permute-start | bytes 884744 | tf_op jit(solution)/shard_map/ppermute | solution.py:526
  14.2 0.0 copy-done.4
  14.2 0.0 copy-done.8
  14.2 0.0 copy-done.9
  14.2 0.0 copy-done.14
  14.2 0.0 copy-done.18
  14.2 0.0 copy-done.22
  14.2 3.3 %local.1 = (f32[3,256,512]{2,1,0:T(8,128)S(1)}, f32[256,512]{1,0:T(8,128)S(1)}, f32[256,512]{1,0:T(8,128)S(1)}, f32[48,512]{1,0:T(8,128)S(1)}, f32[96,512]{1,0:T(8,128)S(1)}, /*index=5*/f32[2,128,256]{2,1,0:T(8,128)S(1)}) custom-call(f32[3,3]{1,0:T(4,128)S(1)} %copy-done.8, f32[3,3]{1,0:T(4,128)S(1)} %copy-done.9, f32[256]{0:T(256)S(1)} %copy-done.22, ...), custom_call_target="tpu_custom_call" | custom-call | flops 1000000000 | bytes 4194304 | tf_op jit(solution)/shard_map/local/pallas_call | solution.py:529
  17.5 0.1 collective-permute-start.4
  17.6 0.0 collective-permute-done.1.z_first
  17.6 1.5 %collective-permute-start.5 = (bf16[1,96,512]{2,1,0:T(8,128)(2,1)S(1)}, bf16[1,96,512]{2,1,0:T(8,128)(2,1)S(1)}, u32[]{:S(2)}, u32[]{:S(2)}) collective-permute-start(bf16[1,96,512]{2,1,0:T(8,128)(2,1)S(1)} %get-tuple-element.40), channel_id=1, source_target_pairs={{0,124},{4,8},{8,4},{12,16},{16,12},{20,24},{24,20},{28,32},{32,28... | collective-permute-start | bytes 294920 | tf_op jit(solution)/shard_map/ppermute | solution.py:550
  19.2 0.0 collective-permute-done.y_first
  19.2 0.0 copy-done.20
  19.2 0.0 copy-done.1
  19.2 0.0 copy-done.2
  19.2 0.0 copy-done.7
  19.2 0.0 copy-done.13
  19.2 0.0 copy-start
  19.2 0.0 copy-start.5
  19.3 0.0 copy-start.6
  19.3 3.0 %early.1 = (f32[3,256,512]{2,1,0:T(8,128)S(1)}, f32[512,512]{1,0:T(8,128)S(1)}) custom-call(f32[3,3]{1,0:T(4,128)S(1)} %copy-done.8, f32[3,256,512]{2,1,0:T(8,128)S(1)} %get-tuple-element.26.partial, f32[256,512]{1,0:T(8,128)S(1)} %get-tuple-element.27.carrier_y, f32[48,512]{1,0:T(8,128)S(1)} %get-tuple-element.31.carrier_z, ...), custom_call_target="tpu_custom_call" | custom-call | flops 3000000000 | bytes 8388608 | tf_op jit(solution)/shard_map/early/pallas_call | solution.py:553
  22.2 0.0 collective-permute-done.3.z_second
  22.2 3.1 %collective-permute-done.2.y_second = bf16[3,96,512]{2,1,0:T(8,128)(2,1)S(1)} collective-permute-done((bf16[3,96,512]{2,1,0:T(8,128)(2,1)S(1)}, bf16[3,96,512]{2,1,0:T(8,128)(2,1)S(1)}, u32[]{:S(2)}, u32[]{:S(2)}) %collective-permute-start.2) | collective-permute-done | bytes 294944 | tf_op jit(solution)/shard_map/ppermute | solution.py:526
  25.3 0.0 copy-done
  25.3 0.0 copy-done.5
  25.3 0.0 copy-done.6
  25.3 0.0 slice-start.1
  25.4 0.0 copy-start.10
  25.4 2.6 %forward.1 = (f32[3,256,512]{2,1,0:T(8,128)S(1)}, f32[128,16,128]{2,1,0:T(8,128)S(1)}) custom-call(f32[3,3]{1,0:T(4,128)S(1)} %copy-done.8, f32[3,256,512]{2,1,0:T(8,128)S(1)} %get-tuple-element.33.partial, f32[512,512]{1,0:T(8,128)S(1)} %get-tuple-element.34.spectrum, f32[256,512]{1,0:T(8,128)S(1)} %get-tuple-element.27.carrier_y, ...), custom_call_target="tpu_custom_call" | custom-call | flops 2000000000 | bytes 8388608 | tf_op jit(solution)/shard_map/forward/pallas_call | solution.py:574
  28.0 0.0 copy-start.15
  28.0 0.0 copy-start.16
  28.0 0.0 copy-start.17
  28.1 0.0 collective-permute-done.4.y_first
  28.1 1.2 %collective-permute-done.5.y_second = bf16[1,96,512]{2,1,0:T(8,128)(2,1)S(1)} collective-permute-done((bf16[1,96,512]{2,1,0:T(8,128)(2,1)S(1)}, bf16[1,96,512]{2,1,0:T(8,128)(2,1)S(1)}, u32[]{:S(2)}, u32[]{:S(2)}) %collective-permute-start.5) | collective-permute-done | bytes 98336 | tf_op jit(solution)/shard_map/ppermute | solution.py:550
  29.2 25.4 %all_to_all.10.got = f32[128,16,128]{2,1,0:T(8,128)S(1)} all-to-all(f32[128,16,128]{2,1,0:T(8,128)S(1)} %get-tuple-element.41), channel_id=1, replica_groups=mesh['gy'=32,'gz'=4] {'gy','gz'}, dimensions={0} | all-to-all | bytes 2097152 | tf_op jit(solution)/shard_map/all_to_all | solution.py:601
  54.6 0.0 slice-done
  54.6 0.0 slice-done.1
  54.6 0.0 copy-done.10
  54.6 0.0 copy-done.15
  54.6 0.0 copy-done.16
  54.7 0.0 copy-done.17
  54.7 0.0 copy-start.12
  54.7 4.5 %plane.1 = f32[128,16,128]{2,1,0:T(8,128)S(1)} custom-call(f32[2,128,256]{2,1,0:T(8,128)S(1)} %get-tuple-element.25.factors, f32[128,16,128]{2,1,0:T(8,128)S(1)} %all_to_all.10.got, bf16[256,768]{1,0:T(8,128)(2,1)S(1)} %copy-done.17, bf16[256,1280]{1,0:T(8,128)(2,1)S(1)} %copy-done.15, f32[2,128,512]{2,1,0:T(8,128)S(1)} %copy-done.16, ...), custom_call_target="tpu_custom_call" | custom-call | flops 3600000000 | bytes 8388608 | tf_op jit(solution)/shard_map/plane/pallas_call | solution.py:602
  59.2 0.0 copy-start.11
  59.2 0.0 copy-start.19
  59.2 0.0 copy-start.21
  59.2 23.0 %all_to_all.11.got = f32[128,16,128]{2,1,0:T(8,128)S(1)} all-to-all(f32[128,16,128]{2,1,0:T(8,128)S(1)} %plane.1), channel_id=1, replica_groups=mesh['gy'=32,'gz'=4] {'gy','gz'}, dimensions={0} | all-to-all | bytes 2097152 | tf_op jit(solution)/shard_map/all_to_all | solution.py:613
  82.2 0.0 copy-done.12
  82.2 0.0 copy-done.11
  82.2 0.0 copy-done.21
  82.2 4.4 %project.1 = (f32[3,256,512]{2,1,0:T(8,128)}, f32[256,512]{1,0:T(8,128)}) custom-call(f32[3,3]{1,0:T(4,128)S(1)} %copy-done.8, f32[128,16,128]{2,1,0:T(8,128)S(1)} %all_to_all.11.got, bf16[512,1536]{1,0:T(8,128)(2,1)S(1)} %copy-done.12, bf16[256,512]{1,0:T(8,128)(2,1)S(1)} %copy-done.19, bf16[1536,512]{1,0:T(8,128)(2,1)S(1)} %copy-done.11, ...), custom_call_target="tpu_custom_call" | custom-call | flops 2500000000 | bytes 8388608 | tf_op jit(solution)/shard_map/project/pallas_call | solution.py:614
  (8 shorter events, 0.0 us)
Async XLA Ops:
  0.6 1.2 %copy-start.3 = (bf16[4,32,8,512]{3,2,1,0:T(8,128)(2,1)S(1)}, bf16[4,32,8,512]{3,2,1,0:T(8,128)(2,1)}, u32[]{:S(2)}) copy-start(bf16[4,32,8,512]{3,2,1,0:T(8,128)(2,1)} %param.23) | copy-start | bytes 3145732
  2.1 12.0 %copy-start.4 = (bf16[4,32,8,512]{3,2,1,0:T(8,128)(2,1)S(1)}, bf16[4,32,8,512]{3,2,1,0:T(8,128)(2,1)}, u32[]{:S(2)}) copy-start(bf16[4,32,8,512]{3,2,1,0:T(8,128)(2,1)} %param.23) | copy-start | bytes 3145732
  2.1 12.0 %copy-start.8 = (f32[3,3]{1,0:T(4,128)S(1)}, f32[3,3]{1,0:T(4,128)}, u32[]{:S(2)}) copy-start(f32[3,3]{1,0:T(4,128)} %metric.7) | copy-start | bytes 112
  2.1 12.0 %copy-start.9 = (f32[3,3]{1,0:T(4,128)S(1)}, f32[3,3]{1,0:T(4,128)}, u32[]{:S(2)}) copy-start(f32[3,3]{1,0:T(4,128)} %strain.1) | copy-start | bytes 112
  2.2 12.0 %copy-start.14 = (bf16[768,512]{1,0:T(8,128)(2,1)S(1)}, bf16[768,512]{1,0:T(8,128)(2,1)}, u32[]{:S(2)}) copy-start(bf16[768,512]{1,0:T(8,128)(2,1)} %constant.41.clone.along) | copy-start | bytes 2359300
  2.2 12.0 %copy-start.18 = (f32[3,128,256]{2,1,0:T(8,128)S(1)}, f32[3,128,256]{2,1,0:T(8,128)}, u32[]{:S(2)}) copy-start(f32[3,128,256]{2,1,0:T(8,128)} %constant.42.clone.waves) | copy-start | bytes 1179652
  2.2 12.0 %copy-start.22 = (f32[256]{0:T(256)S(1)}, f32[256]{0:T(256)}, u32[]{:S(2)}) copy-start(f32[256]{0:T(256)} %constant.40.clone.wave_x) | copy-start | bytes 3076
  2.2 17.0 %collective-permute-start = (bf16[3,96,512]{2,1,0:T(8,128)(2,1)S(1)}, bf16[3,96,512]{2,1,0:T(8,128)(2,1)S(1)}, u32[]{:S(2)}, u32[]{:S(2)}) collective-permute-start(bf16[3,96,512]{2,1,0:T(8,128)(2,1)S(1)} %first.1), channel_id=1, source_target_pairs={{0,4},{4,0},{8,12},{12,8},{16,20},{20,16},{24,28},{28,24},{32,36},... | collective-permute-start | bytes 884744 | tf_op jit(solution)/shard_map/ppermute | solution.py:525
  4.3 14.9 %copy-start.20 = (bf16[2,256,96]{2,1,0:T(8,128)(2,1)S(1)}, bf16[2,256,96]{2,1,0:T(8,128)(2,1)}, u32[]{:S(2)}) copy-start(bf16[2,256,96]{2,1,0:T(8,128)(2,1)} %constant.43.clone.along_first) | copy-start | bytes 294916
  4.7 12.9 %collective-permute-start.1 = (bf16[4,24,512]{2,1,0:T(8,128)(2,1)S(1)}, bf16[4,24,512]{2,1,0:T(8,128)(2,1)S(1)}, u32[]{:S(2)}, u32[]{:S(2)}) collective-permute-start(bf16[4,24,512]{2,1,0:T(8,128)(2,1)S(1)} %get-tuple-element.32), channel_id=1, source_target_pairs={{0,1},{1,0},{2,3},{3,2},{4,5},{5,4},{6,7},{7,6},{8,9},{9,8},{10,11... | collective-permute-start | bytes 294920 | tf_op jit(solution)/shard_map/ppermute | solution.py:527
  5.8 16.5 %collective-permute-start.3 = (bf16[4,24,512]{2,1,0:T(8,128)(2,1)S(1)}, bf16[4,24,512]{2,1,0:T(8,128)(2,1)S(1)}, u32[]{:S(2)}, u32[]{:S(2)}) collective-permute-start(bf16[4,24,512]{2,1,0:T(8,128)(2,1)S(1)} %get-tuple-element.37), channel_id=1, source_target_pairs={{0,3},{1,2},{2,1},{3,0},{4,7},{5,6},{6,5},{7,4},{8,11},{9,10},{10,... | collective-permute-start | bytes 294920 | tf_op jit(solution)/shard_map/ppermute | solution.py:528
  8.2 11.0 %copy-start.1 = (bf16[512,1536]{1,0:T(8,128)(2,1)S(1)}, bf16[512,1536]{1,0:T(8,128)(2,1)}, u32[]{:S(2)}) copy-start(bf16[512,1536]{1,0:T(8,128)(2,1)} %constant.47.clone.waves) | copy-start | bytes 4718596
  8.2 11.0 %copy-start.2 = (bf16[1024,512]{1,0:T(8,128)(2,1)S(1)}, bf16[1024,512]{1,0:T(8,128)(2,1)}, u32[]{:S(2)}) copy-start(bf16[1024,512]{1,0:T(8,128)(2,1)} %constant.46.clone.along_x) | copy-start | bytes 3145732
  8.2 11.0 %copy-start.7 = (bf16[2,24,24]{2,1,0:T(8,128)(2,1)S(1)}, bf16[2,24,24]{2,1,0:T(8,128)(2,1)}, u32[]{:S(2)}) copy-start(bf16[2,24,24]{2,1,0:T(8,128)(2,1)} %constant.44.clone.along_z) | copy-start | bytes 6916
  8.2 11.0 %copy-start.13 = (bf16[512,1024]{1,0:T(8,128)(2,1)S(1)}, bf16[512,1024]{1,0:T(8,128)(2,1)}, u32[]{:S(2)}) copy-start(bf16[512,1024]{1,0:T(8,128)(2,1)} %constant.45.clone.spread) | copy-start | bytes 3145732
  8.2 17.1 %collective-permute-start.2 = (bf16[3,96,512]{2,1,0:T(8,128)(2,1)S(1)}, bf16[3,96,512]{2,1,0:T(8,128)(2,1)S(1)}, u32[]{:S(2)}, u32[]{:S(2)}) collective-permute-start(bf16[3,96,512]{2,1,0:T(8,128)(2,1)S(1)} %get-tuple-element.36), channel_id=1, source_target_pairs={{0,124},{4,8},{8,4},{12,16},{16,12},{20,24},{24,20},{28,32},{32,28... | collective-permute-start | bytes 884744 | tf_op jit(solution)/shard_map/ppermute | solution.py:526
  17.5 10.5 %collective-permute-start.4 = (bf16[1,96,512]{2,1,0:T(8,128)(2,1)S(1)}, bf16[1,96,512]{2,1,0:T(8,128)(2,1)S(1)}, u32[]{:S(2)}, u32[]{:S(2)}) collective-permute-start(bf16[1,96,512]{2,1,0:T(8,128)(2,1)S(1)} %get-tuple-element.39), channel_id=1, source_target_pairs={{0,4},{4,0},{8,12},{12,8},{16,20},{20,16},{24,28},{28,24},{32,36},... | collective-permute-start | bytes 294920 | tf_op jit(solution)/shard_map/ppermute | solution.py:549
  17.6 11.6 %collective-permute-start.5 = (bf16[1,96,512]{2,1,0:T(8,128)(2,1)S(1)}, bf16[1,96,512]{2,1,0:T(8,128)(2,1)S(1)}, u32[]{:S(2)}, u32[]{:S(2)}) collective-permute-start(bf16[1,96,512]{2,1,0:T(8,128)(2,1)S(1)} %get-tuple-element.40), channel_id=1, source_target_pairs={{0,124},{4,8},{8,4},{12,16},{16,12},{20,24},{24,20},{28,32},{32,28... | collective-permute-start | bytes 294920 | tf_op jit(solution)/shard_map/ppermute | solution.py:550
  19.2 6.1 %copy-start = (bf16[4,768,512]{2,1,0:T(8,128)(2,1)S(1)}, bf16[4,768,512]{2,1,0:T(8,128)(2,1)}, u32[]{:S(2)}) copy-start(bf16[4,768,512]{2,1,0:T(8,128)(2,1)} %constant.50.clone.spread_rows) | copy-start | bytes 9437188
  19.2 6.1 %copy-start.5 = (bf16[2,256,96]{2,1,0:T(8,128)(2,1)S(1)}, bf16[2,256,96]{2,1,0:T(8,128)(2,1)}, u32[]{:S(2)}) copy-start(bf16[2,256,96]{2,1,0:T(8,128)(2,1)} %constant.48.clone.along_second) | copy-start | bytes 294916
  19.3 6.1 %copy-start.6 = (bf16[2,96,96]{2,1,0:T(8,128)(2,1)S(1)}, bf16[2,96,96]{2,1,0:T(8,128)(2,1)}, u32[]{:S(2)}) copy-start(bf16[2,96,96]{2,1,0:T(8,128)(2,1)} %constant.49.clone.along_rows) | copy-start | bytes 110596
  25.3 29.3 %slice-start = ((s8[5242880]{0:T(1024)(128)(4,1)}), s8[4194304]{0:T(1024)(128)(4,1)S(1)}, s32[]{:S(2)}) async-start(s8[5242880]{0:T(1024)(128)(4,1)} %bitcast.6), calls=%async_computation.2 | async-start | bytes 8388608
  25.3 29.3 %slice-start.1 = ((s8[5242880]{0:T(1024)(128)(4,1)}), s8[1048576]{0:T(1024)(128)(4,1)S(1)}, s32[]{:S(2)}) async-start(s8[5242880]{0:T(1024)(128)(4,1)} %bitcast.6), calls=%async_computation.3 | async-start | bytes 2097152
  25.4 29.3 %copy-start.10 = (bf16[3072,512]{1,0:T(8,128)(2,1)S(1)}, bf16[3072,512]{1,0:T(8,128)(2,1)}, u32[]{:S(2)}) copy-start(bf16[3072,512]{1,0:T(8,128)(2,1)} %constant.54.clone.inner) | copy-start | bytes 9437188
  28.0 26.6 %copy-start.15 = (bf16[256,1280]{1,0:T(8,128)(2,1)S(1)}, bf16[256,1280]{1,0:T(8,128)(2,1)}, u32[]{:S(2)}) copy-start(bf16[256,1280]{1,0:T(8,128)(2,1)} %constant.52.clone.outer_back) | copy-start | bytes 1966084
  28.0 26.6 %copy-start.16 = (f32[2,128,512]{2,1,0:T(8,128)S(1)}, f32[2,128,512]{2,1,0:T(8,128)}, u32[]{:S(2)}) copy-start(f32[2,128,512]{2,1,0:T(8,128)} %constant.53.clone.twist) | copy-start | bytes 1572868
  28.0 26.6 %copy-start.17 = (bf16[256,768]{1,0:T(8,128)(2,1)S(1)}, bf16[256,768]{1,0:T(8,128)(2,1)}, u32[]{:S(2)}) copy-start(bf16[256,768]{1,0:T(8,128)(2,1)} %constant.51.clone.outer) | copy-start | bytes 1179652
  54.7 27.6 %copy-start.12 = (bf16[512,1536]{1,0:T(8,128)(2,1)S(1)}, bf16[512,1536]{1,0:T(8,128)(2,1)}, u32[]{:S(2)}) copy-start(bf16[512,1536]{1,0:T(8,128)(2,1)} %constant.56.clone.gather) | copy-start | bytes 4718596
  59.2 23.1 %copy-start.11 = (bf16[1536,512]{1,0:T(8,128)(2,1)S(1)}, bf16[1536,512]{1,0:T(8,128)(2,1)}, u32[]{:S(2)}) copy-start(bf16[1536,512]{1,0:T(8,128)(2,1)} %constant.58.clone.inverse) | copy-start | bytes 4718596
  59.2 23.0 %copy-start.19 = (bf16[256,512]{1,0:T(8,128)(2,1)S(1)}, bf16[256,512]{1,0:T(8,128)(2,1)}, u32[]{:S(2)}) copy-start(bf16[256,512]{1,0:T(8,128)(2,1)} %constant.57.clone.keep) | copy-start | bytes 786436
  59.2 23.0 %copy-start.21 = (f32[2,1,128]{2,1,0:T(1,128)S(1)}, f32[2,1,128]{2,1,0:T(1,128)}, u32[]{:S(2)}) copy-start(f32[2,1,128]{2,1,0:T(1,128)} %constant.59.clone.symbol) | copy-start | bytes 3076
